TPU v7x, 32 devices: a whole 2x2x4 slice. The times are simulated.
32 devices in a mesh: fsdp: 8 (over z, x), ns: 4 (over y, core).
Axes of the slice: x: 2, y: 2, z: 4, core: 2. Of those that a mesh axis runs over, the one named last changes fastest.
Arguments:
- tokens: bfloat16 [32768, 384], P(('fsdp', 'ns')), may hold values from -6 to 6
- cotangent: bfloat16 [32768, 384], P(('fsdp', 'ns')), may hold values from -30 to 30
- lengths: int32 [512], P(('fsdp', 'ns')), may hold values from 32 to 64, as said below
- variates: int32 [512, 64], P(('fsdp', 'ns')), may hold values from 0 to 3
- times: int32 [32768], P(('fsdp', 'ns')), may hold values from 0 to 63
- weight_qkv: float32 [3, 384, 384], P(None, None, 'fsdp'), may hold values from -0.3125 to 0.3125
- weight_out: float32 [384, 384], P('fsdp'), may hold values from -0.875 to 0.875
- weight_gate_up: float32 [2, 384, 1024], P(None, None, 'fsdp'), may hold values from -0.3125 to 0.3125
- weight_down: float32 [1024, 384], P('fsdp'), may hold values from -0.1875 to 0.1875
- momentum_qkv: float32 [3, 384, 384], P(None, None, 'fsdp'), may hold values from -2896.3094 to 2896.3094
- momentum_out: float32 [384, 384], P('fsdp'), may hold values from -2896.3094 to 2896.3094
- momentum_gate_up: float32 [2, 384, 1024], P(None, None, 'fsdp'), may hold values from -2896.3094 to 2896.3094
- momentum_down: float32 [1024, 384], P('fsdp'), may hold values from -2896.3094 to 2896.3094
- gains: float32 [2, 384], replicated, may hold values from 0.5 to 1.5
- attn_bias: float32 [2, 6], replicated, may hold values from -3 to 3
- gain_moment: float32 [2, 384], replicated, may hold values from -128 to 128
- gain_square: float32 [2, 384], replicated, may hold values from 1638.4 to 6553.6
- bias_moment: float32 [2, 6], replicated, may hold values from -256 to 256
- bias_square: float32 [2, 6], replicated, may hold values from 9830.4 to 39321.6
Outputs:
- out_tokens: bfloat16 [32768, 384], P(('fsdp', 'ns'))
- grad_tokens: bfloat16 [32768, 384], P(('fsdp', 'ns'))
- grad_qkv: float32 [3, 384, 384], P(None, None, 'fsdp')
- grad_out: float32 [384, 384], P('fsdp')
- grad_gate_up: float32 [2, 384, 1024], P(None, None, 'fsdp')
- grad_down: float32 [1024, 384], P('fsdp')
- new_momentum_qkv: float32 [3, 384, 384], P(None, None, 'fsdp')
- new_momentum_out: float32 [384, 384], P('fsdp')
- new_momentum_gate_up: float32 [2, 384, 1024], P(None, None, 'fsdp')
- new_momentum_down: float32 [1024, 384], P('fsdp')
- new_weight_qkv: float32 [3, 384, 384], P(None, None, 'fsdp')
- new_weight_out: float32 [384, 384], P('fsdp')
- new_weight_gate_up: float32 [2, 384, 1024], P(None, None, 'fsdp')
- new_weight_down: float32 [1024, 384], P('fsdp')
- grad_gains: float32 [2, 384], replicated
- new_gain_moment: float32 [2, 384], replicated
- new_gain_square: float32 [2, 384], replicated
- new_gains: float32 [2, 384], replicated
- grad_bias: float32 [2, 6], replicated
- new_bias_moment: float32 [2, 6], replicated
- new_bias_square: float32 [2, 6], replicated
- new_bias: float32 [2, 6], replicated
Inputs may be any that keep to these rules, and one draw needn't show every extreme that they name: `lengths`: one bucket of all has all 64 slots live.
All inputs are finite; a program needn't handle non-finite values.
Results may differ from a plain program's by a relative error of at most 0.022.
The roundings to bfloat16 on the way count: a program that leaves them out, or rounds other values in their place, can miss the bound.
Values may be sent and summed in bfloat16 or wider, within the bound.
A program may use at most 128 MiB of HBM per device.

v0:
```python
import math

import jax
import jax.numpy as jnp
from jax import lax
from jax.sharding import PartitionSpec as P

D = 384
HEADS = 6
HEAD_DIM = 64
FF = 1024
NS_ITERS = 5
STEP = 10


EPS_NORM = 1e-06
ROPE_BASE = 10000.0
NEG_FILL = -1000000000.0
COEF_A = 3.4445
COEF_B = -4.775
COEF_C = 2.0315
NS_EPS = 1e-07
MUON_MU = 0.95
MUON_RATE = 0.25
MUON_DECAY = 0.01
ADAM_RATE = 0.8
BETA_ONE = 0.9
BETA_TWO = 0.95
ADAM_EPS = 1e-08


def rotary_tables(positions, head_size):
    half_dim = head_size // 2
    frequency = ROPE_BASE ** (-2.0 * jnp.arange(half_dim, dtype=jnp.float32) / head_size)
    angles = positions.astype(jnp.float32)[:, None] * frequency[None, :]
    return (jnp.cos(angles), jnp.sin(angles))


def rotate(vectors, cosine, sine_tab):
    half_dim = vectors.shape[-1] // 2
    first_half = vectors[..., :half_dim]
    second_half = vectors[..., half_dim:]
    cos_b = cosine[:, None, :]
    sin_b = sine_tab[:, None, :]
    return jnp.concatenate(
        [first_half * cos_b - second_half * sin_b, first_half * sin_b + second_half * cos_b],
        axis=-1,
    )


def unrotate(vectors, cosine, sine_tab):
    half_dim = vectors.shape[-1] // 2
    first_half = vectors[..., :half_dim]
    second_half = vectors[..., half_dim:]
    cos_b = cosine[:, None, :]
    sin_b = sine_tab[:, None, :]
    return jnp.concatenate(
        [first_half * cos_b + second_half * sin_b, second_half * cos_b - first_half * sin_b],
        axis=-1,
    )


def rms_scale(values):
    return lax.rsqrt(jnp.mean(values * values, axis=-1, keepdims=True) + EPS_NORM)


def norm_back(source, scale, gain_row, incoming):
    normed = source * scale
    gain_grad = jnp.sum(incoming * normed, axis=0)
    scaled_in = incoming * gain_row
    back = scale * (scaled_in - normed * jnp.mean(scaled_in * normed, axis=-1, keepdims=True))
    return (back, gain_grad)


def gram_local(current):
    return jnp.einsum(
        "mdn,men->mde",
        current,
        current,
        precision=lax.Precision.HIGHEST,
        preferred_element_type=jnp.float32,
    )


def newton_schulz(advance, gram_total):
    current = advance
    for turn_idx in range(NS_ITERS):
        gram_mat = gram_total(gram_local(current))
        if turn_idx == 0:
            norm_val = jnp.sqrt(jnp.trace(gram_mat, axis1=1, axis2=2))[:, None, None] + NS_EPS
            current = current / norm_val
            gram_mat = gram_mat / (norm_val * norm_val)
        poly_mat = COEF_B * gram_mat + COEF_C * jnp.einsum(
            "mde,mef->mdf",
            gram_mat,
            gram_mat,
            precision=lax.Precision.HIGHEST,
            preferred_element_type=jnp.float32,
        )
        current = COEF_A * current + jnp.einsum(
            "mde,men->mdn",
            poly_mat,
            current,
            precision=lax.Precision.HIGHEST,
            preferred_element_type=jnp.float32,
        )
    return current


def adam_step(param, grad, moment, square):
    new_moment = BETA_ONE * moment + (1.0 - BETA_ONE) * grad
    new_square = BETA_TWO * square + (1.0 - BETA_TWO) * grad * grad
    corrected = new_moment / (1.0 - BETA_ONE**STEP)
    scaled = jnp.sqrt(new_square / (1.0 - BETA_TWO**STEP)) + ADAM_EPS
    return (new_moment, new_square, param - ADAM_RATE * corrected / scaled)


def body(
    tokens,
    cotangent,
    lengths,
    variates,
    times,
    weight_qkv,
    weight_out,
    weight_gate_up,
    weight_down,
    momentum_qkv,
    momentum_out,
    momentum_gate_up,
    momentum_down,
    gains,
    attn_bias,
    gain_moment,
    gain_square,
    bias_moment,
    bias_square,
):
    low_type = jnp.bfloat16
    tok_rows = tokens.shape[0]
    bucket_count = lengths.shape[0]
    bucket_len = tok_rows // bucket_count
    head_count = attn_bias.shape[1]
    attn_width = head_count * HEAD_DIM
    shape_four = (bucket_count, bucket_len, head_count, HEAD_DIM)
    shards = (
        weight_qkv.astype(low_type),
        weight_out.astype(low_type),
        weight_gate_up.astype(low_type),
        weight_down.astype(low_type),
    )
    full_qkv, full_out, full_gate_up, full_down = (
        lax.all_gather(shards[0], "fsdp", axis=2, tiled=True),
        lax.all_gather(shards[1], "fsdp", axis=0, tiled=True),
        lax.all_gather(shards[2], "fsdp", axis=2, tiled=True),
        lax.all_gather(shards[3], "fsdp", axis=0, tiled=True),
    )
    tokens_wide = tokens.astype(jnp.float32)
    scale_one = rms_scale(tokens_wide)
    normed_one = (tokens_wide * scale_one * gains[0]).astype(low_type)
    qkv_proj = jnp.einsum("td,kde->kte", normed_one, full_qkv, preferred_element_type=jnp.float32)
    cosine, sine_tab = rotary_tables(times, HEAD_DIM)
    query_scale = HEAD_DIM ** (-0.5)
    query_rot = (
        (
            rotate(qkv_proj[0].reshape(tok_rows, head_count, HEAD_DIM), cosine, sine_tab)
            * query_scale
        )
        .astype(low_type)
        .reshape(shape_four)
    )
    key_rot = (
        rotate(qkv_proj[1].reshape(tok_rows, head_count, HEAD_DIM), cosine, sine_tab)
        .astype(low_type)
        .reshape(shape_four)
    )
    value_low = qkv_proj[2].astype(low_type).reshape(shape_four)
    live_keys = jnp.arange(bucket_len, dtype=jnp.int32)[None, :] < lengths[:, None]
    same_var = (variates[:, :, None] == variates[:, None, :]).astype(jnp.float32)[:, None]

    def scores_of(query_part, key_part):
        raw_scores = jnp.einsum(
            "bqhd,bkhd->bhqk", query_part, key_part, preferred_element_type=jnp.float32
        )
        biased = (
            raw_scores
            + attn_bias[0][None, :, None, None] * same_var
            + attn_bias[1][None, :, None, None] * (1.0 - same_var)
        )
        return jnp.where(live_keys[:, None, None, :], biased, NEG_FILL)

    scores = scores_of(query_rot, key_rot)
    row_top = jnp.max(scores, axis=-1, keepdims=True)
    exponent = jnp.exp(scores - row_top)
    row_total = jnp.sum(exponent, axis=-1, keepdims=True)
    attn_probs = exponent / row_total
    log_total = row_top + jnp.log(row_total)
    attended = (
        jnp.einsum(
            "bhqk,bkhd->bqhd",
            attn_probs.astype(low_type),
            value_low,
            preferred_element_type=jnp.float32,
        )
        .reshape(tok_rows, attn_width)
        .astype(low_type)
    )
    mid_resid = tokens_wide + jnp.dot(attended, full_out, preferred_element_type=jnp.float32)
    scale_two = rms_scale(mid_resid)
    normed_two = (mid_resid * scale_two * gains[1]).astype(low_type)
    gate_up = jnp.einsum(
        "td,kdf->ktf", normed_two, full_gate_up, preferred_element_type=jnp.float32
    )
    gate_val = gate_up[0]
    up_val = gate_up[1]
    sigmoid_g = jax.nn.sigmoid(gate_val)
    silu_val = gate_val * sigmoid_g
    hidden = (silu_val * up_val).astype(low_type)
    out_tokens = (
        mid_resid + jnp.dot(hidden, full_down, preferred_element_type=jnp.float32)
    ).astype(low_type)
    full_qkv, full_out, full_gate_up, full_down = (
        lax.all_gather(shards[0], "fsdp", axis=2, tiled=True),
        lax.all_gather(shards[1], "fsdp", axis=0, tiled=True),
        lax.all_gather(shards[2], "fsdp", axis=2, tiled=True),
        lax.all_gather(shards[3], "fsdp", axis=0, tiled=True),
    )
    live_rows = live_keys.reshape(tok_rows).astype(jnp.float32)
    grad_block = cotangent.astype(jnp.float32) * live_rows[:, None]
    grad_low = grad_block.astype(low_type)
    grad_down = jnp.einsum("tf,td->fd", hidden, grad_low, preferred_element_type=jnp.float32)
    grad_hidden = jnp.einsum("td,fd->tf", grad_low, full_down, preferred_element_type=jnp.float32)
    grad_gate = grad_hidden * up_val * sigmoid_g * (1.0 + gate_val * (1.0 - sigmoid_g))
    grad_up = grad_hidden * silu_val
    grad_pair = jnp.stack([grad_gate, grad_up]).astype(low_type)
    grad_gate_up = jnp.einsum(
        "td,ktf->kdf", normed_two, grad_pair, preferred_element_type=jnp.float32
    )
    grad_norm_two = jnp.einsum(
        "ktf,kdf->td", grad_pair, full_gate_up, preferred_element_type=jnp.float32
    )
    back_two, gain_two_grad = norm_back(mid_resid, scale_two, gains[1], grad_norm_two)
    grad_mid = grad_block + back_two
    grad_mid_low = grad_mid.astype(low_type)
    grad_out = jnp.einsum("te,td->ed", attended, grad_mid_low, preferred_element_type=jnp.float32)
    grad_att = (
        jnp.einsum("td,ed->te", grad_mid_low, full_out, preferred_element_type=jnp.float32)
        .astype(low_type)
        .reshape(shape_four)
    )
    probs_again = jnp.exp(scores_of(query_rot, key_rot) - log_total)
    grad_probs = jnp.einsum(
        "bqhd,bkhd->bhqk", grad_att, value_low, preferred_element_type=jnp.float32
    )
    row_dot = jnp.sum(probs_again * grad_probs, axis=-1, keepdims=True)
    grad_scores = probs_again * (grad_probs - row_dot)
    same_part = jnp.sum(grad_scores * same_var, axis=(0, 2, 3))
    other_part = jnp.sum(grad_scores * (1.0 - same_var), axis=(0, 2, 3))
    bias_grads = jnp.stack([same_part, other_part])
    scores_low = grad_scores.astype(low_type)
    grad_query = jnp.einsum(
        "bhqk,bkhd->bqhd", scores_low, key_rot, preferred_element_type=jnp.float32
    )
    grad_keys = jnp.einsum(
        "bhqk,bqhd->bkhd", scores_low, query_rot, preferred_element_type=jnp.float32
    )
    grad_values = jnp.einsum(
        "bhqk,bqhd->bkhd",
        probs_again.astype(low_type),
        grad_att,
        preferred_element_type=jnp.float32,
    )
    grad_q = (
        unrotate(grad_query.reshape(tok_rows, head_count, HEAD_DIM), cosine, sine_tab) * query_scale
    )
    grad_k = unrotate(grad_keys.reshape(tok_rows, head_count, HEAD_DIM), cosine, sine_tab)
    grad_triple = jnp.stack(
        [
            grad_q.reshape(tok_rows, attn_width),
            grad_k.reshape(tok_rows, attn_width),
            grad_values.reshape(tok_rows, attn_width),
        ]
    ).astype(low_type)
    grad_qkv = jnp.einsum(
        "td,kte->kde", normed_one, grad_triple, preferred_element_type=jnp.float32
    )
    grad_norm_one = jnp.einsum(
        "kte,kde->td", grad_triple, full_qkv, preferred_element_type=jnp.float32
    )
    back_one, gain_one_grad = norm_back(tokens_wide, scale_one, gains[0], grad_norm_one)
    grad_tokens = (grad_mid + back_one).astype(low_type)
    summed = (
        lax.psum_scatter(grad_qkv, "fsdp", scatter_dimension=2, tiled=True),
        lax.psum_scatter(grad_out, "fsdp", scatter_dimension=0, tiled=True),
        lax.psum_scatter(grad_gate_up, "fsdp", scatter_dimension=2, tiled=True),
        lax.psum_scatter(grad_down, "fsdp", scatter_dimension=0, tiled=True),
    )
    grad_qkv, grad_out, grad_gate_up, grad_down = (
        lax.psum(summed[0].astype(jnp.bfloat16), "ns").astype(jnp.float32),
        lax.psum(summed[1].astype(jnp.bfloat16), "ns").astype(jnp.float32),
        lax.psum(summed[2].astype(jnp.bfloat16), "ns").astype(jnp.float32),
        lax.psum(summed[3].astype(jnp.bfloat16), "ns").astype(jnp.float32),
    )
    grad_gains, grad_bias = lax.psum(
        (jnp.stack([gain_one_grad, gain_two_grad]), bias_grads), ("fsdp", "ns")
    )
    new_momentum_qkv = MUON_MU * momentum_qkv + grad_qkv
    new_momentum_out = MUON_MU * momentum_out + grad_out
    new_momentum_gate_up = MUON_MU * momentum_gate_up + grad_gate_up
    new_momentum_down = MUON_MU * momentum_down + grad_down
    look_qkv = grad_qkv + MUON_MU * new_momentum_qkv
    look_out = grad_out + MUON_MU * new_momentum_out
    look_gate_up = grad_gate_up + MUON_MU * new_momentum_gate_up
    look_down = grad_down + MUON_MU * new_momentum_down
    attn_stack = jnp.concatenate([look_qkv, look_out.T[None]], axis=0)
    ff_stack = jnp.concatenate([look_gate_up, look_down.T[None]], axis=0)
    attn_ortho = newton_schulz(attn_stack, lambda partial_gram: lax.psum(partial_gram, "fsdp"))
    quarter = ff_stack.shape[2] // lax.axis_size("ns")
    own_cols = lax.dynamic_slice_in_dim(ff_stack, lax.axis_index("ns") * quarter, quarter, 2)
    own_ortho = newton_schulz(own_cols, lambda partial_gram: lax.psum(partial_gram, ("fsdp", "ns")))
    ff_ortho = lax.all_gather(own_ortho, "ns", axis=2, tiled=True)
    shrink = 1.0 - MUON_RATE * MUON_DECAY
    attn_factor = MUON_RATE * 0.2 * math.sqrt(max(D, HEADS * HEAD_DIM))
    ff_factor = MUON_RATE * 0.2 * math.sqrt(max(D, FF))
    new_weight_qkv = weight_qkv * shrink - attn_factor * attn_ortho[:3]
    new_weight_out = weight_out * shrink - attn_factor * attn_ortho[3].T
    new_weight_gate_up = weight_gate_up * shrink - ff_factor * ff_ortho[:2]
    new_weight_down = weight_down * shrink - ff_factor * ff_ortho[2].T
    new_gain_moment, new_gain_square, new_gains = adam_step(
        gains, grad_gains, gain_moment, gain_square
    )
    new_bias_moment, new_bias_square, new_bias = adam_step(
        attn_bias, grad_bias, bias_moment, bias_square
    )
    return (
        out_tokens,
        grad_tokens,
        grad_qkv,
        grad_out,
        grad_gate_up,
        grad_down,
        new_momentum_qkv,
        new_momentum_out,
        new_momentum_gate_up,
        new_momentum_down,
        new_weight_qkv,
        new_weight_out,
        new_weight_gate_up,
        new_weight_down,
        grad_gains,
        new_gain_moment,
        new_gain_square,
        new_gains,
        grad_bias,
        new_bias_moment,
        new_bias_square,
        new_bias,
    )


def solution(mesh):
    return jax.shard_map(
        body,
        mesh=mesh,
        in_specs=(
            P(("fsdp", "ns"), None),
            P(("fsdp", "ns"), None),
            P(("fsdp", "ns")),
            P(("fsdp", "ns"), None),
            P(("fsdp", "ns")),
            P(None, None, "fsdp"),
            P("fsdp", None),
            P(None, None, "fsdp"),
            P("fsdp", None),
            P(None, None, "fsdp"),
            P("fsdp", None),
            P(None, None, "fsdp"),
            P("fsdp", None),
            P(),
            P(),
            P(),
            P(),
            P(),
            P(),
        ),
        out_specs=(
            P(("fsdp", "ns"), None),
            P(("fsdp", "ns"), None),
            P(None, None, "fsdp"),
            P("fsdp", None),
            P(None, None, "fsdp"),
            P("fsdp", None),
            P(None, None, "fsdp"),
            P("fsdp", None),
            P(None, None, "fsdp"),
            P("fsdp", None),
            P(None, None, "fsdp"),
            P("fsdp", None),
            P(None, None, "fsdp"),
            P("fsdp", None),
            P(),
            P(),
            P(),
            P(),
            P(),
            P(),
            P(),
            P(),
        ),
        check_vma=False,
    )
```

profile of v0, /device:TPU:15, one launch (start us, length us, event | category | flops | bytes accessed | tf_op | source)
XLA Modules:
  0.0 1751.0 jit_solution(1876615144483900583)
XLA Ops:
  10.8 26.4 %all_gather.19 = bf16[3,384,384]{1,2,0:T(8,128)(2,1)S(1)} all-gather(bf16[3,384,48]{1,2,0:T(8,128)(2,1)S(1)} %convert_element_type.122), channel_id=1, replica_groups=mesh['fsdp'=8,'ns'=4] {'fsdp'}, dimensions={2}, use_global_device_ids=true | all-gather | bytes 995328 | tf_op jit(solution)/shard_map/all_gather | solution.py:153
  85.9 23.5 %all_gather.20 = bf16[384,384]{1,0:T(8,128)(2,1)S(1)} all-gather(bf16[48,384]{1,0:T(8,128)(2,1)S(1)} %convert_element_type.131), channel_id=1, replica_groups=mesh['fsdp'=8,'ns'=4] {'fsdp'}, dimensions={0}, use_global_device_ids=true | all-gather | bytes 331776 | tf_op jit(solution)/shard_map/all_gather | solution.py:154
  112.6 29.2 %all_gather.22 = bf16[1024,384]{1,0:T(8,128)(2,1)} all-gather(bf16[128,384]{1,0:T(8,128)(2,1)S(1)} %convert_element_type.135), channel_id=1, replica_groups=mesh['fsdp'=8,'ns'=4] {'fsdp'}, dimensions={0}, use_global_device_ids=true | all-gather | bytes 884736 | tf_op jit(solution)/shard_map/all_gather | solution.py:156
  226.0 13.4 reduce-scatter.11.cloned.1.call-done
  241.0 67.3 %reduce-scatter.5.cloned.1.call-done = f32[3,384,48]{1,2,0:T(8,128)} async-done(((f32[3,384,384]{1,2,0:T(8,128)}), f32[3,384,48]{1,2,0:T(8,128)}) %reduce-scatter.5.cloned.1.call-update) | async-done | bytes 221200 | tf_op jit(solution)/shard_map/reduce_scatter | solution.py:293
  309.9 76.4 %reduce-scatter.9.cloned.1.call-done = f32[2,384,128]{1,2,0:T(8,128)} async-done(((f32[2,384,1024]{1,2,0:T(8,128)}), f32[2,384,128]{1,2,0:T(8,128)}) %reduce-scatter.9.cloned.1.call-update) | async-done | bytes 393232 | tf_op jit(solution)/shard_map/reduce_scatter | solution.py:295
  389.8 31.5 %all-reduce.34.cloned.1.call-done = (bf16[2,384,128]{1,2,0:T(8,128)(2,1)}, bf16[3,384,48]{1,2,0:T(8,128)(2,1)}, bf16[128,384]{1,0:T(8,128)(2,1)}) async-done(((bf16[2,384,128]{1,2,0:T(8,128)(2,1)}, bf16[3,384,48]{1,2,0:T(8,128)(2,1)}, bf16[128,384]{1,0:T(8,128)(2,1)}), (bf16[2,384,128]{1,2,0:T(8,128)(2,1)}, bf16[3,384,48]{1,2,0:T(8,128)(2,1)}, bf16[128,384]{1,0:T(8,128)(2,1)})) %all-reduce.34.cloned.1.call-update) | async-done | bytes 405520 | tf_op jit(solution)/shard_map/psum | solution.py:301
  427.8 59.0 %reduce-scatter.7.cloned.1.call-done = f32[48,384]{1,0:T(8,128)} async-done(((f32[384,384]{1,0:T(8,128)}), f32[48,384]{1,0:T(8,128)}) %reduce-scatter.7.cloned.1.call-update) | async-done | bytes 73744 | tf_op jit(solution)/shard_map/reduce_scatter | solution.py:294
  487.8 13.1 psum.113
  506.0 117.8 %all-reduce.24.cloned.1.call-done = f32[3,384,384]{2,1,0:T(8,128)} async-done(((f32[3,384,384]{2,1,0:T(8,128)}), f32[3,384,384]{2,1,0:T(8,128)}) %all-reduce.24.cloned.1.call-update) | async-done | bytes 1769488 | tf_op jit(solution)/shard_map/psum | solution.py:320
  634.6 101.8 %all-reduce.14.cloned.1.call-done = f32[4,384,384]{2,1,0:T(8,128)} async-done(((f32[4,384,384]{2,1,0:T(8,128)}), f32[4,384,384]{2,1,0:T(8,128)}) %all-reduce.14.cloned.1.call-update) | async-done | bytes 2359312 | tf_op jit(solution)/shard_map/psum | solution.py:317
  750.3 122.9 %all-reduce.26.cloned.1.call-done = f32[3,384,384]{2,1,0:T(8,128)} async-done(((f32[3,384,384]{2,1,0:T(8,128)}), f32[3,384,384]{2,1,0:T(8,128)}) %all-reduce.26.cloned.1.call-update) | async-done | bytes 1769488 | tf_op jit(solution)/shard_map/psum | solution.py:320
  884.1 102.0 %all-reduce.16.cloned.1.call-done = f32[4,384,384]{2,1,0:T(8,128)} async-done(((f32[4,384,384]{2,1,0:T(8,128)}), f32[4,384,384]{2,1,0:T(8,128)}) %all-reduce.16.cloned.1.call-update) | async-done | bytes 2359312 | tf_op jit(solution)/shard_map/psum | solution.py:317
  986.1 7.4 fusion.194
  1000.3 121.8 %all-reduce.28.cloned.1.call-done = f32[3,384,384]{2,1,0:T(8,128)} async-done(((f32[3,384,384]{2,1,0:T(8,128)}), f32[3,384,384]{2,1,0:T(8,128)}) %all-reduce.28.cloned.1.call-update) | async-done | bytes 1769488 | tf_op jit(solution)/shard_map/psum | solution.py:320
  1133.5 101.0 %all-reduce.18.cloned.1.call-done = f32[4,384,384]{2,1,0:T(8,128)} async-done(((f32[4,384,384]{2,1,0:T(8,128)}), f32[4,384,384]{2,1,0:T(8,128)}) %all-reduce.18.cloned.1.call-update) | async-done | bytes 2359312 | tf_op jit(solution)/shard_map/psum | solution.py:317
  1234.5 7.3 fusion.196
  1255.1 116.3 %all-reduce.30.cloned.1.call-done = f32[3,384,384]{2,1,0:T(8,128)} async-done(((f32[3,384,384]{2,1,0:T(8,128)}), f32[3,384,384]{2,1,0:T(8,128)}) %all-reduce.30.cloned.1.call-update) | async-done | bytes 1769488 | tf_op jit(solution)/shard_map/psum | solution.py:320
  1382.3 102.0 %all-reduce.20.cloned.1.call-done = f32[4,384,384]{2,1,0:T(8,128)} async-done(((f32[4,384,384]{2,1,0:T(8,128)}), f32[4,384,384]{2,1,0:T(8,128)}) %all-reduce.20.cloned.1.call-update) | async-done | bytes 2359312 | tf_op jit(solution)/shard_map/psum | solution.py:317
  1484.3 7.3 fusion.198
  1505.5 39.7 %all-reduce = (f32[2,384]{1,0:T(2,128)S(1)}, f32[2,6]{1,0:T(2,128)S(1)}) all-reduce(f32[2,384]{1,0:T(2,128)S(1)} %pad_maximum_fusion.15, f32[2,6]{1,0:T(2,128)S(1)} %pad_maximum_fusion.16), channel_id=1, replica_groups=mesh['fsdp'=8,'ns'=4] {'fsdp','ns'}, use_global_device_ids=true, to_apply=%region_29.30 | all-reduce | flops 780 | bytes 6240 | tf_op jit(solution)/shard_map/psum | solution.py:304
  1548.3 71.8 %all-reduce.32.cloned.1.call-done = f32[3,384,384]{2,1,0:T(8,128)} async-done(((f32[3,384,384]{2,1,0:T(8,128)}), f32[3,384,384]{2,1,0:T(8,128)}) %all-reduce.32.cloned.1.call-update) | async-done | bytes 1769488 | tf_op jit(solution)/shard_map/psum | solution.py:320
  1627.9 9.6 all_gather.23
  1639.1 93.4 %all-reduce.22.cloned.1.call-done = f32[4,384,384]{2,1,0:T(8,128)} async-done(((f32[4,384,384]{2,1,0:T(8,128)}), f32[4,384,384]{2,1,0:T(8,128)}) %all-reduce.22.cloned.1.call-update) | async-done | bytes 2359312 | tf_op jit(solution)/shard_map/psum | solution.py:317
  (326 shorter events, 273.3 us)
Async XLA Ops:
  7.2 134.6 %all-gather.2.cloned.1.call-start = ((), (), s32[]{:S(2)}) async-start(), calls=%async_computation.4 | async-start | bytes 1769472 | tf_op jit(solution)/shard_map/all_gather | solution.py:155
  9.0 230.4 %reduce-scatter.11.cloned.1.call-start = ((), (), s32[]{:S(2)}) async-start(), calls=%async_computation.8 | async-start | bytes 1769472 | tf_op jit(solution)/shard_map/reduce_scatter | solution.py:296
  155.7 152.6 %reduce-scatter.5.cloned.1.call-start = ((), (), s32[]{:S(2)}) async-start(), calls=%async_computation.5 | async-start | bytes 1990656 | tf_op jit(solution)/shard_map/reduce_scatter | solution.py:293
  218.2 168.1 %reduce-scatter.9.cloned.1.call-start = ((), (), s32[]{:S(2)}) async-start(), calls=%async_computation.7 | async-start | bytes 3538944 | tf_op jit(solution)/shard_map/reduce_scatter | solution.py:295
  225.9 162.2 %copy-start.1 = (f32[1024,384]{0,1:T(8,128)S(1)}, f32[1024,384]{0,1:T(8,128)}, u32[]{:S(2)}) copy-start(f32[1024,384]{0,1:T(8,128)} %copy-done) | copy-start | bytes 4718596
  225.9 162.2 %copy-start.17 = (bf16[1024,384]{0,1:T(8,128)(2,1)S(1)}, bf16[1024,384]{0,1:T(8,128)(2,1)}, u32[]{:S(2)}) copy-start(bf16[1024,384]{0,1:T(8,128)(2,1)} %convert_element_type.130) | copy-start | bytes 2359300
  226.0 195.4 %all-reduce.34.cloned.1.call-start = ((), (), s32[]{:S(2)}) async-start(), calls=%async_computation.19 | async-start | bytes 811008 | tf_op jit(solution)/shard_map/psum | solution.py:301
  388.1 98.8 %reduce-scatter.7.cloned.1.call-start = ((), (), s32[]{:S(2)}) async-start(), calls=%async_computation.6 | async-start | bytes 663552 | tf_op jit(solution)/shard_map/reduce_scatter | solution.py:294
  389.6 234.3 %all-reduce.24.cloned.1.call-start = ((), (), s32[]{:S(2)}) async-start(), calls=%async_computation.14 | async-start | bytes 3538944 | tf_op jit(solution)/shard_map/psum | solution.py:320
  424.9 76.0 %copy-start.59 = (f32[48,384]{1,0:T(8,128)S(1)}, f32[48,384]{1,0:T(8,128)}, u32[]{:S(2)}) copy-start(f32[48,384]{1,0:T(8,128)} %param.29) | copy-start | bytes 221188
  424.9 76.7 %copy-start.56 = (f32[3,384,48]{1,2,0:T(8,128)S(1)}, f32[3,384,48]{1,2,0:T(8,128)}, u32[]{:S(2)}) copy-start(f32[3,384,48]{1,2,0:T(8,128)} %param.28) | copy-start | bytes 663556
  424.9 76.7 %copy-start.58 = (bf16[3,384,48]{1,2,0:T(8,128)(2,1)S(1)}, bf16[3,384,48]{1,2,0:T(8,128)(2,1)}, u32[]{:S(2)}) copy-start(bf16[3,384,48]{1,2,0:T(8,128)(2,1)} %get-tuple-element.77) | copy-start | bytes 331780
  427.8 308.6 %all-reduce.14.cloned.1.call-start = ((), (), s32[]{:S(2)}) async-start(), calls=%async_computation.9 | async-start | bytes 4718592 | tf_op jit(solution)/shard_map/psum | solution.py:317
  505.9 367.4 %all-reduce.26.cloned.1.call-start = ((), (), s32[]{:S(2)}) async-start(), calls=%async_computation.15 | async-start | bytes 3538944 | tf_op jit(solution)/shard_map/psum | solution.py:320
  634.4 351.7 %all-reduce.16.cloned.1.call-start = ((), (), s32[]{:S(2)}) async-start(), calls=%async_computation.10 | async-start | bytes 4718592 | tf_op jit(solution)/shard_map/psum | solution.py:317
  750.1 372.0 %all-reduce.28.cloned.1.call-start = ((), (), s32[]{:S(2)}) async-start(), calls=%async_computation.16 | async-start | bytes 3538944 | tf_op jit(solution)/shard_map/psum | solution.py:320
  883.8 350.7 %all-reduce.18.cloned.1.call-start = ((), (), s32[]{:S(2)}) async-start(), calls=%async_computation.11 | async-start | bytes 4718592 | tf_op jit(solution)/shard_map/psum | solution.py:317
  999.8 371.6 %all-reduce.30.cloned.1.call-start = ((), (), s32[]{:S(2)}) async-start(), calls=%async_computation.17 | async-start | bytes 3538944 | tf_op jit(solution)/shard_map/psum | solution.py:320
  1133.3 350.9 %all-reduce.20.cloned.1.call-start = ((), (), s32[]{:S(2)}) async-start(), calls=%async_computation.12 | async-start | bytes 4718592 | tf_op jit(solution)/shard_map/psum | solution.py:317
  1248.1 372.0 %all-reduce.32.cloned.1.call-start = ((), (), s32[]{:S(2)}) async-start(), calls=%async_computation.18 | async-start | bytes 3538944 | tf_op jit(solution)/shard_map/psum | solution.py:320
  1255.1 122.1 %copy-start.25 = (f32[3,384,32]{1,2,0:T(8,128)S(1)}, f32[3,384,32]{1,2,0:T(8,128)}, u32[]{:S(2)}) copy-start(f32[3,384,32]{1,2,0:T(8,128)} %copy-done.24) | copy-start | bytes 442372
  1382.0 350.6 %all-reduce.22.cloned.1.call-start = ((), (), s32[]{:S(2)}) async-start(), calls=%async_computation.13 | async-start | bytes 4718592 | tf_op jit(solution)/shard_map/psum | solution.py:317
  1545.2 80.6 %copy-start.69 = (f32[2,384]{1,0:T(2,128)}, f32[2,384]{1,0:T(2,128)S(1)}, u32[]{:S(2)}) copy-start(f32[2,384]{1,0:T(2,128)S(1)} %get-tuple-element.74) | copy-start | bytes 9220
  1545.2 80.6 %copy-start.76 = (f32[2,6]{1,0:T(2,128)}, f32[2,6]{1,0:T(2,128)S(1)}, u32[]{:S(2)}) copy-start(f32[2,6]{1,0:T(2,128)S(1)} %get-tuple-element.75) | copy-start | bytes 148
  (74 other events, 706.5 us)
Sparse Core Ops, SparseCore 0:
  10.7 47.2 all-gather.1
  155.8 83.5 reduce-scatter.10
  243.3 64.9 reduce-scatter.4
  311.7 74.5 reduce-scatter.8
  389.9 31.4 all-reduce.33
  425.4 61.4 reduce-scatter.6
  492.3 131.5 all-reduce.23
  627.4 108.9 all-reduce.13
  742.7 130.5 all-reduce.25
  877.1 108.9 all-reduce.15
  991.5 130.5 all-reduce.27
  1125.5 108.9 all-reduce.17
  1240.8 130.5 all-reduce.29
  1375.2 108.9 all-reduce.19
  1489.5 130.5 all-reduce.31
  1623.5 108.9 all-reduce.21
where the time goes:
time: 1760 us; the launch traced here: 1750 us
  waiting for transfers between devices  1300 us (74%)
  matrix products  170 us (10%)
  blocking collectives  141 us (8%)
  local copies, waits for them, and re-layouts  81.6 us (5%)
  other arithmetic  41.5 us (2%)
    psum x5, waiting for transfers between devices, body(): lax.psum(partial_gram, ('fsdp', 'ns'))  551 us
    psum x5, waiting for transfers between devices, body(): lax.psum(partial_gram, 'fsdp')  500 us
    reduce_scatter x1, waiting for transfers between devices, body(): lax.psum_scatter(grad_gate_up, 'fsdp', scatter_dimension=2, tiled=True)  76.4 us
    reduce_scatter x1, waiting for transfers between devices, body(): lax.psum_scatter(grad_qkv, 'fsdp', scatter_dimension=2, tiled=True)  67.3 us
    dot_general x10, matrix products, newton_schulz(): jnp.einsum('mde,mef->mdf', gram_mat, gram_mat, precision=lax.Precision.HI...  60.7 us
    reduce_scatter x1, waiting for transfers between devices, body(): lax.psum_scatter(grad_out, 'fsdp', scatter_dimension=0, tiled=True)  59 us
    psum x1, blocking collectives, body(): lax.psum((jnp.stack([gain_one_grad, gain_two_grad]), bias_grads), ('fsdp'...  39.7 us
  transfers between devices with their start and end apart: 16, of which 15 were waited for; matrix products, arithmetic and copies ran while one was open for 15% of the time, Pallas kernels for 0%

commit v1 on v0

--- a/solution.py
+++ b/solution.py
@@ -83,28 +83,26 @@
 
 
 def newton_schulz(advance, gram_total):
-    current = advance
-    for turn_idx in range(NS_ITERS):
-        gram_mat = gram_total(gram_local(current))
-        if turn_idx == 0:
-            norm_val = jnp.sqrt(jnp.trace(gram_mat, axis1=1, axis2=2))[:, None, None] + NS_EPS
-            current = current / norm_val
-            gram_mat = gram_mat / (norm_val * norm_val)
-        poly_mat = COEF_B * gram_mat + COEF_C * jnp.einsum(
+    def product(left, right):
+        return jnp.einsum(
             "mde,mef->mdf",
-            gram_mat,
-            gram_mat,
+            left,
+            right,
             precision=lax.Precision.HIGHEST,
             preferred_element_type=jnp.float32,
         )
-        current = COEF_A * current + jnp.einsum(
-            "mde,men->mdn",
-            poly_mat,
-            current,
-            precision=lax.Precision.HIGHEST,
-            preferred_element_type=jnp.float32,
-        )
-    return current
+
+    gram_mat = gram_total(gram_local(advance))
+    norm_val = jnp.sqrt(jnp.trace(gram_mat, axis1=1, axis2=2))[:, None, None] + NS_EPS
+    gram_mat = gram_mat / (norm_val * norm_val)
+    unit = jnp.eye(D, dtype=jnp.float32)[None]
+    chain = None
+    for turn_idx in range(NS_ITERS):
+        poly_mat = COEF_A * unit + COEF_B * gram_mat + COEF_C * product(gram_mat, gram_mat)
+        chain = poly_mat if chain is None else product(poly_mat, chain)
+        if turn_idx < NS_ITERS - 1:
+            gram_mat = product(product(poly_mat, gram_mat), poly_mat)
+    return product(chain, advance / norm_val)
 
 
 def adam_step(param, grad, moment, square):

time: 1760 us -> 840 us (0.48)
  waiting for transfers between devices: 1300 us -> 350 us
  matrix products: 170 us -> 213 us
    psum x5 -> x1, waiting for transfers between devices: 500 us -> 33.8 us  [body(): lax.psum(partial_gram, 'fsdp')]
    psum x5 -> x1, waiting for transfers between devices: 551 us -> 117 us  [body(): lax.psum(partial_gram, ('fsdp', 'ns'))]
    dot_general x20 -> x36, matrix products: 84.5 us -> 153 us  [product(): jnp.einsum('mde,mef->mdf', left, right, precision=lax.Precision.HIGHEST,...]
    psum x1, waiting for transfers between devices: 31.5 us -> 0.01 us  [body(): lax.psum(summed[2].astype(jnp.bfloat16), 'ns').astype(jnp.float32)]
    dot_general x10 -> x2, matrix products: 31.4 us -> 6.36 us  [gram_local(): jnp.einsum('mdn,men->mde', current, current, precision=lax.Precision.HIGH...]
  transfers between devices with their start and end apart: 16 -> 8, of which waited for: 15 -> 6; matrix products, arithmetic and copies ran while one was open for 15% -> 26% of each run, Pallas kernels for 0% -> 0%
where the time goes in v1:
time: 840 us; the launch traced here: 832 us
  waiting for transfers between devices  350 us (42%)
  matrix products  213 us (25%)
  blocking collectives  139 us (17%)
  local copies, waits for them, and re-layouts  72.3 us (9%)
  other arithmetic  42.6 us (5%)
  between operations  15.6 us (2%)
    dot_general x36, matrix products, product(): jnp.einsum('mde,mef->mdf', left, right, precision=lax.Precision.HIGHEST,...  153 us
    psum x1, waiting for transfers between devices, body(): lax.psum(partial_gram, ('fsdp', 'ns'))  117 us
    reduce_scatter x1, waiting for transfers between devices, body(): lax.psum_scatter(grad_gate_up, 'fsdp', scatter_dimension=2, tiled=True)  76.2 us
    reduce_scatter x1, waiting for transfers between devices, body(): lax.psum_scatter(grad_qkv, 'fsdp', scatter_dimension=2, tiled=True)  67.8 us
    reduce_scatter x1, waiting for transfers between devices, body(): lax.psum_scatter(grad_out, 'fsdp', scatter_dimension=0, tiled=True)  45.8 us
    psum x1, blocking collectives, body(): lax.psum((jnp.stack([gain_one_grad, gain_two_grad]), bias_grads), ('fsdp'...  38.7 us
    psum x1, waiting for transfers between devices, body(): lax.psum(partial_gram, 'fsdp')  33.8 us
    all_gather x1, blocking collectives, body(): lax.all_gather(shards[3], 'fsdp', axis=0, tiled=True)  28.4 us
  transfers between devices with their start and end apart: 8, of which 6 were waited for; matrix products, arithmetic and copies ran while one was open for 26% of the time, Pallas kernels for 0%

profile of v1, /device:TPU:15, one launch (start us, length us, event | category | flops | bytes accessed | tf_op | source)
XLA Modules:
  0.0 832.1 jit_solution(2048454603667067896)
XLA Ops:
  10.1 25.7 %all_gather.19 = bf16[3,384,384]{1,2,0:T(8,128)(2,1)S(1)} all-gather(bf16[3,384,48]{1,2,0:T(8,128)(2,1)S(1)} %convert_element_type.125), channel_id=1, replica_groups=mesh['fsdp'=8,'ns'=4] {'fsdp'}, dimensions={2}, use_global_device_ids=true | all-gather | bytes 995328 | tf_op jit(solution)/shard_map/all_gather | solution.py:151
  84.0 24.0 %all_gather.20 = bf16[384,384]{1,0:T(8,128)(2,1)S(1)} all-gather(bf16[48,384]{1,0:T(8,128)(2,1)S(1)} %convert_element_type.134), channel_id=1, replica_groups=mesh['fsdp'=8,'ns'=4] {'fsdp'}, dimensions={0}, use_global_device_ids=true | all-gather | bytes 331776 | tf_op jit(solution)/shard_map/all_gather | solution.py:152
  111.2 28.4 %all_gather.22 = bf16[1024,384]{1,0:T(8,128)(2,1)} all-gather(bf16[128,384]{1,0:T(8,128)(2,1)S(1)} %copy-done.40), channel_id=1, replica_groups=mesh['fsdp'=8,'ns'=4] {'fsdp'}, dimensions={0}, use_global_device_ids=true | all-gather | bytes 884736 | tf_op jit(solution)/shard_map/all_gather | solution.py:154
  209.3 6.3 fusion.40
  228.3 8.6 %reduce-scatter.11.cloned.1.call-done = f32[128,384]{1,0:T(8,128)} async-done(((f32[1024,384]{1,0:T(8,128)}), f32[128,384]{1,0:T(8,128)}) %reduce-scatter.11.cloned.1.call-update) | async-done | bytes 196624 | tf_op jit(solution)/shard_map/reduce_scatter | solution.py:294
  238.5 67.8 %reduce-scatter.5.cloned.1.call-done = f32[3,384,48]{1,2,0:T(8,128)} async-done(((f32[3,384,384]{1,2,0:T(8,128)}), f32[3,384,48]{1,2,0:T(8,128)}) %reduce-scatter.5.cloned.1.call-update) | async-done | bytes 221200 | tf_op jit(solution)/shard_map/reduce_scatter | solution.py:291
  307.9 76.2 %reduce-scatter.9.cloned.1.call-done = f32[2,384,128]{1,2,0:T(8,128)} async-done(((f32[2,384,1024]{1,2,0:T(8,128)}), f32[2,384,128]{1,2,0:T(8,128)}) %reduce-scatter.9.cloned.1.call-update) | async-done | bytes 393232 | tf_op jit(solution)/shard_map/reduce_scatter | solution.py:293
  392.7 38.7 %all-reduce = (f32[2,384]{1,0:T(2,128)S(1)}, f32[2,6]{1,0:T(2,128)S(1)}) all-reduce(f32[2,384]{1,0:T(2,128)S(1)} %pad_maximum_fusion.15, f32[2,6]{1,0:T(2,128)S(1)} %pad_maximum_fusion.16), channel_id=1, replica_groups=mesh['fsdp'=8,'ns'=4] {'fsdp','ns'}, use_global_device_ids=true, to_apply=%region_21.22 | all-reduce | flops 780 | bytes 6240 | tf_op jit(solution)/shard_map/psum | solution.py:302
  438.3 45.8 %reduce-scatter.7.cloned.1.call-done = f32[48,384]{1,0:T(8,128)} async-done(((f32[384,384]{1,0:T(8,128)}), f32[48,384]{1,0:T(8,128)}) %reduce-scatter.7.cloned.1.call-update) | async-done | bytes 73744 | tf_op jit(solution)/shard_map/reduce_scatter | solution.py:292
  485.1 12.4 %psum.57 = bf16[48,384]{1,0:T(8,128)(2,1)S(1)} all-reduce(bf16[48,384]{1,0:T(8,128)(2,1)S(1)} %convert_element_type.151), channel_id=1, replica_groups=mesh['fsdp'=8,'ns'=4] {'ns'}, use_global_device_ids=true, to_apply=%region_10.11 | all-reduce | flops 18432 | bytes 73728 | tf_op jit(solution)/shard_map/psum | solution.py:298
  504.3 116.7 %all-reduce.8.cloned.1.call-done = f32[3,384,384]{2,1,0:T(8,128)} async-done(((f32[3,384,384]{2,1,0:T(8,128)}), f32[3,384,384]{2,1,0:T(8,128)}) %all-reduce.8.cloned.1.call-update) | async-done | bytes 1769488 | tf_op jit(solution)/shard_map/psum | solution.py:318
  688.3 9.7 %all_gather.23 = f32[3,384,128]{1,2,0:T(8,128)S(1)} all-gather(f32[3,384,32]{1,2,0:T(8,128)S(1)} %fusion.181), channel_id=1, replica_groups=mesh['fsdp'=8,'ns'=4] {'ns'}, dimensions={2}, use_global_device_ids=true | all-gather | bytes 737280 | tf_op jit(solution)/shard_map/all_gather | solution.py:319
  699.8 33.8 %all-reduce.6.cloned.1.call-done = f32[4,384,384]{2,1,0:T(8,128)} async-done(((f32[4,384,384]{2,1,0:T(8,128)}), f32[4,384,384]{2,1,0:T(8,128)}) %all-reduce.6.cloned.1.call-update) | async-done | bytes 2359312 | tf_op jit(solution)/shard_map/psum | solution.py:315
  740.7 5.1 fusion.34
  745.8 5.2 fusion.33
  755.7 5.3 fusion.29
  770.5 4.9 fusion.23
  775.4 5.2 fusion.27
  780.7 5.0 fusion.21
  785.7 5.0 fusion.22
  790.7 5.2 fusion.263
  800.8 4.9 fusion.15
  805.7 5.3 fusion.16
  815.7 5.3 fusion.10
  (291 shorter events, 265.9 us)
Async XLA Ops:
  7.2 28.6 %copy-start.31 = (bf16[1024,384]{1,0:T(8,128)(2,1)S(1)}, bf16[1024,384]{1,0:T(8,128)(2,1)}, u32[]{:S(2)}) copy-start(bf16[1024,384]{1,0:T(8,128)(2,1)} %param.19) | copy-start | bytes 2359300
  7.2 28.9 %copy-start.55 = (f32[2,384]{1,0:T(2,128)S(1)}, f32[2,384]{1,0:T(2,128)}, u32[]{:S(2)}) copy-start(f32[2,384]{1,0:T(2,128)} %param.32) | copy-start | bytes 9220
  7.2 132.4 %all-gather.2.cloned.1.call-start = ((), (), s32[]{:S(2)}) async-start(), calls=%async_computation.4 | async-start | bytes 1769472 | tf_op jit(solution)/shard_map/all_gather | solution.py:153
  9.0 227.9 %reduce-scatter.11.cloned.1.call-start = ((), (), s32[]{:S(2)}) async-start(), calls=%async_computation.8 | async-start | bytes 1769472 | tf_op jit(solution)/shard_map/reduce_scatter | solution.py:294
  10.1 26.3 %copy-start.49 = (s32[16,64]{1,0:T(8,128)S(1)}, s32[16,64]{1,0:T(8,128)}, u32[]{:S(2)}) copy-start(s32[16,64]{1,0:T(8,128)} %param.22) | copy-start | bytes 12292
  10.1 27.3 %copy-start.57 = (f32[2,6]{1,0:T(2,128)S(1)}, f32[2,6]{1,0:T(2,128)}, u32[]{:S(2)}) copy-start(f32[2,6]{1,0:T(2,128)} %param.33) | copy-start | bytes 148
  77.5 6.5 copy-start.52
  152.9 153.4 %reduce-scatter.5.cloned.1.call-start = ((), (), s32[]{:S(2)}) async-start(), calls=%async_computation.5 | async-start | bytes 1990656 | tf_op jit(solution)/shard_map/reduce_scatter | solution.py:291
  207.9 176.2 %reduce-scatter.9.cloned.1.call-start = ((), (), s32[]{:S(2)}) async-start(), calls=%async_computation.7 | async-start | bytes 3538944 | tf_op jit(solution)/shard_map/reduce_scatter | solution.py:293
  215.7 216.4 %all-reduce.10.cloned.1.call-start = ((), (), s32[]{:S(2)}) async-start(), calls=%async_computation.11 | async-start | bytes 811008 | tf_op jit(solution)/shard_map/psum | solution.py:299
  385.8 98.4 %reduce-scatter.7.cloned.1.call-start = ((), (), s32[]{:S(2)}) async-start(), calls=%async_computation.6 | async-start | bytes 663552 | tf_op jit(solution)/shard_map/reduce_scatter | solution.py:292
  386.3 234.7 %all-reduce.8.cloned.1.call-start = ((), (), s32[]{:S(2)}) async-start(), calls=%async_computation.10 | async-start | bytes 3538944 | tf_op jit(solution)/shard_map/psum | solution.py:318
  389.1 42.3 %copy-start.56 = (f32[2,384]{1,0:T(2,128)S(1)}, f32[2,384]{1,0:T(2,128)}, u32[]{:S(2)}) copy-start(f32[2,384]{1,0:T(2,128)} %param.32) | copy-start | bytes 9220
  389.1 42.3 %copy-start.60 = (f32[2,384]{1,0:T(2,128)S(1)}, f32[2,384]{1,0:T(2,128)}, u32[]{:S(2)}) copy-start(f32[2,384]{1,0:T(2,128)} %param.35) | copy-start | bytes 9220
  389.1 42.3 %copy-start.61 = (f32[2,384]{1,0:T(2,128)S(1)}, f32[2,384]{1,0:T(2,128)}, u32[]{:S(2)}) copy-start(f32[2,384]{1,0:T(2,128)} %param.34) | copy-start | bytes 9220
  389.1 43.0 %copy-start.48 = (f32[128,384]{1,0:T(8,128)S(1)}, f32[128,384]{1,0:T(8,128)}, u32[]{:S(2)}) copy-start(f32[128,384]{1,0:T(8,128)} %param.31) | copy-start | bytes 589828
  389.1 44.6 %copy-start.24 = (f32[2,384,128]{1,2,0:T(8,128)S(1)}, f32[2,384,128]{1,2,0:T(8,128)}, u32[]{:S(2)}) copy-start(f32[2,384,128]{1,2,0:T(8,128)} %copy.106) | copy-start | bytes 1179652
  431.5 6.3 copy-start.66
  434.8 62.7 %copy-start.51 = (f32[48,384]{1,0:T(8,128)S(1)}, f32[48,384]{1,0:T(8,128)}, u32[]{:S(2)}) copy-start(f32[48,384]{1,0:T(8,128)} %param.29) | copy-start | bytes 221188
  434.8 63.3 %copy-start.39 = (bf16[2,384,128]{1,2,0:T(8,128)(2,1)S(1)}, bf16[2,384,128]{1,2,0:T(8,128)(2,1)}, u32[]{:S(2)}) copy-start(bf16[2,384,128]{1,2,0:T(8,128)(2,1)} %get-tuple-element.76) | copy-start | bytes 589828
  437.6 62.3 %copy-start.47 = (f32[3,384,48]{1,2,0:T(8,128)S(1)}, f32[3,384,48]{1,2,0:T(8,128)}, u32[]{:S(2)}) copy-start(f32[3,384,48]{1,2,0:T(8,128)} %param.28) | copy-start | bytes 663556
  437.6 62.3 %copy-start.50 = (bf16[3,384,48]{1,2,0:T(8,128)(2,1)S(1)}, bf16[3,384,48]{1,2,0:T(8,128)(2,1)}, u32[]{:S(2)}) copy-start(bf16[3,384,48]{1,2,0:T(8,128)(2,1)} %get-tuple-element.77) | copy-start | bytes 331780
  437.7 295.9 %all-reduce.6.cloned.1.call-start = ((), (), s32[]{:S(2)}) async-start(), calls=%async_computation.9 | async-start | bytes 4718592 | tf_op jit(solution)/shard_map/psum | solution.py:315
  688.3 10.7 %copy-start.37 = (f32[128,384]{1,0:T(8,128)S(1)}, f32[128,384]{1,0:T(8,128)}, u32[]{:S(2)}) copy-start(f32[128,384]{1,0:T(8,128)} %param.27) | copy-start | bytes 589828
  (56 other events, 158.1 us)
Sparse Core Ops, SparseCore 0:
  10.7 47.3 all-gather.1
  153.0 83.8 reduce-scatter.10
  240.8 65.4 reduce-scatter.4
  309.7 74.2 reduce-scatter.8
  387.6 31.5 all-reduce.9
  422.7 61.4 reduce-scatter.6
  489.5 131.4 all-reduce.7
  624.6 108.9 all-reduce.5

commit v2 on v1

v2 whole, which is shorter than its diff:
```python
import functools
import math

import jax
import jax.numpy as jnp
from jax import lax
from jax.experimental import pallas as pl
from jax.experimental.pallas import tpu as pltpu
from jax.sharding import PartitionSpec as P

HEAD_DIM = 64
BUCKET = 64
TIME_SLOTS = 64
NS_ITERS = 5
STEP = 10

EPS_NORM = 1e-06
ROPE_BASE = 10000.0
NEG_FILL = -1000000000.0
COEF_A = 3.4445
COEF_B = -4.775
COEF_C = 2.0315
NS_EPS = 1e-07
MUON_MU = 0.95
MUON_RATE = 0.25
MUON_DECAY = 0.01
ADAM_RATE = 0.8
BETA_ONE = 0.9
BETA_TWO = 0.95
ADAM_EPS = 1e-08

LOW = jnp.bfloat16
WIDE = jnp.float32
BLOCK = 256
PAIR = 2 * BUCKET
LANES = 2 * HEAD_DIM
WHOLE = pl.BlockSpec(memory_space=pltpu.VMEM)
SCALARS = pl.BlockSpec(memory_space=pltpu.SMEM)


def mul_nn(left, right):
    return lax.dot_general(left, right, (((1,), (0,)), ((), ())), preferred_element_type=WIDE)


def mul_nt(left, right):
    return lax.dot_general(left, right, (((1,), (1,)), ((), ())), preferred_element_type=WIDE)


def mul_tn(left, right):
    return lax.dot_general(left, right, (((0,), (0,)), ((), ())), preferred_element_type=WIDE)


def offsets(attn_rows, ff_rows):
    counts = [attn_rows] * 4 + [ff_rows] * 3
    starts = [sum(counts[:i]) for i in range(7)]
    return list(zip(starts, counts))


def layer_kernel(
    pieces,
    lengths,
    bias,
    tok_ref,
    cot_ref,
    var_ref,
    time_ref,
    table_ref,
    gain_ref,
    w_ref,
    out_ref,
    gtok_ref,
    grad_ref,
    ggain_ref,
    gbias_ref,
    n1_s,
    n2_s,
    att_s,
    gml_s,
    hid_s,
    glow_s,
    gg_s,
    gu_s,
    gqkv_s,
):
    step = pl.program_id(0)
    rows, width = tok_ref.shape
    heads = bias.shape[1]
    here = pl.ds(pl.multiple_of(step * rows, rows), rows)

    def weight(first, last):
        parts = []
        for i in range(first, last):
            start, count = pieces[i]
            part = w_ref[:, start : start + count, :]
            parts.append(part.reshape(part.shape[0] * count, width))
        return parts[0] if len(parts) == 1 else jnp.concatenate(parts, axis=0)

    @pl.when(step == 0)
    def _():
        ggain_ref[...] = jnp.zeros_like(ggain_ref)
        gbias_ref[...] = jnp.zeros_like(gbias_ref)

    lane = lax.broadcasted_iota(jnp.int32, (1, LANES), 1)
    low_head = lane < HEAD_DIM
    low_half = lane % HEAD_DIM < HEAD_DIM // 2
    per_block = rows // PAIR
    var_rows = var_ref[pl.ds(step * per_block, per_block), :]
    time_rows = time_ref[pl.ds(step * per_block, per_block), :]
    filler = jnp.zeros((8 - 2 * per_block, PAIR), WIDE)
    columns = jnp.concatenate([var_rows, time_rows, filler], axis=0).T
    slots = lax.broadcasted_iota(jnp.int32, (1, TIME_SLOTS), 1).astype(WIDE)
    hot = jnp.concatenate(
        [(columns[:, per_block + p : per_block + p + 1] == slots) for p in range(per_block)], axis=0
    ).astype(LOW)
    looked = mul_nn(hot, table_ref[0]) + mul_nn(hot, table_ref[1]) + mul_nn(hot, table_ref[2])
    cosine = looked[:, :LANES]
    sine = looked[:, LANES:]

    def swapped(values):
        half = HEAD_DIM // 2
        return jnp.where(
            low_half, pltpu.roll(values, LANES - half, 1), pltpu.roll(values, half, 1)
        )

    gain_one = gain_ref[0:1, :]
    gain_two = gain_ref[1:2, :]
    tokens = tok_ref[...].astype(WIDE)
    scale_one = lax.rsqrt(jnp.mean(tokens * tokens, axis=-1, keepdims=True) + EPS_NORM)
    unit_one = tokens * scale_one
    normed_one = (unit_one * gain_one).astype(LOW)
    n1_s[here, :] = normed_one
    qkv = mul_nt(normed_one, weight(0, 3))

    query_scale = HEAD_DIM ** (-0.5)
    units = []
    attended = []
    row_id = lax.broadcasted_iota(jnp.int32, (PAIR, 1), 0)
    lane_id = lax.broadcasted_iota(jnp.int32, (1, PAIR), 1)
    same_bucket = (row_id < BUCKET) == (lane_id < BUCKET)
    masks = []
    live_cols = []
    for p in range(per_block):
        first = lengths[(step * per_block + p) * 2]
        second = lengths[(step * per_block + p) * 2 + 1]
        live_key = lane_id % BUCKET < jnp.where(lane_id < BUCKET, first, second)
        live_cols.append(row_id % BUCKET < jnp.where(row_id < BUCKET, first, second))
        mask = same_bucket & live_key
        same_var = columns[:, p : p + 1] == var_rows[p : p + 1, :]
        masks.append((mask, same_var))

    for hp in range(heads // 2):
        cols = slice(hp * LANES, (hp + 1) * LANES)
        q = qkv[:, cols]
        k = qkv[:, width + hp * LANES : width + (hp + 1) * LANES]
        v = qkv[:, 2 * width + hp * LANES : 2 * width + (hp + 1) * LANES].astype(LOW)
        q = ((q * cosine + swapped(q) * sine) * query_scale).astype(LOW)
        k = (k * cosine + swapped(k) * sine).astype(LOW)
        q_first = jnp.where(low_head, q, jnp.zeros_like(q))
        q_second = jnp.where(low_head, jnp.zeros_like(q), q)
        att_pairs = []
        for p in range(per_block):
            part = slice(p * PAIR, (p + 1) * PAIR)
            mask, same_var = masks[p]
            q2 = jnp.concatenate([q_first[part], q_second[part]], axis=0)
            kp = k[part]
            vp = v[part]
            raw = mul_nt(q2, kp)
            halves = []
            for j in range(2):
                h = 2 * hp + j
                biased = raw[j * PAIR : (j + 1) * PAIR] + jnp.where(
                    same_var, bias[0, h], bias[1, h]
                )
                halves.append(jnp.where(mask, biased, NEG_FILL))
            scores = jnp.concatenate(halves, axis=0)
            top = jnp.max(scores, axis=-1, keepdims=True)
            exponent = jnp.exp(scores - top)
            probs = exponent / jnp.sum(exponent, axis=-1, keepdims=True)
            probs_low = probs.astype(LOW)
            both = mul_nn(probs_low, vp)
            att_pairs.append(jnp.where(low_head, both[:PAIR], both[PAIR:]))
            units.append((hp, p, q2, kp, vp, probs, probs_low))
        attended.append(jnp.concatenate(att_pairs, axis=0).astype(LOW))
    attended = jnp.concatenate(attended, axis=1)
    att_s[here, :] = attended
    w_out = weight(3, 4)
    mid = tokens + mul_nn(attended, w_out)
    scale_two = lax.rsqrt(jnp.mean(mid * mid, axis=-1, keepdims=True) + EPS_NORM)
    unit_two = mid * scale_two
    normed_two = (unit_two * gain_two).astype(LOW)
    n2_s[here, :] = normed_two
    w_gate = weight(4, 5)
    w_up = weight(5, 6)
    w_down = weight(6, 7)
    gate = mul_nt(normed_two, w_gate)
    up = mul_nt(normed_two, w_up)
    sig = 1.0 / (1.0 + jnp.exp(-gate))
    silu = gate * sig
    hidden = (silu * up).astype(LOW)
    hid_s[here, :] = hidden
    out_ref[...] = (mid + mul_nn(hidden, w_down)).astype(LOW)

    live_row = jnp.concatenate(live_cols, axis=0)
    g_out = jnp.where(live_row, cot_ref[...].astype(WIDE), 0.0)
    g_low = g_out.astype(LOW)
    glow_s[here, :] = g_low
    g_hidden = mul_nt(g_low, w_down)
    g_gate = (g_hidden * up * sig * (1.0 + gate * (1.0 - sig))).astype(LOW)
    g_up = (g_hidden * silu).astype(LOW)
    gg_s[here, :] = g_gate
    gu_s[here, :] = g_up
    e_two = mul_nn(g_gate, w_gate) + mul_nn(g_up, w_up)
    ggain_ref[1:2, :] += jnp.sum(e_two * unit_two, axis=0, keepdims=True)
    scaled = e_two * gain_two
    g_mid = g_out + scale_two * (
        scaled - unit_two * jnp.mean(scaled * unit_two, axis=-1, keepdims=True)
    )
    g_mid_low = g_mid.astype(LOW)
    gml_s[here, :] = g_mid_low
    g_att = mul_nt(g_mid_low, w_out).astype(LOW)

    parts_q = [[None] * per_block for _ in range(heads // 2)]
    parts_k = [[None] * per_block for _ in range(heads // 2)]
    parts_v = [[None] * per_block for _ in range(heads // 2)]
    for hp, p, q2, kp, vp, probs, probs_low in units:
        part = slice(p * PAIR, (p + 1) * PAIR)
        mask, same_var = masks[p]
        ga = g_att[part, hp * LANES : (hp + 1) * LANES]
        ga2 = jnp.concatenate(
            [
                jnp.where(low_head, ga, jnp.zeros_like(ga)),
                jnp.where(low_head, jnp.zeros_like(ga), ga),
            ],
            axis=0,
        )
        g_probs = mul_nt(ga2, vp)
        row_dot = jnp.sum(probs * g_probs, axis=-1, keepdims=True)
        g_scores = probs * (g_probs - row_dot)
        for j in range(2):
            h = 2 * hp + j
            mine = g_scores[j * PAIR : (j + 1) * PAIR]
            gbias_ref[h : h + 1, :] += jnp.sum(
                jnp.where(same_var, mine, 0.0), axis=0, keepdims=True
            )
            gbias_ref[8 + h : 9 + h, :] += jnp.sum(
                jnp.where(same_var, 0.0, mine), axis=0, keepdims=True
            )
        low_scores = g_scores.astype(LOW)
        both = mul_nn(low_scores, kp)
        parts_q[hp][p] = jnp.where(low_head, both[:PAIR], both[PAIR:])
        parts_k[hp][p] = mul_tn(low_scores, q2)
        parts_v[hp][p] = mul_tn(probs_low, ga2)
    g_q = []
    g_k = []
    g_v = []
    for hp in range(heads // 2):
        dq = jnp.concatenate(parts_q[hp], axis=0)
        dk = jnp.concatenate(parts_k[hp], axis=0)
        g_q.append(((dq * cosine - swapped(dq) * sine) * query_scale).astype(LOW))
        g_k.append((dk * cosine - swapped(dk) * sine).astype(LOW))
        g_v.append(jnp.concatenate(parts_v[hp], axis=0).astype(LOW))
    g_qkv = jnp.concatenate(g_q + g_k + g_v, axis=1)
    gqkv_s[here, :] = g_qkv
    e_one = mul_nn(g_qkv, weight(0, 3))
    ggain_ref[0:1, :] += jnp.sum(e_one * unit_one, axis=0, keepdims=True)
    scaled = e_one * gain_one
    gtok_ref[...] = (
        g_mid
        + scale_one * (scaled - unit_one * jnp.mean(scaled * unit_one, axis=-1, keepdims=True))
    ).astype(LOW)

    @pl.when(step == pl.num_programs(0) - 1)
    def _():
        def put(index, left, right):
            start, count = pieces[index]
            grad_ref[:, start : start + count, :] = (
                mul_tn(left, right)
                .reshape(grad_ref.shape[0], count, width)
                .astype(grad_ref.dtype)
            )

        for j in range(3):
            put(j, gqkv_s[:, j * width : (j + 1) * width], n1_s[...])
        put(3, att_s[...], gml_s[...])
        put(4, gg_s[...], n2_s[...])
        put(5, gu_s[...], n2_s[...])
        put(6, hid_s[...], glow_s[...])


def layer(tokens, cotangent, lengths, variates, times, packed, gains, attn_bias, ff, grad_type):
    rows, width = tokens.shape
    heads = attn_bias.shape[1]
    copies, shard_rows, _ = packed.shape
    pieces = offsets(heads * HEAD_DIM // copies, ff // copies)
    half = HEAD_DIM // 2
    frequency = ROPE_BASE ** (-2.0 * jnp.arange(half, dtype=WIDE) / HEAD_DIM)
    angles = jnp.arange(TIME_SLOTS, dtype=WIDE)[:, None] * frequency[None, :]
    cosine, sine = jnp.cos(angles), jnp.sin(angles)
    table = jnp.concatenate([cosine] * 4 + [-sine, sine, -sine, sine], axis=1)
    first = table.astype(LOW)
    rest = table - first.astype(WIDE)
    second = rest.astype(LOW)
    third = (rest - second.astype(WIDE)).astype(LOW)
    table = jnp.stack([first, second, third])
    grid = rows // BLOCK
    block = pl.BlockSpec((BLOCK, width), lambda i: (i, 0))
    low_scratch = lambda columns: pltpu.VMEM((rows, columns), LOW)
    return pl.pallas_call(
        functools.partial(layer_kernel, pieces),
        grid=(grid,),
        out_shape=(
            jax.ShapeDtypeStruct((rows, width), LOW),
            jax.ShapeDtypeStruct((rows, width), LOW),
            jax.ShapeDtypeStruct((copies, shard_rows, width), grad_type),
            jax.ShapeDtypeStruct((2, width), WIDE),
            jax.ShapeDtypeStruct((16, PAIR), WIDE),
        ),
        in_specs=[SCALARS, SCALARS, block, block, WHOLE, WHOLE, WHOLE, WHOLE, WHOLE],
        out_specs=(block, block, WHOLE, WHOLE, WHOLE),
        scratch_shapes=[
            low_scratch(width),
            low_scratch(width),
            low_scratch(width),
            low_scratch(width),
            low_scratch(ff),
            low_scratch(width),
            low_scratch(ff),
            low_scratch(ff),
            low_scratch(3 * width),
        ],
        compiler_params=pltpu.CompilerParams(vmem_limit_bytes=58 << 20),
        name="layer",
    )(
        lengths,
        attn_bias,
        tokens,
        cotangent,
        variates.astype(WIDE).reshape(rows // PAIR, PAIR),
        times.astype(WIDE).reshape(rows // PAIR, PAIR),
        table,
        gains,
        packed,
    )


def pack(qkv, out, gate_up, down):
    width = out.shape[-1]
    return jnp.concatenate(
        [
            jnp.swapaxes(qkv, 1, 2).reshape(-1, width),
            out,
            jnp.swapaxes(gate_up, 1, 2).reshape(-1, width),
            down,
        ],
        axis=0,
    )


def unpack(packed, attn_rows, ff_rows):
    width = packed.shape[-1]
    qkv = jnp.swapaxes(packed[: 3 * attn_rows].reshape(3, attn_rows, width), 1, 2)
    out = packed[3 * attn_rows : 4 * attn_rows]
    ends = 4 * attn_rows + 2 * ff_rows
    gate_up = jnp.swapaxes(packed[4 * attn_rows : ends].reshape(2, ff_rows, width), 1, 2)
    return qkv, out, gate_up, packed[ends:]


def newton_schulz(gram_mat):
    def product(left, right):
        return jnp.einsum(
            "mde,mef->mdf",
            left,
            right,
            precision=lax.Precision.HIGHEST,
            preferred_element_type=WIDE,
        )

    norm_val = jnp.sqrt(jnp.trace(gram_mat, axis1=1, axis2=2))[:, None, None] + NS_EPS
    gram_mat = gram_mat / (norm_val * norm_val)
    unit = jnp.eye(gram_mat.shape[-1], dtype=WIDE)[None]
    chain = None
    for turn_idx in range(NS_ITERS):
        poly_mat = COEF_A * unit + COEF_B * gram_mat + COEF_C * product(gram_mat, gram_mat)
        chain = poly_mat if chain is None else product(poly_mat, chain)
        if turn_idx < NS_ITERS - 1:
            gram_mat = product(product(poly_mat, gram_mat), poly_mat)
    return chain / norm_val


def adam_step(param, grad, moment, square):
    new_moment = BETA_ONE * moment + (1.0 - BETA_ONE) * grad
    new_square = BETA_TWO * square + (1.0 - BETA_TWO) * grad * grad
    corrected = new_moment / (1.0 - BETA_ONE**STEP)
    scaled = jnp.sqrt(new_square / (1.0 - BETA_TWO**STEP)) + ADAM_EPS
    return (new_moment, new_square, param - ADAM_RATE * corrected / scaled)


def body(
    tokens,
    cotangent,
    lengths,
    variates,
    times,
    weight_qkv,
    weight_out,
    weight_gate_up,
    weight_down,
    momentum_qkv,
    momentum_out,
    momentum_gate_up,
    momentum_down,
    gains,
    attn_bias,
    gain_moment,
    gain_square,
    bias_moment,
    bias_square,
):
    width = tokens.shape[1]
    heads = attn_bias.shape[1]
    attn_rows = weight_out.shape[0]
    ff_rows = weight_down.shape[0]
    fsdp = lax.axis_size("fsdp")
    ff = ff_rows * fsdp
    attn_width = attn_rows * fsdp
    weights = pack(weight_qkv, weight_out, weight_gate_up, weight_down)
    momenta = pack(momentum_qkv, momentum_out, momentum_gate_up, momentum_down)
    full = lax.all_gather(weights.astype(LOW), "fsdp", axis=0, tiled=False)
    aligned = attn_rows % 16 == 0 and ff_rows % 16 == 0
    pieces = offsets(attn_rows, ff_rows)
    if not aligned:
        full = jnp.concatenate(
            [full[:, s : s + n].reshape(1, fsdp * n, width) for s, n in pieces], axis=1
        )
    out_tokens, grad_tokens, grads, gain_rows, bias_rows = layer(
        tokens, cotangent, lengths, variates, times, full, gains, attn_bias, ff, WIDE
    )
    if not aligned:
        wholes = offsets(attn_width, ff)
        grads = jnp.concatenate(
            [grads[0, s : s + n].reshape(fsdp, n // fsdp, width) for s, n in wholes], axis=1
        )
    summed = lax.psum_scatter(grads, "fsdp", scatter_dimension=0, tiled=False)
    grad_rows = lax.psum(summed.astype(LOW), "ns").astype(WIDE)
    bias_part = jnp.sum(bias_rows, axis=1).reshape(2, 8)[:, :heads]
    grad_gains, grad_bias = lax.psum((gain_rows, bias_part), ("fsdp", "ns"))

    new_momenta = MUON_MU * momenta + grad_rows
    advance = grad_rows + MUON_MU * new_momenta
    parts = [advance[s : s + n] for s, n in pieces]
    grams = jnp.stack(
        [
            lax.dot_general(
                y,
                y,
                (((0,), (0,)), ((), ())),
                precision=lax.Precision.HIGHEST,
                preferred_element_type=WIDE,
            )
            for y in parts
        ]
    )
    factor = newton_schulz(lax.psum(grams, "fsdp"))
    shrink = 1.0 - MUON_RATE * MUON_DECAY
    scale_attn = MUON_RATE * 0.2 * math.sqrt(max(width, attn_width))
    scale_ff = MUON_RATE * 0.2 * math.sqrt(max(width, ff))
    turned = jnp.concatenate(
        [
            (scale_attn if i < 4 else scale_ff)
            * jnp.dot(
                y, factor[i], precision=lax.Precision.HIGHEST, preferred_element_type=WIDE
            )
            for i, y in enumerate(parts)
        ],
        axis=0,
    )
    new_weights = weights * shrink - turned
    new_gain_moment, new_gain_square, new_gains = adam_step(
        gains, grad_gains, gain_moment, gain_square
    )
    new_bias_moment, new_bias_square, new_bias = adam_step(
        attn_bias, grad_bias, bias_moment, bias_square
    )
    return (
        out_tokens,
        grad_tokens,
        *unpack(grad_rows, attn_rows, ff_rows),
        *unpack(new_momenta, attn_rows, ff_rows),
        *unpack(new_weights, attn_rows, ff_rows),
        grad_gains,
        new_gain_moment,
        new_gain_square,
        new_gains,
        grad_bias,
        new_bias_moment,
        new_bias_square,
        new_bias,
    )


def solution(mesh):
    rows = P(("fsdp", "ns"), None)
    line = P(("fsdp", "ns"))
    matrices = (P(None, None, "fsdp"), P("fsdp", None), P(None, None, "fsdp"), P("fsdp", None))
    return jax.shard_map(
        body,
        mesh=mesh,
        in_specs=(rows, rows, line, rows, line, *matrices, *matrices, *([P()] * 6)),
        out_specs=(rows, rows, *matrices, *matrices, *matrices, *([P()] * 8)),
        check_vma=False,
    )
```

time: 840 us -> 650 us (0.77)
  blocking collectives: 139 us -> 44.6 us
  local copies, waits for them, and re-layouts: 72.3 us -> 11.6 us
  Pallas kernels: 0 us -> 38.2 us
  other arithmetic: 42.6 us -> 15.1 us
  waiting for transfers between devices: 350 us -> 323 us
  matrix products: 213 us -> 191 us
    all_gather x4 -> x0, blocking collectives: 87.8 us -> none  [the longest x1 28.4 us: body(): lax.all_gather(shards[3], 'fsdp', axis=0, tiled=True)]
    reduce_scatter x4 -> x1, waiting for transfers between devices: 198 us -> 129 us  [body(): summed = lax.psum_scatter(grads, 'fsdp', scatter_dimension=0, tiled=False)]
    all_gather x1, waiting for transfers between devices: 0.01 us -> 60.3 us  [body(): full = lax.all_gather(weights.astype(LOW), 'fsdp', axis=0, tiled=False)]
    dot_general x20 -> x14, matrix products: 59.9 us -> 14 us  [the longest x7 10.5 us: body(): lax.dot_general(y, y, (((0,), (0,)), ((), ())), precision=lax.Precision.H...]
    pallas_call x0 -> x1, Pallas kernels: none -> 38.2 us  [layer(): pl.pallas_call(functools.partial(layer_kernel, pieces), grid=(grid,), out...]
    dot_general x36 -> x17, matrix products: 153 us -> 177 us  [product(): jnp.einsum('mde,mef->mdf', left, right, precision=lax.Precision.HIGHEST,...]
    unnamed x153 -> x50, local copies, waits for them, and re-layouts: 18 us -> 0.56 us
    psum x3 -> x2, waiting for transfers between devices: 151 us -> 134 us  [the longest x1 102 us: body(): factor = newton_schulz(lax.psum(grams, 'fsdp'))]
  transfers between devices with their start and end apart: 8 -> 4, of which waited for: 6 -> 4; matrix products, arithmetic and copies ran while one was open for 26% -> 2% of each run, Pallas kernels for 0% -> 0%
where the time goes in v2:
time: 650 us; the launch traced here: 638 us
  waiting for transfers between devices  323 us (50%)
  matrix products  191 us (29%)
  blocking collectives  44.6 us (7%)
  Pallas kernels  38.2 us (6%)
  other arithmetic  15.1 us (2%)
  between operations  14.7 us (2%)
  local copies, waits for them, and re-layouts  11.6 us (2%)
    dot_general x17, matrix products, product(): jnp.einsum('mde,mef->mdf', left, right, precision=lax.Precision.HIGHEST,...  177 us
    reduce_scatter x1, waiting for transfers between devices, body(): summed = lax.psum_scatter(grads, 'fsdp', scatter_dimension=0, tiled=False)  129 us
    psum x1, waiting for transfers between devices, body(): factor = newton_schulz(lax.psum(grams, 'fsdp'))  102 us
    all_gather x1, waiting for transfers between devices, body(): full = lax.all_gather(weights.astype(LOW), 'fsdp', axis=0, tiled=False)  60.3 us
    psum x1, blocking collectives, body(): grad_gains, grad_bias = lax.psum((gain_rows, bias_part), ('fsdp', 'ns'))  44.6 us
    pallas_call x1, Pallas kernels, layer(): pl.pallas_call(functools.partial(layer_kernel, pieces), grid=(grid,), out...  38.2 us
    psum x1, waiting for transfers between devices, body(): grad_rows = lax.psum(summed.astype(LOW), 'ns').astype(WIDE)  31.7 us
  transfers between devices with their start and end apart: 4, of which 4 were waited for; matrix products, arithmetic and copies ran while one was open for 2% of the time, Pallas kernels for 0%

profile of v2, /device:TPU:15, one launch (start us, length us, event | category | flops | bytes accessed | tf_op | source)
XLA Modules:
  0.0 638.5 jit_solution(12107876875633660555)
XLA Ops:
  15.7 60.3 %all-gather.2.cloned.1.call-done.w_ref = bf16[8,576,384]{2,1,0:T(8,128)(2,1)} async-done(((bf16[1,576,384]{2,1,0:T(8,128)(2,1)}), bf16[8,576,384]{2,1,0:T(8,128)(2,1)}) %all-gather.2.cloned.1.call-update) | async-done | bytes 3538960 | tf_op jit(solution)/shard_map/all_gather | solution.py:428
  76.0 38.2 %layer.1 = (bf16[1024,384]{1,0:T(8,128)(2,1)}, bf16[1024,384]{1,0:T(8,128)(2,1)}, f32[8,576,384]{2,1,0:T(8,128)}, f32[2,384]{1,0:T(2,128)}, f32[16,128]{1,0:T(8,128)}) custom-call(s32[16]{0:T(128)} %lengths.1, f32[2,6]{1,0:T(2,128)} %bias.1, bf16[1024,384]{1,0:T(8,128)(2,1)} %tok_ref.1, bf16[1024,384]{1,0:T(8,128)(2,1)} %cot_ref.1, ...), custom_call_target="tpu_custom_call" | custom-call | tf_op jit(solution)/shard_map/layer/pallas_call | solution.py:308
  114.4 128.9 %reduce-scatter.2.cloned.1.call-done = f32[1,576,384]{2,1,0:T(8,128)} async-done(((f32[8,576,384]{2,1,0:T(8,128)}), f32[1,576,384]{2,1,0:T(8,128)}) %reduce-scatter.2.cloned.1.call-update) | async-done | bytes 884752 | tf_op jit(solution)/shard_map/reduce_scatter | solution.py:443
  245.8 31.7 %all-reduce.4.cloned.1.call-done = bf16[576,384]{1,0:T(8,128)(2,1)} async-done(((bf16[576,384]{1,0:T(8,128)(2,1)}), bf16[576,384]{1,0:T(8,128)(2,1)}) %all-reduce.4.cloned.1.call-update) | async-done | bytes 442384 | tf_op jit(solution)/shard_map/psum | solution.py:444
  290.6 44.6 %all-reduce = (f32[2,384]{1,0:T(2,128)S(1)}, f32[2,6]{1,0:T(2,128)S(1)}) all-reduce(f32[2,384]{1,0:T(2,128)S(1)} %copy-done.17, f32[2,6]{1,0:T(2,128)S(1)} %bitcast.128), channel_id=1, replica_groups=mesh['fsdp'=8,'ns'=4] {'fsdp','ns'}, use_global_device_ids=true, to_apply=%region_4.0 | all-reduce | flops 780 | bytes 6240 | tf_op jit(solution)/shard_map/psum | solution.py:446
  342.4 101.9 %all-reduce.6.cloned.1.call-done = f32[7,384,384]{2,1,0:T(8,128)} async-done(((f32[7,384,384]{2,1,0:T(8,128)}), f32[7,384,384]{2,1,0:T(8,128)}) %all-reduce.6.cloned.1.call-update) | async-done | bytes 4128784 | tf_op jit(solution)/shard_map/psum | solution.py:463
  444.2 3.0 select_reduce_fusion
  447.7 8.5 %fusion.126 = f32[7,384,384]{2,1,0:T(8,128)S(1)} fusion(f32[7,384,384]{2,1,0:T(8,128)S(1)} %copy-done.2, f32[7]{0:T(128)S(1)} %get-tuple-element.45), kind=kOutput, calls=%fused_computation.178 | convolution fusion | flops 4757372928 | bytes 8257564 | tf_op jit(solution)/shard_map/mde,mef->mdf/dot_general | solution.py:370
  456.2 17.7 %fusion.24 = f32[7,384,384]{2,1,0:T(8,128)S(1)} fusion(f32[7,384,384]{2,1,0:T(8,128)S(1)} %fusion.126, f32[384,384]{1,0:T(8,128)S(1)} %broadcast_select_fusion, f32[7,384,384]{2,1,0:T(8,128)S(1)} %copy-done.2, f32[7]{0:T(128)S(1)} %get-tuple-element.45), kind=kOutput, calls=%fused_computation.28 | convolution fusion | flops 4762533888 | bytes 12976156 | tf_op jit(solution)/shard_map/mde,mef->mdf/dot_general | solution.py:370
  473.9 9.3 %fusion.23 = f32[7,384,384]{2,1,0:T(8,128)S(1)} fusion(f32[7,384,384]{2,1,0:T(8,128)S(1)} %fusion.24, f32[7,384,384]{2,1,0:T(8,128)S(1)} %fusion.126, f32[384,384]{1,0:T(8,128)S(1)} %broadcast_select_fusion, f32[7,384,384]{2,1,0:T(8,128)S(1)} %copy-done.2, f32[7]{0:T(128)S(1)} %get-tuple-element.45), kind=kOutput, calls=%fused_computation.27 | convolution fusion | flops 4761501696 | bytes 17104924 | tf_op jit(solution)/shard_map/mde,mef->mdf/dot_general | solution.py:370
  483.2 8.5 %fusion.130 = f32[7,384,384]{2,1,0:T(8,128)S(1)} fusion(f32[7,384,384]{2,1,0:T(8,128)S(1)} %fusion.23), kind=kOutput, calls=%fused_computation.180 | convolution fusion | flops 4756340736 | bytes 8257536 | tf_op jit(solution)/shard_map/mde,mef->mdf/dot_general | solution.py:370
  491.8 9.2 %fusion.19 = f32[7,384,384]{2,1,0:T(8,128)S(1)} fusion(f32[7,384,384]{2,1,0:T(8,128)S(1)} %fusion.23, f32[7,384,384]{2,1,0:T(8,128)S(1)} %fusion.130, f32[384,384]{1,0:T(8,128)S(1)} %broadcast_select_fusion), kind=kOutput, calls=%fused_computation.22 | convolution fusion | flops 4760469504 | bytes 12976128 | tf_op jit(solution)/shard_map/mde,mef->mdf/dot_general | solution.py:370
  501.0 9.0 %fusion.18 = f32[7,384,384]{2,1,0:T(8,128)S(1)} fusion(f32[7,384,384]{2,1,0:T(8,128)S(1)} %fusion.19, f32[7,384,384]{2,1,0:T(8,128)S(1)} %fusion.130, f32[7,384,384]{2,1,0:T(8,128)S(1)} %fusion.23, f32[384,384]{1,0:T(8,128)S(1)} %broadcast_select_fusion), kind=kOutput, calls=%fused_computation.21 | convolution fusion | flops 4760469504 | bytes 17104896 | tf_op jit(solution)/shard_map/mde,mef->mdf/dot_general | solution.py:370
  510.1 9.0 %fusion.131 = f32[7,384,384]{2,1,0:T(8,128)S(1)} fusion(f32[7,384,384]{2,1,0:T(8,128)S(1)} %fusion.18), kind=kOutput, calls=%fused_computation.181 | convolution fusion | flops 4756340736 | bytes 8257536 | tf_op jit(solution)/shard_map/mde,mef->mdf/dot_general | solution.py:370
  519.1 11.4 %fusion.13 = f32[7,384,384]{2,1,0:T(8,128)} fusion(f32[7,384,384]{2,1,0:T(8,128)S(1)} %fusion.18, f32[7,384,384]{2,1,0:T(8,128)S(1)} %fusion.131, f32[384,384]{1,0:T(8,128)S(1)} %broadcast_select_fusion), kind=kOutput, calls=%fused_computation.15 | convolution fusion | flops 4760469504 | bytes 12976128 | tf_op jit(solution)/shard_map/mde,mef->mdf/dot_general | solution.py:370
  530.5 15.5 %fusion.17 = f32[7,384,384]{2,1,0:T(8,128)} fusion(f32[7,384,384]{2,1,0:T(8,128)S(1)} %fusion.130, f32[7,384,384]{2,1,0:T(8,128)S(1)} %fusion.23, f32[7,384,384]{2,1,0:T(8,128)} %copy-done.24, f32[384,384]{1,0:T(8,128)S(1)} %broadcast_select_fusion, f32[7,384,384]{2,1,0:T(8,128)} %all-reduce.6.cloned.1.call-done, f32[7]{0:T(128)S(1)} %get-tuple-element.45), kind=kOutput, calls=%fused_computation.20 | convolution fusion | flops 4765630464 | bytes 21233692 | tf_op jit(solution)/shard_map/mde,mef->mdf/dot_general | solution.py:370
  546.0 13.8 %fusion.11 = f32[7,384,384]{2,1,0:T(8,128)} fusion(f32[7,384,384]{2,1,0:T(8,128)} %fusion.17, f32[7,384,384]{2,1,0:T(8,128)S(1)} %fusion.131, f32[7,384,384]{2,1,0:T(8,128)S(1)} %fusion.18, f32[384,384]{1,0:T(8,128)S(1)} %broadcast_select_fusion), kind=kOutput, calls=%fused_computation.13 | convolution fusion | flops 4760469504 | bytes 17104896 | tf_op jit(solution)/shard_map/mde,mef->mdf/dot_general | solution.py:370
  559.8 8.9 %fusion.12 = f32[7,384,384]{2,1,0:T(8,128)S(1)} fusion(f32[7,384,384]{2,1,0:T(8,128)S(1)} %copy-done, f32[7,384,384]{2,1,0:T(8,128)S(1)} %fusion.131, f32[7,384,384]{2,1,0:T(8,128)S(1)} %fusion.18, f32[384,384]{1,0:T(8,128)S(1)} %broadcast_select_fusion), kind=kOutput, calls=%fused_computation.14 | convolution fusion | flops 4760469504 | bytes 17104896 | tf_op jit(solution)/shard_map/mde,mef->mdf/dot_general | solution.py:370
  568.7 9.0 %fusion.132 = f32[7,384,384]{2,1,0:T(8,128)S(1)} fusion(f32[7,384,384]{2,1,0:T(8,128)S(1)} %fusion.12), kind=kOutput, calls=%fused_computation.182 | convolution fusion | flops 4756340736 | bytes 8257536 | tf_op jit(solution)/shard_map/mde,mef->mdf/dot_general | solution.py:370
  577.7 9.0 %fusion.7 = f32[7,384,384]{2,1,0:T(8,128)S(1)} fusion(f32[7,384,384]{2,1,0:T(8,128)S(1)} %fusion.12, f32[7,384,384]{2,1,0:T(8,128)S(1)} %fusion.132, f32[384,384]{1,0:T(8,128)S(1)} %broadcast_select_fusion), kind=kOutput, calls=%fused_computation.8 | convolution fusion | flops 4760469504 | bytes 12976128 | tf_op jit(solution)/shard_map/mde,mef->mdf/dot_general | solution.py:370
  586.7 11.4 %fusion.5 = f32[7,384,384]{2,1,0:T(8,128)} fusion(f32[7,384,384]{2,1,0:T(8,128)S(1)} %copy-done.1, f32[7,384,384]{2,1,0:T(8,128)S(1)} %fusion.132, f32[7,384,384]{2,1,0:T(8,128)S(1)} %fusion.12, f32[384,384]{1,0:T(8,128)S(1)} %broadcast_select_fusion), kind=kOutput, calls=%fused_computation.6 | convolution fusion | flops 4760469504 | bytes 17104896 | tf_op jit(solution)/shard_map/mde,mef->mdf/dot_general | solution.py:370
  598.1 8.9 %fusion.6 = f32[7,384,384]{2,1,0:T(8,128)S(1)} fusion(f32[7,384,384]{2,1,0:T(8,128)S(1)} %fusion.7, f32[7,384,384]{2,1,0:T(8,128)S(1)} %fusion.132, f32[7,384,384]{2,1,0:T(8,128)S(1)} %fusion.12, f32[384,384]{1,0:T(8,128)S(1)} %broadcast_select_fusion), kind=kOutput, calls=%fused_computation.7 | convolution fusion | flops 4760469504 | bytes 17104896 | tf_op jit(solution)/shard_map/mde,mef->mdf/dot_general | solution.py:370
  607.0 8.8 %fusion.133 = f32[7,384,384]{2,1,0:T(8,128)S(1)} fusion(f32[7,384,384]{2,1,0:T(8,128)S(1)} %fusion.6), kind=kOutput, calls=%fused_computation.183 | convolution fusion | flops 4756340736 | bytes 8257536 | tf_op jit(solution)/shard_map/mde,mef->mdf/dot_general | solution.py:370
  615.8 9.0 %broadcast_divide_fusion = f32[7,384,384]{2,1,0:T(8,128)S(1)} fusion(f32[7]{0:T(128)S(1)} %get-tuple-element.46, f32[7,384,384]{2,1,0:T(8,128)S(1)} %copy-done.3, f32[7,384,384]{2,1,0:T(8,128)S(1)} %fusion.133, f32[7,384,384]{2,1,0:T(8,128)S(1)} %fusion.6, f32[384,384]{1,0:T(8,128)S(1)} %broadcast_select_fusion), kind=kOutput, calls=%fused_computation.33 | convolution fusion | flops 4761501696 | bytes 17104924 | tf_op jit(solution)/shard_map/mde,mef->mdf/dot_general | solution.py:370
  (113 shorter events, 38.2 us)
Async XLA Ops:
  7.2 68.9 %all-gather.2.cloned.1.call-start = ((), (), s32[]{:S(2)}) async-start(), calls=%async_computation.1 | async-start | bytes 3981312 | tf_op jit(solution)/shard_map/all_gather | solution.py:428
  12.1 231.3 %reduce-scatter.2.cloned.1.call-start = ((), (), s32[]{:S(2)}) async-start(), calls=%async_computation.2 | async-start | bytes 7962624 | tf_op jit(solution)/shard_map/reduce_scatter | solution.py:443
  114.3 131.4 %copy-start.9 = (f32[2,384,128]{2,1,0:T(8,128)S(1)}, f32[2,384,128]{2,1,0:T(8,128)}, u32[]{:S(2)}) copy-start(f32[2,384,128]{2,1,0:T(8,128)} %param.30) | copy-start | bytes 1179652
  114.3 163.3 %copy-start.11 = (f32[3,384,48]{1,2,0:T(8,128)S(1)}, f32[3,384,48]{1,2,0:T(8,128)}, u32[]{:S(2)}) copy-start(f32[3,384,48]{1,2,0:T(8,128)} %param.28) | copy-start | bytes 663556
  114.3 163.3 %copy-start.12 = (f32[128,384]{1,0:T(8,128)S(1)}, f32[128,384]{1,0:T(8,128)}, u32[]{:S(2)}) copy-start(f32[128,384]{1,0:T(8,128)} %param.31) | copy-start | bytes 589828
  114.3 163.3 %copy-start.13 = (f32[48,384]{1,0:T(8,128)S(1)}, f32[48,384]{1,0:T(8,128)}, u32[]{:S(2)}) copy-start(f32[48,384]{1,0:T(8,128)} %param.29) | copy-start | bytes 221188
  114.3 163.2 %all-reduce.4.cloned.1.call-start = ((), (), s32[]{:S(2)}) async-start(), calls=%async_computation.3 | async-start | bytes 884736 | tf_op jit(solution)/shard_map/psum | solution.py:444
  245.4 198.9 %all-reduce.6.cloned.1.call-start = ((), (), s32[]{:S(2)}) async-start(), calls=%async_computation.4 | async-start | bytes 8257536 | tf_op jit(solution)/shard_map/psum | solution.py:463
  280.3 9.1 %copy-start.5 = (f32[2,384,128]{2,1,0:T(8,128)S(1)}, f32[2,384,128]{2,1,0:T(8,128)}, u32[]{:S(2)}) copy-start(f32[2,384,128]{2,1,0:T(8,128)} %param.26) | copy-start | bytes 1179652
  284.7 5.6 copy-start.15
  284.8 5.8 copy-start.17
  284.8 50.5 %copy-start.16 = (f32[2,6]{1,0:T(2,128)S(1)}, f32[2,6]{1,0:T(2,128)}, u32[]{:S(2)}) copy-start(f32[2,6]{1,0:T(2,128)} %bias.1) | copy-start | bytes 148
  284.8 50.5 %copy-start.21 = (f32[2,6]{1,0:T(2,128)S(1)}, f32[2,6]{1,0:T(2,128)}, u32[]{:S(2)}) copy-start(f32[2,6]{1,0:T(2,128)} %param.37) | copy-start | bytes 148
  284.8 50.5 %copy-start.22 = (f32[2,6]{1,0:T(2,128)S(1)}, f32[2,6]{1,0:T(2,128)}, u32[]{:S(2)}) copy-start(f32[2,6]{1,0:T(2,128)} %param.36) | copy-start | bytes 148
  284.8 51.0 %copy-start.14 = (f32[2,384]{1,0:T(2,128)S(1)}, f32[2,384]{1,0:T(2,128)}, u32[]{:S(2)}) copy-start(f32[2,384]{1,0:T(2,128)} %gain_ref.1) | copy-start | bytes 9220
  284.8 51.0 %copy-start.18 = (f32[2,384]{1,0:T(2,128)S(1)}, f32[2,384]{1,0:T(2,128)}, u32[]{:S(2)}) copy-start(f32[2,384]{1,0:T(2,128)} %param.35) | copy-start | bytes 9220
  284.8 51.0 %copy-start.19 = (f32[2,384]{1,0:T(2,128)S(1)}, f32[2,384]{1,0:T(2,128)}, u32[]{:S(2)}) copy-start(f32[2,384]{1,0:T(2,128)} %param.34) | copy-start | bytes 9220
  287.8 50.7 %copy-start.4 = (bf16[576,384]{1,0:T(8,128)(2,1)S(1)}, bf16[576,384]{1,0:T(8,128)(2,1)}, u32[]{:S(2)}) copy-start(bf16[576,384]{1,0:T(8,128)(2,1)} %all-reduce.4.cloned.1.call-done) | copy-start | bytes 1327108
  335.2 112.0 %copy-start.20 = (f32[2,384]{1,0:T(2,128)}, f32[2,384]{1,0:T(2,128)S(1)}, u32[]{:S(2)}) copy-start(f32[2,384]{1,0:T(2,128)S(1)} %get-tuple-element.32) | copy-start | bytes 9220
  335.2 112.0 %copy-start.23 = (f32[2,6]{1,0:T(2,128)}, f32[2,6]{1,0:T(2,128)S(1)}, u32[]{:S(2)}) copy-start(f32[2,6]{1,0:T(2,128)S(1)} %get-tuple-element.33) | copy-start | bytes 148
  456.2 17.7 %copy-start.24 = (f32[7,384,384]{2,1,0:T(8,128)}, f32[7,384,384]{2,1,0:T(8,128)S(1)}, u32[]{:S(2)}) copy-start(f32[7,384,384]{2,1,0:T(8,128)S(1)} %fusion.126) | copy-start | bytes 12386308
  546.0 13.8 %copy-start = (f32[7,384,384]{2,1,0:T(8,128)S(1)}, f32[7,384,384]{2,1,0:T(8,128)}, u32[]{:S(2)}) copy-start(f32[7,384,384]{2,1,0:T(8,128)} %fusion.13) | copy-start | bytes 12386308
  577.7 9.0 %copy-start.1 = (f32[7,384,384]{2,1,0:T(8,128)S(1)}, f32[7,384,384]{2,1,0:T(8,128)}, u32[]{:S(2)}) copy-start(f32[7,384,384]{2,1,0:T(8,128)} %fusion.11) | copy-start | bytes 12386308
  607.0 8.8 %copy-start.3 = (f32[7,384,384]{2,1,0:T(8,128)S(1)}, f32[7,384,384]{2,1,0:T(8,128)}, u32[]{:S(2)}) copy-start(f32[7,384,384]{2,1,0:T(8,128)} %fusion.5) | copy-start | bytes 12386308
  (5 other events, 17.7 us)
Sparse Core Ops, SparseCore 0:
  12.2 63.8 all-gather.1
  114.5 128.8 reduce-scatter.1
  245.8 31.6 all-reduce.3
  289.5 154.7 all-reduce.5

commit v3 on v2

--- a/solution.py
+++ b/solution.py
@@ -34,6 +34,7 @@
 BLOCK = 256
 PAIR = 2 * BUCKET
 LANES = 2 * HEAD_DIM
+STATS = 24
 WHOLE = pl.BlockSpec(memory_space=pltpu.VMEM)
 SCALARS = pl.BlockSpec(memory_space=pltpu.SMEM)
 
@@ -70,8 +71,7 @@
     out_ref,
     gtok_ref,
     grad_ref,
-    ggain_ref,
-    gbias_ref,
+    stat_ref,
     n1_s,
     n2_s,
     att_s,
@@ -97,8 +97,7 @@
 
     @pl.when(step == 0)
     def _():
-        ggain_ref[...] = jnp.zeros_like(ggain_ref)
-        gbias_ref[...] = jnp.zeros_like(gbias_ref)
+        stat_ref[...] = jnp.zeros_like(stat_ref)
 
     lane = lax.broadcasted_iota(jnp.int32, (1, LANES), 1)
     low_head = lane < HEAD_DIM
@@ -210,7 +209,7 @@
     gg_s[here, :] = g_gate
     gu_s[here, :] = g_up
     e_two = mul_nn(g_gate, w_gate) + mul_nn(g_up, w_up)
-    ggain_ref[1:2, :] += jnp.sum(e_two * unit_two, axis=0, keepdims=True)
+    stat_ref[1:2, :] += jnp.sum(e_two * unit_two, axis=0, keepdims=True)
     scaled = e_two * gain_two
     g_mid = g_out + scale_two * (
         scaled - unit_two * jnp.mean(scaled * unit_two, axis=-1, keepdims=True)
@@ -239,10 +238,10 @@
         for j in range(2):
             h = 2 * hp + j
             mine = g_scores[j * PAIR : (j + 1) * PAIR]
-            gbias_ref[h : h + 1, :] += jnp.sum(
+            stat_ref[8 + h : 9 + h, :PAIR] += jnp.sum(
                 jnp.where(same_var, mine, 0.0), axis=0, keepdims=True
             )
-            gbias_ref[8 + h : 9 + h, :] += jnp.sum(
+            stat_ref[16 + h : 17 + h, :PAIR] += jnp.sum(
                 jnp.where(same_var, 0.0, mine), axis=0, keepdims=True
             )
         low_scores = g_scores.astype(LOW)
@@ -262,7 +261,7 @@
     g_qkv = jnp.concatenate(g_q + g_k + g_v, axis=1)
     gqkv_s[here, :] = g_qkv
     e_one = mul_nn(g_qkv, weight(0, 3))
-    ggain_ref[0:1, :] += jnp.sum(e_one * unit_one, axis=0, keepdims=True)
+    stat_ref[0:1, :] += jnp.sum(e_one * unit_one, axis=0, keepdims=True)
     scaled = e_one * gain_one
     gtok_ref[...] = (
         g_mid
@@ -312,11 +311,10 @@
             jax.ShapeDtypeStruct((rows, width), LOW),
             jax.ShapeDtypeStruct((rows, width), LOW),
             jax.ShapeDtypeStruct((copies, shard_rows, width), grad_type),
-            jax.ShapeDtypeStruct((2, width), WIDE),
-            jax.ShapeDtypeStruct((16, PAIR), WIDE),
+            jax.ShapeDtypeStruct((STATS, width), WIDE),
         ),
         in_specs=[SCALARS, SCALARS, block, block, WHOLE, WHOLE, WHOLE, WHOLE, WHOLE],
-        out_specs=(block, block, WHOLE, WHOLE, WHOLE),
+        out_specs=(block, block, WHOLE, WHOLE),
         scratch_shapes=[
             low_scratch(width),
             low_scratch(width),
@@ -393,6 +391,864 @@
     corrected = new_moment / (1.0 - BETA_ONE**STEP)
     scaled = jnp.sqrt(new_square / (1.0 - BETA_TWO**STEP)) + ADAM_EPS
     return (new_moment, new_square, param - ADAM_RATE * corrected / scaled)
+
+
+DEPTH, ACROSS = 4, 2
+SIDES, CORES = 2, 2
+TURNS = (2, 1, 3, 0)
+OWNERS = (
+    (2, 0, 0, 0),
+    (2, 1, 0, 1),
+    (1, 1, 0, 0),
+    (2, 1, 1, 0),
+    (2, 0, 1, 1),
+    (1, 0, 0, 1),
+    (1, 1, 1, 0),
+)
+
+
+def place():
+    f = lax.axis_index("fsdp")
+    n = lax.axis_index("ns")
+    return f // ACROSS, f % ACROSS, n // CORES, n % CORES
+
+
+def device(z, x, y, c):
+    return (z * ACROSS + x, y * CORES + c)
+
+
+def remote(src, dst, send_sem, recv_sem, where):
+    return pltpu.make_async_remote_copy(
+        src_ref=src,
+        dst_ref=dst,
+        send_sem=send_sem,
+        recv_sem=recv_sem,
+        device_id=where,
+        device_id_type=pl.DeviceIdType.MESH,
+    )
+
+
+def greet(where):
+    pl.semaphore_signal(
+        pltpu.get_barrier_semaphore(),
+        inc=1,
+        device_id=where,
+        device_id_type=pl.DeviceIdType.MESH,
+    )
+
+
+def gather_kernel(
+    pieces,
+    qkv_ref,
+    out_ref,
+    gate_up_ref,
+    down_ref,
+    full,
+    up_send,
+    down_send,
+    x_send,
+    sib_send,
+    below_recv,
+    above_recv,
+    x_recv,
+    sib_recv,
+):
+    z, x, y, c = place()
+    me = z * ACROSS + x
+    rows = full.shape[1]
+    half = rows // 2
+    mine = pl.ds(pl.multiple_of(c * half, 16), half)
+    sibling = device(z, x, y, 1 - c)
+    beside = device(z, 1 - x, y, c)
+    upper = device(z + 1, x, y, c)
+    lower = device(z - 1, x, y, c)
+    greet(sibling)
+    greet(beside)
+
+    @pl.when(z < DEPTH - 1)
+    def _():
+        greet(upper)
+
+    @pl.when(z > 0)
+    def _():
+        greet(lower)
+
+    def put(index, value):
+        start, count = pieces[index]
+        full[me, start : start + count, :] = value.astype(LOW)
+
+    for j in range(3):
+        put(j, qkv_ref[j].T)
+    put(3, out_ref[...])
+    put(4, gate_up_ref[0].T)
+    put(5, gate_up_ref[1].T)
+    put(6, down_ref[...])
+    near = 2 + (z < DEPTH - 1).astype(jnp.int32) + (z > 0).astype(jnp.int32)
+    pl.semaphore_wait(pltpu.get_barrier_semaphore(), near)
+
+    def part(shard):
+        return full.at[shard, mine]
+
+    def shard_at(rel):
+        return me + rel * ACROSS
+
+    def up_copy(d):
+        return remote(
+            part(shard_at(-d)), part(shard_at(-d)), up_send.at[d], below_recv.at[d], upper
+        )
+
+    def down_copy(d):
+        return remote(
+            part(shard_at(d)), part(shard_at(d)), down_send.at[d], above_recv.at[d], lower
+        )
+
+    def x_copy(rel):
+        return remote(
+            part(shard_at(rel)), part(shard_at(rel)), x_send.at[rel + 3], x_recv.at[rel + 3], beside
+        )
+
+    def other_at(rel):
+        return (z + rel) * ACROSS + 1 - x
+
+    def sib_copy(rel):
+        shard = shard_at(rel)
+        return remote(
+            part(shard), part(shard), sib_send.at[0, rel + 3], sib_recv.at[0, rel + 3], sibling
+        )
+
+    def sib_other(rel):
+        shard = other_at(rel)
+        return remote(
+            part(shard), part(shard), sib_send.at[1, rel + 3], sib_recv.at[1, rel + 3], sibling
+        )
+
+    has_up = z < DEPTH - 1
+    has_down = z > 0
+
+    def exists(rel):
+        return (z + rel >= 0) & (z + rel < DEPTH)
+
+    @pl.when(has_up)
+    def _():
+        up_copy(0).start()
+
+    @pl.when(has_down)
+    def _():
+        down_copy(0).start()
+
+    x_copy(0).start()
+    for d in range(1, DEPTH):
+
+        @pl.when(exists(-d))
+        def _():
+            remote(
+                part(shard_at(-d)), part(shard_at(-d)), up_send.at[d], below_recv.at[d - 1], lower
+            ).wait_recv()
+
+            if d < DEPTH - 1:
+
+                @pl.when(has_up)
+                def _():
+                    up_copy(d).start()
+
+            x_copy(-d).start()
+            sib_copy(-d).start()
+
+        @pl.when(exists(d))
+        def _():
+            remote(
+                part(shard_at(d)), part(shard_at(d)), down_send.at[d], above_recv.at[d - 1], upper
+            ).wait_recv()
+
+            if d < DEPTH - 1:
+
+                @pl.when(has_down)
+                def _():
+                    down_copy(d).start()
+
+            x_copy(d).start()
+            sib_copy(d).start()
+
+    def from_beside(rel):
+        remote(
+            part(other_at(rel)), part(other_at(rel)), x_send.at[rel + 3], x_recv.at[rel + 3], beside
+        ).wait_recv()
+        sib_other(rel).start()
+
+    from_beside(0)
+    for d in range(1, DEPTH):
+        for rel in (-d, d):
+
+            @pl.when(exists(rel))
+            def _():
+                from_beside(rel)
+
+    theirs = pl.ds(pl.multiple_of((1 - c) * half, 16), half)
+
+    def sib_done(kind, rel, shard):
+        remote(
+            full.at[shard, theirs],
+            full.at[shard, theirs],
+            sib_send.at[kind, rel + 3],
+            sib_recv.at[kind, rel + 3],
+            sibling,
+        ).wait_recv()
+
+    for rel in range(1 - DEPTH, DEPTH):
+
+        @pl.when(exists(rel))
+        def _():
+            if rel != 0:
+                sib_done(0, rel, shard_at(rel))
+                sib_copy(rel).wait_send()
+            sib_done(1, rel, other_at(rel))
+            sib_other(rel).wait_send()
+            x_copy(rel).wait_send()
+
+    for d in range(DEPTH - 1):
+
+        @pl.when(exists(-d) & has_up)
+        def _():
+            up_copy(d).wait_send()
+
+        @pl.when(exists(d) & has_down)
+        def _():
+            down_copy(d).wait_send()
+
+
+def gather(qkv, out, gate_up, down):
+    attn_rows, width = out.shape
+    pieces = offsets(attn_rows, down.shape[0])
+    dma = pltpu.SemaphoreType.DMA
+    return pl.pallas_call(
+        functools.partial(gather_kernel, pieces),
+        out_shape=jax.ShapeDtypeStruct(
+            (DEPTH * ACROSS, pieces[-1][0] + pieces[-1][1], width), LOW
+        ),
+        in_specs=[WHOLE] * 4,
+        out_specs=WHOLE,
+        scratch_shapes=[
+            dma((DEPTH,)),
+            dma((DEPTH,)),
+            dma((2 * DEPTH - 1,)),
+            dma((2, 2 * DEPTH - 1)),
+            dma((DEPTH,)),
+            dma((DEPTH,)),
+            dma((2 * DEPTH - 1,)),
+            dma((2, 2 * DEPTH - 1)),
+        ],
+        compiler_params=pltpu.CompilerParams(
+            vmem_limit_bytes=32 << 20, collective_id=0, has_side_effects=True
+        ),
+        name="gather",
+    )(qkv, out, gate_up, down)
+
+
+def halves(value):
+    high = value.astype(LOW)
+    return high, (value - high.astype(WIDE)).astype(LOW)
+
+
+def mul_wide(left, right):
+    columns = right.shape[1]
+    left_high, left_low = halves(left)
+    right_high, right_low = halves(right)
+    first = mul_nn(left_high, jnp.concatenate([right_high, right_low], axis=1))
+    return first[:, :columns] + (first[:, columns:] + mul_nn(left_low, right_high))
+
+
+def gram_wide(value):
+    high, low = halves(value)
+    cross = mul_tn(high, low)
+    return mul_tn(high, high) + (cross + cross.T)
+
+
+def reduce_kernel(
+    pieces,
+    grad_ref,
+    stat_ref,
+    mqkv_ref,
+    mout_ref,
+    mgate_up_ref,
+    mdown_ref,
+    grows_ref,
+    xrows_ref,
+    total_ref,
+    in_zero,
+    acc_zero,
+    in_one,
+    acc_one,
+    in_two,
+    acc_two,
+    in_three,
+    momenta,
+    advance,
+    y_attn,
+    y_ff,
+    x_attn,
+    x_ff,
+    gram_s,
+    chain_s,
+    stat_in,
+    stat_acc,
+    stat_line,
+    send_zero,
+    send_one,
+    send_two,
+    send_three,
+    recv_zero,
+    recv_one,
+    recv_two,
+    recv_three,
+    stat_send,
+    stat_recv,
+    adv_send,
+    adv_recv,
+    row_send,
+    row_recv,
+    x_send,
+    x_recv,
+    fan_send,
+    fan_recv,
+):
+    z, x, y, c = place()
+    shard = z * ACROSS + x
+    rows = grad_ref.shape[2]
+    width = grad_ref.shape[3]
+    half, quarter = rows // 2, rows // 4
+    sibling = device(z, x, y, 1 - c)
+    facing = device(z, x, 1 - y, c)
+    corner = device(z, x, 1 - y, 1 - c)
+    beside = device(z, 1 - x, y, c)
+    world = DEPTH * ACROSS * SIDES * CORES
+    rank = shard * (SIDES * CORES) + y * CORES + c
+
+    def hello(i, carry):
+        other = lax.rem(rank + 1 + i, world)
+        greet((other // (SIDES * CORES), lax.rem(other, SIDES * CORES)))
+        return carry
+
+    lax.fori_loop(0, world - 1, hello, 0)
+    pl.semaphore_wait(pltpu.get_barrier_semaphore(), world - 1)
+
+    keep_half = pl.ds(pl.multiple_of(c * half, 16), half)
+    give_half = pl.ds(pl.multiple_of((1 - c) * half, 16), half)
+    keep_quarter = pl.ds(pl.multiple_of(y * quarter, 16), quarter)
+    give_quarter = pl.ds(pl.multiple_of((1 - y) * quarter, 16), quarter)
+    line = [lax.rem(z + k, DEPTH) for k in range(DEPTH)]
+
+    def zero(k):
+        return remote(
+            grad_ref.at[line[k], :, give_half],
+            in_zero.at[k],
+            send_zero.at[k],
+            recv_zero.at[k],
+            sibling,
+        )
+
+    def one_y(k):
+        return remote(
+            acc_zero.at[k, :, give_quarter],
+            in_one.at[k, :, pl.ds(0, quarter)],
+            send_one.at[k],
+            recv_one.at[k],
+            facing,
+        )
+
+    def two_x(k):
+        return remote(
+            acc_one.at[k, 1 - x, pl.ds(0, quarter)],
+            in_two.at[k],
+            send_two.at[k],
+            recv_two.at[k],
+            beside,
+        )
+
+    def one_x(k):
+        return remote(
+            acc_zero.at[k, 1 - x], in_one.at[k, 0], send_one.at[k], recv_one.at[k], beside
+        )
+
+    def two_y(k):
+        return remote(
+            acc_one.at[k, 0, give_quarter],
+            in_two.at[k],
+            send_two.at[k],
+            recv_two.at[k],
+            facing,
+        )
+
+    def three(k):
+        return remote(
+            acc_two.at[k],
+            in_three.at[k],
+            send_three.at[k],
+            recv_three.at[k],
+            device(line[k], x, y, c),
+        )
+
+    for k in TURNS:
+        zero(k).start()
+
+    def stat_copy(step, src, where):
+        return remote(src, stat_in.at[step], stat_send.at[step], stat_recv.at[step], where)
+
+    stat_copy(0, stat_ref, sibling).start()
+
+    def put(index, value):
+        start, count = pieces[index]
+        momenta[start : start + count, :] = value
+
+    for j in range(3):
+        put(j, mqkv_ref[j].T)
+    put(3, mout_ref[...])
+    put(4, mgate_up_ref[0].T)
+    put(5, mgate_up_ref[1].T)
+    put(6, mdown_ref[...])
+
+    stat_copy(0, stat_ref, sibling).wait()
+    stat_acc[0] = stat_ref[...] + stat_in[0]
+    stat_copy(1, stat_acc.at[0], facing).start()
+
+    def add(left, right):
+        return left.astype(WIDE) + right.astype(WIDE)
+
+    for t in range(DEPTH + 2):
+        if t < DEPTH:
+            k = TURNS[t]
+            zero(k).wait_recv()
+            acc_zero[k] = add(grad_ref[line[k], :, keep_half], in_zero[k]).astype(LOW)
+
+            @pl.when(c == 0)
+            def _():
+                one_y(k).start()
+
+            @pl.when(c == 1)
+            def _():
+                one_x(k).start()
+
+        if 1 <= t <= DEPTH:
+            k = TURNS[t - 1]
+
+            @pl.when(c == 0)
+            def _():
+                one_y(k).wait_recv()
+                acc_one[k, :, :quarter] = add(
+                    acc_zero[k, :, keep_quarter], in_one[k, :, :quarter]
+                ).astype(LOW)
+                two_x(k).start()
+
+            @pl.when(c == 1)
+            def _():
+                one_x(k).wait_recv()
+                acc_one[k, 0] = add(acc_zero[k, x], in_one[k, 0]).astype(LOW)
+                two_y(k).start()
+
+        if t == 1:
+            stat_copy(1, stat_acc.at[0], facing).wait()
+            stat_acc[1] = stat_acc[0] + stat_in[1]
+            stat_copy(2, stat_acc.at[1], beside).start()
+        if t == 3:
+            stat_copy(2, stat_acc.at[1], beside).wait()
+            stat_acc[2] = stat_acc[1] + stat_in[2]
+            stat_line[z] = stat_acc[2]
+            for j in range(1, DEPTH):
+                remote(
+                    stat_acc.at[2],
+                    stat_line.at[z],
+                    stat_send.at[2 + j],
+                    stat_recv.at[2 + j],
+                    device(line[j], x, y, c),
+                ).start()
+
+        if t >= 2:
+            k = TURNS[t - 2]
+
+            @pl.when(c == 0)
+            def _():
+                two_x(k).wait_recv()
+                acc_two[k] = add(acc_one[k, x, :quarter], in_two[k]).astype(LOW)
+
+            @pl.when(c == 1)
+            def _():
+                two_y(k).wait_recv()
+                acc_two[k] = add(acc_one[k, 0, keep_quarter], in_two[k]).astype(LOW)
+
+            if k != 0:
+                three(k).start()
+
+    total = acc_two[0].astype(WIDE)
+    for k in range(1, DEPTH):
+        three(k).wait_recv()
+        total = total + in_three[k].astype(WIDE)
+    part = 2 * c + y
+    here = pl.ds(pl.multiple_of(part * quarter, 16), quarter)
+    old = momenta[here, :]
+    advance[...] = total + MUON_MU * (MUON_MU * old + total)
+
+    def segments(index):
+        found = []
+        for m, (start, count) in enumerate(pieces):
+            first = max(start, index * quarter)
+            last = min(start + count, (index + 1) * quarter)
+            if first < last:
+                found.append((m, first - index * quarter, first - start, last - first))
+        return found
+
+    def owned(m):
+        oz, ox, oy, oc = OWNERS[m]
+        return (z == oz) & (x == ox) & (y == oy) & (c == oc)
+
+    def stage(m):
+        return y_attn if m < 4 else y_ff
+
+    def adv_copy(index, i):
+        m, first, to, count = segments(index)[i]
+        return remote(
+            advance.at[pl.ds(first, count)],
+            stage(m).at[shard, pl.ds(to, count)],
+            adv_send.at[i],
+            adv_recv.at[0],
+            device(*OWNERS[m]),
+        )
+
+    for index in range(4):
+        for i, (m, first, to, count) in enumerate(segments(index)):
+
+            @pl.when((part == index) & jnp.logical_not(owned(m)))
+            def _():
+                adv_copy(index, i).start()
+
+            @pl.when((part == index) & owned(m))
+            def _():
+                pltpu.make_async_copy(
+                    advance.at[pl.ds(first, count)],
+                    stage(m).at[shard, pl.ds(to, count)],
+                    adv_recv.at[0],
+                ).start()
+
+    grows_ref[here, :] = total.astype(LOW)
+
+    def row_copy(j, where):
+        return remote(
+            grows_ref.at[here], grows_ref.at[here], row_send.at[j], row_recv.at[j], where
+        )
+
+    mates = (sibling, facing, corner)
+    for j, where in enumerate(mates):
+        row_copy(j, where).start()
+
+    attn_owner = functools.reduce(jnp.logical_or, [owned(m) for m in range(4)])
+    ff_owner = functools.reduce(jnp.logical_or, [owned(m) for m in range(4, 7)])
+
+    def arrived(buffer):
+        pltpu.make_async_copy(buffer, buffer, adv_recv.at[0]).wait()
+
+    @pl.when(attn_owner)
+    def _():
+        arrived(y_attn)
+        value = y_attn[...].reshape(-1, width)
+        gram_s[...] = gram_wide(value)
+
+    @pl.when(ff_owner)
+    def _():
+        arrived(y_ff)
+        value = y_ff[...].reshape(-1, width)
+        gram_s[...] = gram_wide(value)
+
+    @pl.when(attn_owner | ff_owner)
+    def _():
+        row_id = lax.broadcasted_iota(jnp.int32, (width, width), 0)
+        col_id = lax.broadcasted_iota(jnp.int32, (width, width), 1)
+        unit = row_id == col_id
+        gram_mat = gram_s[...]
+        trace = jnp.sum(jnp.where(unit, gram_mat, 0.0), keepdims=True)
+        norm = jnp.sqrt(trace) + NS_EPS
+        inverse = 1.0 / norm
+        diagonal = jnp.where(unit, COEF_A, 0.0)
+        gram_mat = gram_mat * (inverse * inverse)
+
+        def poly(value):
+            return diagonal + COEF_B * value + COEF_C * mul_wide(value, value)
+
+        step_mat = poly(gram_mat)
+        gram_s[...] = mul_wide(mul_wide(gram_mat, step_mat), step_mat)
+        chain_s[...] = step_mat * inverse
+
+        def turn(i, carry):
+            now = gram_s[...]
+            step_now = poly(now)
+            both = mul_wide(jnp.concatenate([now, chain_s[...]], axis=0), step_now)
+            chain_s[...] = both[width:]
+            gram_s[...] = mul_wide(both[:width], step_now)
+            return carry
+
+        lax.fori_loop(0, NS_ITERS - 2, turn, 0)
+        chain_s[...] = mul_wide(chain_s[...], poly(gram_s[...]))
+
+    @pl.when(attn_owner)
+    def _():
+        value = y_attn[...].reshape(-1, width)
+        x_attn[...] = mul_wide(value, chain_s[...]).astype(LOW).reshape(x_attn.shape)
+
+    @pl.when(ff_owner)
+    def _():
+        value = y_ff[...].reshape(-1, width)
+        x_ff[...] = mul_wide(value, chain_s[...]).astype(LOW).reshape(x_ff.shape)
+
+    chips = DEPTH * ACROSS * SIDES
+
+    def x_copy(m, i):
+        start, count = pieces[m]
+        source = x_attn if m < 4 else x_ff
+        to = i // SIDES
+        return remote(
+            source.at[to],
+            xrows_ref.at[pl.ds(start, count)],
+            x_send.at[i],
+            x_recv.at[m],
+            (to, lax.rem(i, SIDES) * CORES + OWNERS[m][3]),
+        )
+
+    for m in range(7):
+        start, count = pieces[m]
+        source = x_attn if m < 4 else x_ff
+
+        @pl.when(owned(m))
+        def _():
+            mine = shard * SIDES + y
+
+            def send(i, carry):
+                x_copy(m, lax.rem(mine + i, chips)).start()
+                return carry
+
+            lax.fori_loop(1, chips, send, 0)
+            pltpu.make_async_copy(
+                source.at[shard], xrows_ref.at[pl.ds(start, count)], x_recv.at[m]
+            ).start()
+
+    for j in range(1, DEPTH):
+        remote(
+            stat_acc.at[2],
+            stat_line.at[lax.rem(z + DEPTH - j, DEPTH)],
+            stat_send.at[2 + j],
+            stat_recv.at[2 + j],
+            device(line[j], x, y, c),
+        ).wait()
+    total_ref[...] = (stat_line[0] + stat_line[1]) + (stat_line[2] + stat_line[3])
+    for j, (dy, dc) in enumerate(((0, 1), (1, 0), (1, 1))):
+        source = 2 * (c ^ dc) + (y ^ dy)
+        there = pl.ds(pl.multiple_of(source * quarter, 16), quarter)
+        remote(
+            grows_ref.at[here], grows_ref.at[there], row_send.at[j], row_recv.at[j], mates[j]
+        ).wait_recv()
+
+    def fan_copy(m):
+        start, count = pieces[m]
+        rows_m = xrows_ref.at[pl.ds(start, count)]
+        return remote(rows_m, rows_m, fan_send.at[m], fan_recv.at[m], sibling)
+
+    for m in range(7):
+        start, count = pieces[m]
+
+        @pl.when(c == OWNERS[m][3])
+        def _():
+            rows_m = xrows_ref.at[pl.ds(start, count)]
+            pltpu.make_async_copy(rows_m, rows_m, x_recv.at[m]).wait()
+            fan_copy(m).start()
+
+    for m in range(7):
+
+        @pl.when(c != OWNERS[m][3])
+        def _():
+            fan_copy(m).wait_recv()
+
+    for m in range(7):
+
+        @pl.when(c == OWNERS[m][3])
+        def _():
+            fan_copy(m).wait_send()
+
+        @pl.when(owned(m))
+        def _():
+            mine = shard * SIDES + y
+
+            def sent(i, carry):
+                x_copy(m, lax.rem(mine + i, chips)).wait_send()
+                return carry
+
+            lax.fori_loop(1, chips, sent, 0)
+
+    for j, where in enumerate(mates):
+        row_copy(j, where).wait_send()
+    for index in range(4):
+        for i, (m, first, to, count) in enumerate(segments(index)):
+
+            @pl.when((part == index) & jnp.logical_not(owned(m)))
+            def _():
+                adv_copy(index, i).wait_send()
+
+    for k in TURNS:
+        zero(k).wait_send()
+        if k != 0:
+            three(k).wait_send()
+
+        @pl.when(c == 0)
+        def _():
+            one_y(k).wait_send()
+            two_x(k).wait_send()
+
+        @pl.when(c == 1)
+        def _():
+            one_x(k).wait_send()
+            two_y(k).wait_send()
+
+
+def reduce_and_turn(grads, stats, qkv, out, gate_up, down):
+    attn_rows, width = out.shape
+    ff_rows = down.shape[0]
+    pieces = offsets(attn_rows, ff_rows)
+    rows = grads.shape[1]
+    half, quarter = rows // 2, rows // 4
+    shards = DEPTH * ACROSS
+    low = lambda *shape: pltpu.VMEM((*shape, width), LOW)
+    wide = lambda *shape: pltpu.VMEM((*shape, width), WIDE)
+    dma = lambda *shape: pltpu.SemaphoreType.DMA(shape)
+    return pl.pallas_call(
+        functools.partial(reduce_kernel, pieces),
+        out_shape=(
+            jax.ShapeDtypeStruct((rows, width), LOW),
+            jax.ShapeDtypeStruct((rows, width), LOW),
+            jax.ShapeDtypeStruct(stats.shape, WIDE),
+        ),
+        in_specs=[WHOLE] * 6,
+        out_specs=(WHOLE,) * 3,
+        scratch_shapes=[
+            low(DEPTH, ACROSS, half),
+            low(DEPTH, ACROSS, half),
+            low(DEPTH, ACROSS, half),
+            low(DEPTH, ACROSS, half),
+            low(DEPTH, quarter),
+            low(DEPTH, quarter),
+            low(DEPTH, quarter),
+            wide(rows),
+            wide(quarter),
+            wide(shards, attn_rows),
+            wide(shards, ff_rows),
+            low(shards, attn_rows),
+            low(shards, ff_rows),
+            wide(width),
+            wide(width),
+            wide(3, STATS),
+            wide(3, STATS),
+            wide(DEPTH, STATS),
+            *[dma(DEPTH) for _ in range(8)],
+            dma(6),
+            dma(6),
+            dma(3),
+            dma(1),
+            dma(3),
+            dma(3),
+            dma(shards * SIDES),
+            dma(7),
+            dma(7),
+            dma(7),
+        ],
+        compiler_params=pltpu.CompilerParams(
+            vmem_limit_bytes=56 << 20, collective_id=1, has_side_effects=True
+        ),
+        name="reduce",
+    )(grads.reshape(DEPTH, ACROSS, rows, width), stats, qkv, out, gate_up, down)
+
+
+def update_kernel(
+    pieces,
+    factors,
+    grow_ref,
+    xrow_ref,
+    stat_ref,
+    w_qkv,
+    w_out,
+    w_gate_up,
+    w_down,
+    m_qkv,
+    m_out,
+    m_gate_up,
+    m_down,
+    gains,
+    bias,
+    gain_moment,
+    gain_square,
+    bias_moment,
+    bias_square,
+    g_qkv,
+    g_out,
+    g_gate_up,
+    g_down,
+    nm_qkv,
+    nm_out,
+    nm_gate_up,
+    nm_down,
+    nw_qkv,
+    nw_out,
+    nw_gate_up,
+    nw_down,
+    g_gains,
+    n_gain_moment,
+    n_gain_square,
+    n_gains,
+    g_bias,
+    n_bias_moment,
+    n_bias_square,
+    n_bias,
+):
+    shrink = 1.0 - MUON_RATE * MUON_DECAY
+
+    def one(index, turned, g, m, w, nm, nw):
+        start, count = pieces[index]
+        grad = grow_ref[start : start + count, :].astype(WIDE)
+        ortho = xrow_ref[start : start + count, :].astype(WIDE)
+        if turned:
+            grad, ortho = grad.T, ortho.T
+        g[...] = grad
+        nm[...] = MUON_MU * m[...] + grad
+        nw[...] = w[...] * shrink - factors[index] * ortho
+
+    for j in range(3):
+        one(j, True, *[r.at[j] for r in (g_qkv, m_qkv, w_qkv, nm_qkv, nw_qkv)])
+    one(3, False, g_out, m_out, w_out, nm_out, nw_out)
+    for j in range(2):
+        refs = (g_gate_up, m_gate_up, w_gate_up, nm_gate_up, nw_gate_up)
+        one(4 + j, True, *[r.at[j] for r in refs])
+    one(6, False, g_down, m_down, w_down, nm_down, nw_down)
+
+    grad = stat_ref[0:2, :]
+    g_gains[...] = grad
+    n_gain_moment[...], n_gain_square[...], n_gains[...] = adam_step(
+        gains[...], grad, gain_moment[...], gain_square[...]
+    )
+    heads = bias.shape[1]
+    sums = jnp.sum(stat_ref[8:24, :PAIR].T, axis=0, keepdims=True)
+    grad = jnp.concatenate([sums[:, :heads], sums[:, 8 : 8 + heads]], axis=0)
+    g_bias[...] = grad
+    n_bias_moment[...], n_bias_square[...], n_bias[...] = adam_step(
+        bias[...], grad, bias_moment[...], bias_square[...]
+    )
+
+
+def update(factors, grad_rows, ortho_rows, stats, weights, momenta, small):
+    pieces = offsets(weights[1].shape[0], weights[3].shape[0])
+    gains, bias = small[:2]
+    like = lambda a: jax.ShapeDtypeStruct(a.shape, WIDE)
+    outs = [like(a) for a in (*weights, *weights, *weights, *[gains] * 4, *[bias] * 4)]
+    return pl.pallas_call(
+        functools.partial(update_kernel, pieces, factors),
+        out_shape=tuple(outs),
+        in_specs=[WHOLE] * 17,
+        out_specs=(WHOLE,) * len(outs),
+        compiler_params=pltpu.CompilerParams(vmem_limit_bytes=40 << 20),
+        name="update",
+    )(grad_rows, ortho_rows, stats, *weights, *momenta, *small)
 
 
 def body(
@@ -423,6 +1279,27 @@
     fsdp = lax.axis_size("fsdp")
     ff = ff_rows * fsdp
     attn_width = attn_rows * fsdp
+    shrink = 1.0 - MUON_RATE * MUON_DECAY
+    scale_attn = MUON_RATE * 0.2 * math.sqrt(max(width, attn_width))
+    scale_ff = MUON_RATE * 0.2 * math.sqrt(max(width, ff))
+    sizes = (fsdp, lax.axis_size("ns"))
+    if sizes == (DEPTH * ACROSS, SIDES * CORES) and attn_rows == 48 and ff_rows == 128:
+        full = gather(weight_qkv, weight_out, weight_gate_up, weight_down)
+        out_tokens, grad_tokens, grads, stats = layer(
+            tokens, cotangent, lengths, variates, times, full, gains, attn_bias, ff, LOW
+        )
+        momenta = (momentum_qkv, momentum_out, momentum_gate_up, momentum_down)
+        grad_rows, ortho_rows, stats = reduce_and_turn(grads, stats, *momenta)
+        outs = update(
+            (scale_attn,) * 4 + (scale_ff,) * 3,
+            grad_rows,
+            ortho_rows,
+            stats,
+            (weight_qkv, weight_out, weight_gate_up, weight_down),
+            momenta,
+            (gains, attn_bias, gain_moment, gain_square, bias_moment, bias_square),
+        )
+        return (out_tokens, grad_tokens, *outs)
     weights = pack(weight_qkv, weight_out, weight_gate_up, weight_down)
     momenta = pack(momentum_qkv, momentum_out, momentum_gate_up, momentum_down)
     full = lax.all_gather(weights.astype(LOW), "fsdp", axis=0, tiled=False)
@@ -432,7 +1309,7 @@
         full = jnp.concatenate(
             [full[:, s : s + n].reshape(1, fsdp * n, width) for s, n in pieces], axis=1
         )
-    out_tokens, grad_tokens, grads, gain_rows, bias_rows = layer(
+    out_tokens, grad_tokens, grads, stats = layer(
         tokens, cotangent, lengths, variates, times, full, gains, attn_bias, ff, WIDE
     )
     if not aligned:
@@ -442,8 +1319,8 @@
         )
     summed = lax.psum_scatter(grads, "fsdp", scatter_dimension=0, tiled=False)
     grad_rows = lax.psum(summed.astype(LOW), "ns").astype(WIDE)
-    bias_part = jnp.sum(bias_rows, axis=1).reshape(2, 8)[:, :heads]
-    grad_gains, grad_bias = lax.psum((gain_rows, bias_part), ("fsdp", "ns"))
+    bias_part = jnp.sum(stats[8:, :PAIR], axis=1).reshape(2, 8)[:, :heads]
+    grad_gains, grad_bias = lax.psum((stats[:2], bias_part), ("fsdp", "ns"))
 
     new_momenta = MUON_MU * momenta + grad_rows
     advance = grad_rows + MUON_MU * new_momenta
@@ -461,9 +1338,6 @@
         ]
     )
     factor = newton_schulz(lax.psum(grams, "fsdp"))
-    shrink = 1.0 - MUON_RATE * MUON_DECAY
-    scale_attn = MUON_RATE * 0.2 * math.sqrt(max(width, attn_width))
-    scale_ff = MUON_RATE * 0.2 * math.sqrt(max(width, ff))
     turned = jnp.concatenate(
         [
             (scale_attn if i < 4 else scale_ff)

time: 650 us -> 151 us (0.23); the launches traced: 638 us -> 150 us
  waiting for transfers between devices: 323 us -> 0 us
  matrix products: 191 us -> 0 us
  Pallas kernels: 38.2 us -> 132 us
  blocking collectives: 44.6 us -> 0 us
  between operations: 14.7 us -> 0.9 us
  other arithmetic: 15.1 us -> 1.42 us
    dot_general x31 -> x0, matrix products: 191 us -> none  [the longest x17 177 us: product(): jnp.einsum('mde,mef->mdf', left, right, precision=lax.Precision.HIGHEST,...]
    psum x2 -> x0, waiting for transfers between devices: 134 us -> none  [the longest x1 102 us: body(): factor = newton_schulz(lax.psum(grams, 'fsdp'))]
    reduce_scatter x1 -> x0, waiting for transfers between devices: 129 us -> none  [body(): summed = lax.psum_scatter(grads, 'fsdp', scatter_dimension=0, tiled=False)]
    pallas_call x0 -> x3, Pallas kernels: none -> 94.5 us  [the longest x1 68.8 us: reduce_and_turn(): pl.pallas_call(functools.partial(reduce_kernel, pieces), out_shape=(jax.S...]
    all_gather x1 -> x0, waiting for transfers between devices: 60.3 us -> none  [body(): full = lax.all_gather(weights.astype(LOW), 'fsdp', axis=0, tiled=False)]
    psum x1 -> x0, blocking collectives: 44.6 us -> none  [body(): grad_gains, grad_bias = lax.psum((gain_rows, bias_part), ('fsdp', 'ns'))]
    unnamed x50 -> x51, local copies, waits for them, and re-layouts: 0.56 us -> 15.5 us
  transfers between devices with their start and end apart: 4 -> 0, of which waited for: 4 -> 0; matrix products, arithmetic and copies ran while one was open for 2% -> 0% of each run, Pallas kernels for 0% -> 0%
where the time goes in v3:
time: 151 us; the launch traced here: 150 us
  Pallas kernels  132 us (87%)
  local copies, waits for them, and re-layouts  16.3 us (11%)
    pallas_call x1, Pallas kernels, reduce_and_turn(): pl.pallas_call(functools.partial(reduce_kernel, pieces), out_shape=(jax.S...  68.8 us
    pallas_call x1, Pallas kernels, layer(): pl.pallas_call(functools.partial(layer_kernel, pieces), grid=(grid,), out...  37.1 us
    pallas_call x1, Pallas kernels, gather(): pl.pallas_call(functools.partial(gather_kernel, pieces), out_shape=jax.Sh...  23.9 us
    unnamed x51, local copies, waits for them, and re-layouts  15.5 us

profile of v3, /device:TPU:15, one launch (start us, length us, event | category | flops | bytes accessed | tf_op | source)
XLA Modules:
  0.0 150.2 jit_solution(11153838266177009665)
XLA Ops:
  0.7 0.1 fusion.2
  1.0 0.7 pad_maximum_fusion.table_ref
  1.6 1.2 copy.41.qkv_ref.w_qkv
  2.8 1.0 copy-done.2
  3.8 0.9 copy-done.5
  4.7 0.9 copy-done.10
  5.6 23.9 %gather.1.w_ref = bf16[8,576,384]{2,1,0:T(8,128)(2,1)S(1)} custom-call(f32[3,384,48]{2,1,0:T(8,128)S(1)} %copy.41.qkv_ref.w_qkv, f32[48,384]{1,0:T(8,128)S(1)} %copy-done.10, f32[2,384,128]{2,1,0:T(8,128)S(1)} %copy-done.2, f32[128,384]{1,0:T(8,128)S(1)} %copy-done.5), custom_call_target="tpu_custom_call" | custom-call | tf_op jit(solution)/shard_map/gather/pallas_call | solution.py:623
  29.5 1.8 %copy-done = bf16[8,576,384]{2,1,0:T(8,128)(2,1)} copy-done((bf16[8,576,384]{2,1,0:T(8,128)(2,1)}, bf16[8,576,384]{2,1,0:T(8,128)(2,1)S(1)}, u32[]{:S(2)}) %copy-start) | copy-done | bytes 3538968
  31.3 0.7 reshape.469.var_ref
  32.0 0.6 convert_bitcast_fusion.time_ref
  32.6 37.1 %layer.1 = (bf16[1024,384]{1,0:T(8,128)(2,1)}, bf16[1024,384]{1,0:T(8,128)(2,1)}, bf16[8,576,384]{2,1,0:T(8,128)(2,1)}, f32[24,384]{1,0:T(8,128)}) custom-call(s32[16]{0:T(128)} %lengths.1, f32[2,6]{1,0:T(2,128)} %bias.3, bf16[1024,384]{1,0:T(8,128)(2,1)} %tok_ref.1, bf16[1024,384]{1,0:T(8,128)(2,1)} %cot_ref.1, f32[8,128]{1,0:T(8,128)} %reshape.469.var_ref, ...), custom_call_target="tpu_custom_call" | custom-call | tf_op jit(solution)/shard_map/layer/pallas_call | solution.py:307
  69.8 1.1 copy.42.mqkv_ref.m_qkv
  70.8 68.8 %reduce.1 = (bf16[576,384]{1,0:T(8,128)(2,1)}, bf16[576,384]{1,0:T(8,128)(2,1)}, f32[24,384]{1,0:T(8,128)}) custom-call(bf16[4,2,576,384]{3,2,1,0:T(8,128)(2,1)} %bitcast.9, f32[24,384]{1,0:T(8,128)} %get-tuple-element.52.stat_ref, f32[3,384,48]{2,1,0:T(8,128)} %copy.42.mqkv_ref.m_qkv, f32[48,384]{1,0:T(8,128)} %m_out.1, f32[2,384,128]{2,1,0:T(8,128)} %m_gate_up.1, ...), custom_call_target="tpu_custom_call" | custom-call | tf_op jit(solution)/shard_map/reduce/pallas_call | solution.py:1117
  139.7 1.0 copy-done.8
  140.7 1.0 copy-done.9
  141.7 0.9 copy-done.11
  142.6 0.9 copy-done.12
  143.5 0.8 copy-done.13
  144.2 0.7 copy-done.18
  144.9 0.7 copy-done.19
  145.6 1.9 %update.1 = (f32[3,384,48]{2,1,0:T(8,128)S(1)}, f32[48,384]{1,0:T(8,128)}, f32[2,384,128]{2,1,0:T(8,128)}, f32[128,384]{1,0:T(8,128)}, f32[3,384,48]{2,1,0:T(8,1...) custom-call(bf16[576,384]{1,0:T(8,128)(2,1)S(1)} %copy-done.8, ...), custom_call_target="tpu_custom_call" | custom-call | tf_op jit(solution)/shard_map/update/pallas_call | solution.py:1244
  147.5 0.9 copy.45
  148.4 0.9 copy.46
  149.3 0.9 copy.47
  (39 shorter events, 0.2 us)
Async XLA Ops:
  0.7 30.7 %copy-start.21 = (s32[16,64]{1,0:T(8,128)S(1)}, s32[16,64]{1,0:T(8,128)}, u32[]{:S(2)}) copy-start(s32[16,64]{1,0:T(8,128)} %param.22) | copy-start | bytes 12292
  0.7 31.3 %copy-start.22 = (s32[1024]{0:T(1024)S(1)}, s32[1024]{0:T(1024)}, u32[]{:S(2)}) copy-start(s32[1024]{0:T(1024)} %param.23) | copy-start | bytes 12292
  2.8 1.0 copy-start.2
  3.8 0.9 copy-start.5
  4.7 0.9 copy-start.10
  29.5 1.8 %copy-start = (bf16[8,576,384]{2,1,0:T(8,128)(2,1)}, bf16[8,576,384]{2,1,0:T(8,128)(2,1)S(1)}, u32[]{:S(2)}) copy-start(bf16[8,576,384]{2,1,0:T(8,128)(2,1)S(1)} %gather.1.w_ref) | copy-start | bytes 10616836
  31.3 38.4 %copy-start.20 = (f32[3,384,48]{1,2,0:T(8,128)S(1)}, f32[3,384,48]{1,2,0:T(8,128)}, u32[]{:S(2)}) copy-start(f32[3,384,48]{1,2,0:T(8,128)} %param.28) | copy-start | bytes 663556
  69.7 69.9 %copy-start.3 = (f32[2,384,128]{2,1,0:T(8,128)S(1)}, f32[2,384,128]{2,1,0:T(8,128)}, u32[]{:S(2)}) copy-start(f32[2,384,128]{2,1,0:T(8,128)} %w_gate_up.1) | copy-start | bytes 1179652
  69.7 69.9 %copy-start.4 = (f32[2,384,128]{2,1,0:T(8,128)S(1)}, f32[2,384,128]{2,1,0:T(8,128)}, u32[]{:S(2)}) copy-start(f32[2,384,128]{2,1,0:T(8,128)} %m_gate_up.1) | copy-start | bytes 1179652
  69.7 69.9 %copy-start.6 = (f32[128,384]{1,0:T(8,128)S(1)}, f32[128,384]{1,0:T(8,128)}, u32[]{:S(2)}) copy-start(f32[128,384]{1,0:T(8,128)} %w_down.1) | copy-start | bytes 589828
  69.7 69.9 %copy-start.7 = (f32[128,384]{1,0:T(8,128)S(1)}, f32[128,384]{1,0:T(8,128)}, u32[]{:S(2)}) copy-start(f32[128,384]{1,0:T(8,128)} %m_down.1) | copy-start | bytes 589828
  69.7 69.9 %copy-start.14 = (f32[2,384]{1,0:T(2,128)S(1)}, f32[2,384]{1,0:T(2,128)}, u32[]{:S(2)}) copy-start(f32[2,384]{1,0:T(2,128)} %gains.1) | copy-start | bytes 9220
  69.7 69.9 %copy-start.15 = (f32[2,6]{1,0:T(2,128)S(1)}, f32[2,6]{1,0:T(2,128)}, u32[]{:S(2)}) copy-start(f32[2,6]{1,0:T(2,128)} %bias.3) | copy-start | bytes 148
  69.7 69.9 %copy-start.16 = (f32[2,384]{1,0:T(2,128)S(1)}, f32[2,384]{1,0:T(2,128)}, u32[]{:S(2)}) copy-start(f32[2,384]{1,0:T(2,128)} %gain_moment.1) | copy-start | bytes 9220
  69.7 69.9 %copy-start.17 = (f32[2,384]{1,0:T(2,128)S(1)}, f32[2,384]{1,0:T(2,128)}, u32[]{:S(2)}) copy-start(f32[2,384]{1,0:T(2,128)} %gain_square.1) | copy-start | bytes 9220
  70.8 68.8 %copy-start.1 = (f32[3,384,48]{2,1,0:T(8,128)S(1)}, f32[3,384,48]{2,1,0:T(8,128)}, u32[]{:S(2)}) copy-start(f32[3,384,48]{2,1,0:T(8,128)} %copy.42.mqkv_ref.m_qkv) | copy-start | bytes 663556
  139.7 1.0 copy-start.8
  140.7 1.0 copy-start.9
  141.7 0.9 copy-start.11
  142.6 0.9 copy-start.12
  143.5 0.8 copy-start.13
  144.2 0.7 copy-start.18
  144.9 0.7 copy-start.19

commit v4 on v2

--- a/solution.py
+++ b/solution.py
@@ -3,6 +3,7 @@
 
 import jax
 import jax.numpy as jnp
+import numpy as np
 from jax import lax
 from jax.experimental import pallas as pl
 from jax.experimental.pallas import tpu as pltpu
@@ -34,6 +35,7 @@
 BLOCK = 256
 PAIR = 2 * BUCKET
 LANES = 2 * HEAD_DIM
+STATS = 24
 WHOLE = pl.BlockSpec(memory_space=pltpu.VMEM)
 SCALARS = pl.BlockSpec(memory_space=pltpu.SMEM)
 
@@ -70,8 +72,7 @@
     out_ref,
     gtok_ref,
     grad_ref,
-    ggain_ref,
-    gbias_ref,
+    stat_ref,
     n1_s,
     n2_s,
     att_s,
@@ -97,8 +98,7 @@
 
     @pl.when(step == 0)
     def _():
-        ggain_ref[...] = jnp.zeros_like(ggain_ref)
-        gbias_ref[...] = jnp.zeros_like(gbias_ref)
+        stat_ref[...] = jnp.zeros_like(stat_ref)
 
     lane = lax.broadcasted_iota(jnp.int32, (1, LANES), 1)
     low_head = lane < HEAD_DIM
@@ -210,7 +210,7 @@
     gg_s[here, :] = g_gate
     gu_s[here, :] = g_up
     e_two = mul_nn(g_gate, w_gate) + mul_nn(g_up, w_up)
-    ggain_ref[1:2, :] += jnp.sum(e_two * unit_two, axis=0, keepdims=True)
+    stat_ref[1:2, :] += jnp.sum(e_two * unit_two, axis=0, keepdims=True)
     scaled = e_two * gain_two
     g_mid = g_out + scale_two * (
         scaled - unit_two * jnp.mean(scaled * unit_two, axis=-1, keepdims=True)
@@ -239,10 +239,10 @@
         for j in range(2):
             h = 2 * hp + j
             mine = g_scores[j * PAIR : (j + 1) * PAIR]
-            gbias_ref[h : h + 1, :] += jnp.sum(
+            stat_ref[8 + h : 9 + h, :PAIR] += jnp.sum(
                 jnp.where(same_var, mine, 0.0), axis=0, keepdims=True
             )
-            gbias_ref[8 + h : 9 + h, :] += jnp.sum(
+            stat_ref[16 + h : 17 + h, :PAIR] += jnp.sum(
                 jnp.where(same_var, 0.0, mine), axis=0, keepdims=True
             )
         low_scores = g_scores.astype(LOW)
@@ -262,7 +262,7 @@
     g_qkv = jnp.concatenate(g_q + g_k + g_v, axis=1)
     gqkv_s[here, :] = g_qkv
     e_one = mul_nn(g_qkv, weight(0, 3))
-    ggain_ref[0:1, :] += jnp.sum(e_one * unit_one, axis=0, keepdims=True)
+    stat_ref[0:1, :] += jnp.sum(e_one * unit_one, axis=0, keepdims=True)
     scaled = e_one * gain_one
     gtok_ref[...] = (
         g_mid
@@ -312,11 +312,10 @@
             jax.ShapeDtypeStruct((rows, width), LOW),
             jax.ShapeDtypeStruct((rows, width), LOW),
             jax.ShapeDtypeStruct((copies, shard_rows, width), grad_type),
-            jax.ShapeDtypeStruct((2, width), WIDE),
-            jax.ShapeDtypeStruct((16, PAIR), WIDE),
+            jax.ShapeDtypeStruct((STATS, width), WIDE),
         ),
         in_specs=[SCALARS, SCALARS, block, block, WHOLE, WHOLE, WHOLE, WHOLE, WHOLE],
-        out_specs=(block, block, WHOLE, WHOLE, WHOLE),
+        out_specs=(block, block, WHOLE, WHOLE),
         scratch_shapes=[
             low_scratch(width),
             low_scratch(width),
@@ -393,6 +392,1139 @@
     corrected = new_moment / (1.0 - BETA_ONE**STEP)
     scaled = jnp.sqrt(new_square / (1.0 - BETA_TWO**STEP)) + ADAM_EPS
     return (new_moment, new_square, param - ADAM_RATE * corrected / scaled)
+
+
+DEPTH, ACROSS = 4, 2
+SIDES, CORES = 2, 2
+TURNS = (2, 1, 3, 0)
+OWNERS = (
+    (2, 0, 0, 0),
+    (2, 1, 0, 1),
+    (1, 1, 0, 0),
+    (2, 1, 1, 0),
+    (2, 0, 1, 1),
+    (1, 0, 0, 1),
+    (1, 1, 1, 0),
+)
+
+
+def place():
+    f = lax.axis_index("fsdp")
+    n = lax.axis_index("ns")
+    return f // ACROSS, f % ACROSS, n // CORES, n % CORES
+
+
+def device(z, x, y, c):
+    return (z * ACROSS + x, y * CORES + c)
+
+
+def remote(src, dst, send_sem, recv_sem, where):
+    return pltpu.make_async_remote_copy(
+        src_ref=src,
+        dst_ref=dst,
+        send_sem=send_sem,
+        recv_sem=recv_sem,
+        device_id=where,
+        device_id_type=pl.DeviceIdType.MESH,
+    )
+
+
+def greet(where):
+    pl.semaphore_signal(
+        pltpu.get_barrier_semaphore(),
+        inc=1,
+        device_id=where,
+        device_id_type=pl.DeviceIdType.MESH,
+    )
+
+
+def halves(value):
+    high = value.astype(LOW)
+    return high, (value - high.astype(WIDE)).astype(LOW)
+
+
+def mul_wide(left, right):
+    columns = right.shape[1]
+    left_high, left_low = halves(left)
+    right_high, right_low = halves(right)
+    first = mul_nn(left_high, jnp.concatenate([right_high, right_low], axis=1))
+    return first[:, :columns] + (first[:, columns:] + mul_nn(left_low, right_high))
+
+
+def gram_wide(value):
+    high, low = halves(value)
+    cross = mul_tn(high, low)
+    return mul_tn(high, high) + (cross + cross.T)
+
+
+def whole_kernel(
+    pieces,
+    lengths,
+    bias,
+    tok_ref,
+    cot_ref,
+    var_ref,
+    time_ref,
+    table_ref,
+    gain_ref,
+    wqkv_ref,
+    wout_ref,
+    wgate_up_ref,
+    wdown_ref,
+    mqkv_ref,
+    mout_ref,
+    mgate_up_ref,
+    mdown_ref,
+    out_ref,
+    gtok_ref,
+    grows_ref,
+    xrows_ref,
+    total_ref,
+    w_s,
+    grad_s,
+    momenta,
+    n1_s,
+    n2_s,
+    att_s,
+    gml_s,
+    glow_s,
+    hid_s,
+    gg_s,
+    gu_s,
+    low_s,
+    gqkv_s,
+    probs_s,
+    mid_s,
+    gmid_s,
+    gatt_s,
+    scale_s,
+    rope_s,
+    y_attn,
+    y_ff,
+    x_attn,
+    x_ff,
+    gram_s,
+    chain_s,
+    stat_s,
+    stat_in,
+    stat_acc,
+    stat_line,
+    stat_send,
+    stat_recv,
+    adv_recv,
+    x_send,
+    x_recv,
+    fan_send,
+    fan_recv,
+    *per_part,
+):
+    z, x, y, c = place()
+    shard = z * ACROSS + x
+    rows, width = tok_ref.shape
+    heads = bias.shape[1]
+    sibling = device(z, x, y, 1 - c)
+    facing = device(z, x, 1 - y, c)
+    corner = device(z, x, 1 - y, 1 - c)
+    beside = device(z, 1 - x, y, c)
+    upper = device(z + 1, x, y, c)
+    lower = device(z - 1, x, y, c)
+    world = DEPTH * ACROSS * SIDES * CORES
+    rank = shard * (SIDES * CORES) + y * CORES + c
+    line = [lax.rem(z + k, DEPTH) for k in range(DEPTH)]
+    part = 2 * c + y
+
+    def hello(i, carry):
+        other = lax.rem(rank + 1 + i, world)
+        greet((other // (SIDES * CORES), lax.rem(other, SIDES * CORES)))
+        return carry
+
+    lax.fori_loop(0, world - 1, hello, 0)
+
+    def put(index, value):
+        start, count = pieces[index]
+        w_s[shard, start : start + count, :] = value.astype(LOW)
+
+    for j in range(3):
+        put(j, wqkv_ref[j])
+    put(3, wout_ref[...])
+    put(4, wgate_up_ref[0].T)
+    put(5, wgate_up_ref[1].T)
+    put(6, wdown_ref[...])
+    pl.semaphore_wait(pltpu.get_barrier_semaphore(), world - 1)
+
+    has_up = z < DEPTH - 1
+    has_down = z > 0
+
+    def exists(rel):
+        return (z + rel >= 0) & (z + rel < DEPTH)
+
+    class Gather:
+        def __init__(self, start, count, sems):
+            self.start_row, self.half = start, count // 2
+            (
+                self.up_send,
+                self.down_send,
+                self.x_send,
+                self.sib_send,
+                self.below_recv,
+                self.above_recv,
+                self.x_recv,
+                self.sib_recv,
+            ) = sems
+
+        def view(self, at, core):
+            first = pl.multiple_of(self.start_row + core * self.half, 16)
+            return w_s.at[at, pl.ds(first, self.half)]
+
+        def mine(self, rel):
+            return self.view(shard + rel * ACROSS, c)
+
+        def others(self, rel):
+            return self.view((z + rel) * ACROSS + 1 - x, c)
+
+        def up(self, d):
+            return remote(
+                self.mine(-d), self.mine(-d), self.up_send.at[d], self.below_recv.at[d], upper
+            )
+
+        def down(self, d):
+            return remote(
+                self.mine(d), self.mine(d), self.down_send.at[d], self.above_recv.at[d], lower
+            )
+
+        def over(self, rel, where):
+            return remote(
+                self.mine(rel), where, self.x_send.at[rel + 3], self.x_recv.at[rel + 3], beside
+            )
+
+        def sib(self, kind, rel, src):
+            return remote(
+                src, src, self.sib_send.at[kind, rel + 3], self.sib_recv.at[kind, rel + 3], sibling
+            )
+
+        def start(self):
+            @pl.when(has_up)
+            def _():
+                self.up(0).start()
+
+            @pl.when(has_down)
+            def _():
+                self.down(0).start()
+
+            self.over(0, self.mine(0)).start()
+
+        def hop(self, d):
+            @pl.when(exists(-d))
+            def _():
+                here = self.mine(-d)
+                remote(
+                    here, here, self.up_send.at[d], self.below_recv.at[d - 1], lower
+                ).wait_recv()
+                if d < DEPTH - 1:
+
+                    @pl.when(has_up)
+                    def _():
+                        self.up(d).start()
+
+                self.over(-d, here).start()
+                self.sib(0, -d, here).start()
+
+            @pl.when(exists(d))
+            def _():
+                here = self.mine(d)
+                remote(
+                    here, here, self.down_send.at[d], self.above_recv.at[d - 1], upper
+                ).wait_recv()
+                if d < DEPTH - 1:
+
+                    @pl.when(has_down)
+                    def _():
+                        self.down(d).start()
+
+                self.over(d, here).start()
+                self.sib(0, d, here).start()
+
+        def from_beside(self, d):
+            for rel in (0,) if d == 0 else (-d, d):
+
+                @pl.when(exists(rel))
+                def _():
+                    there = self.others(rel)
+                    remote(
+                        there, there, self.x_send.at[rel + 3], self.x_recv.at[rel + 3], beside
+                    ).wait_recv()
+                    self.sib(1, rel, there).start()
+
+        def arrive(self):
+            for rel in range(1 - DEPTH, DEPTH):
+
+                @pl.when(exists(rel))
+                def _():
+                    if rel != 0:
+                        self.sib(0, rel, self.view(shard + rel * ACROSS, 1 - c)).wait_recv()
+                    self.sib(1, rel, self.view((z + rel) * ACROSS + 1 - x, 1 - c)).wait_recv()
+
+        def sent(self):
+            for rel in range(1 - DEPTH, DEPTH):
+
+                @pl.when(exists(rel))
+                def _():
+                    if rel != 0:
+                        self.sib(0, rel, self.mine(rel)).wait_send()
+                    self.sib(1, rel, self.others(rel)).wait_send()
+                    self.over(rel, self.mine(rel)).wait_send()
+
+            for d in range(DEPTH - 1):
+
+                @pl.when(exists(-d) & has_up)
+                def _():
+                    self.up(d).wait_send()
+
+                @pl.when(exists(d) & has_down)
+                def _():
+                    self.down(d).wait_send()
+
+    ff_row = pieces[4][0]
+    last_row = pieces[6][0] + pieces[6][1]
+    spans = ((0, ff_row), (ff_row, last_row - ff_row))
+    each = len(per_part) // 2
+    gathers = [Gather(*spans[i], per_part[i * each : i * each + 8]) for i in range(2)]
+    attn_gather, ff_gather = gathers
+    attn_gather.start()
+
+    for i, (value, turned) in enumerate(((mgate_up_ref[0], 4), (mgate_up_ref[1], 5))):
+        start, count = pieces[turned]
+        momenta[start : start + count, :] = value.T
+    for j in range(3):
+        start, count = pieces[j]
+        momenta[start : start + count, :] = mqkv_ref[j]
+    momenta[pieces[3][0] : pieces[3][0] + pieces[3][1], :] = mout_ref[...]
+    momenta[pieces[6][0] : last_row, :] = mdown_ref[...]
+    stat_s[...] = jnp.zeros_like(stat_s)
+
+    lane = lax.broadcasted_iota(jnp.int32, (1, LANES), 1)
+    low_head = lane < HEAD_DIM
+    low_half = lane % HEAD_DIM < HEAD_DIM // 2
+    row_id = lax.broadcasted_iota(jnp.int32, (PAIR, 1), 0)
+    lane_id = lax.broadcasted_iota(jnp.int32, (1, PAIR), 1)
+    same_bucket = (row_id < BUCKET) == (lane_id < BUCKET)
+    slots = lax.broadcasted_iota(jnp.int32, (1, TIME_SLOTS), 1)
+    query_scale = HEAD_DIM ** (-0.5)
+    gain_one = gain_ref[0:1, :]
+    gain_two = gain_ref[1:2, :]
+
+    def column(row):
+        return jnp.broadcast_to(row, (8, PAIR)).T[:, 0:1]
+
+    def var_row(pair):
+        two = var_ref[pl.ds(2 * pair, 2), :]
+        return jnp.concatenate([two[0:1], two[1:2]], axis=1).astype(WIDE)
+
+    def block_of(i, size):
+        return pl.ds(pl.multiple_of(i * size, size), size)
+
+    def prepare(i, carry):
+        here = block_of(i, PAIR)
+        times = column(time_ref[pl.ds(i, 1), :].astype(WIDE)).astype(jnp.int32)
+        hot = (times == slots).astype(LOW)
+        rope_s[here, :] = (
+            mul_nn(hot, table_ref[0]) + mul_nn(hot, table_ref[1]) + mul_nn(hot, table_ref[2])
+        )
+        tokens = tok_ref[here, :].astype(WIDE)
+        scale = lax.rsqrt(jnp.mean(tokens * tokens, axis=-1, keepdims=True) + EPS_NORM)
+        scale_s[here, 0:1] = scale
+        n1_s[here, :] = (tokens * scale * gain_one).astype(LOW)
+        first, second = lengths[2 * i], lengths[2 * i + 1]
+        live = row_id % BUCKET < jnp.where(row_id < BUCKET, first, second)
+        glow_s[here, :] = jnp.where(live, cot_ref[here, :].astype(WIDE), 0.0).astype(LOW)
+        return carry
+
+    lax.fori_loop(0, rows // PAIR, prepare, 0)
+
+    for d in range(1, DEPTH):
+        attn_gather.hop(d)
+    ff_gather.start()
+    for d in range(DEPTH):
+        attn_gather.from_beside(d)
+    attn_gather.arrive()
+
+    def weight(first, last):
+        parts = []
+        for i in range(first, last):
+            start, count = pieces[i]
+            piece = w_s[:, start : start + count, :]
+            parts.append(piece.reshape(piece.shape[0] * count, width))
+        return parts[0] if len(parts) == 1 else jnp.concatenate(parts, axis=0)
+
+    def swapped(values):
+        half = HEAD_DIM // 2
+        return jnp.where(
+            low_half, pltpu.roll(values, LANES - half, 1), pltpu.roll(values, half, 1)
+        )
+
+    def two_heads(value):
+        none = jnp.zeros_like(value)
+        return jnp.concatenate(
+            [jnp.where(low_head, value, none), jnp.where(low_head, none, value)], axis=0
+        )
+
+    per_block = BLOCK // PAIR
+
+    def attend(i, carry):
+        here = block_of(i, BLOCK)
+        qkv = mul_nt(n1_s[here, :], weight(0, 3))
+        cosine = rope_s[here, :LANES]
+        sine = rope_s[here, LANES:]
+        masks = []
+        for p in range(per_block):
+            pair = i * per_block + p
+            first, second = lengths[2 * pair], lengths[2 * pair + 1]
+            live_key = lane_id % BUCKET < jnp.where(lane_id < BUCKET, first, second)
+            row = var_row(pair)
+            masks.append((same_bucket & live_key, column(row) == row))
+        attended = []
+        for hp in range(heads // 2):
+            first = hp * LANES
+            q = qkv[:, first : first + LANES]
+            k = qkv[:, width + first : width + first + LANES]
+            v = qkv[:, 2 * width + first : 2 * width + first + LANES].astype(LOW)
+            q = ((q * cosine + swapped(q) * sine) * query_scale).astype(LOW)
+            k = (k * cosine + swapped(k) * sine).astype(LOW)
+            low_s[here, first : first + LANES] = q
+            low_s[here, width + first : width + first + LANES] = k
+            low_s[here, 2 * width + first : 2 * width + first + LANES] = v
+            pairs = []
+            for p in range(per_block):
+                span = slice(p * PAIR, (p + 1) * PAIR)
+                mask, same_var = masks[p]
+                raw = mul_nt(two_heads(q[span]), k[span])
+                both = []
+                for j in range(2):
+                    h = 2 * hp + j
+                    biased = raw[j * PAIR : (j + 1) * PAIR] + jnp.where(
+                        same_var, bias[0, h], bias[1, h]
+                    )
+                    both.append(jnp.where(mask, biased, NEG_FILL))
+                scores = jnp.concatenate(both, axis=0)
+                exponent = jnp.exp(scores - jnp.max(scores, axis=-1, keepdims=True))
+                probs = exponent / jnp.sum(exponent, axis=-1, keepdims=True)
+                probs_s[i * per_block + p, hp] = probs
+                both = mul_nn(probs.astype(LOW), v[span])
+                pairs.append(jnp.where(low_head, both[:PAIR], both[PAIR:]))
+            attended.append(jnp.concatenate(pairs, axis=0).astype(LOW))
+        attended = jnp.concatenate(attended, axis=1)
+        att_s[here, :] = attended
+        mid = tok_ref[here, :].astype(WIDE) + mul_nn(attended, weight(3, 4))
+        mid_s[here, :] = mid
+        scale = lax.rsqrt(jnp.mean(mid * mid, axis=-1, keepdims=True) + EPS_NORM)
+        scale_s[here, 1:2] = scale
+        n2_s[here, :] = (mid * scale * gain_two).astype(LOW)
+        for d in range(1, DEPTH):
+
+            @pl.when(i == d - 1)
+            def _():
+                ff_gather.hop(d)
+
+        return carry
+
+    lax.fori_loop(0, rows // BLOCK, attend, 0)
+    for d in range(DEPTH):
+        ff_gather.from_beside(d)
+    ff_gather.arrive()
+
+    def feed(i, carry):
+        here = block_of(i, BLOCK)
+        normed_two = n2_s[here, :]
+        w_gate, w_up, w_down = weight(4, 5), weight(5, 6), weight(6, 7)
+        gate = mul_nt(normed_two, w_gate)
+        up = mul_nt(normed_two, w_up)
+        sig = 1.0 / (1.0 + jnp.exp(-gate))
+        silu = gate * sig
+        hid_s[here, :] = (silu * up).astype(LOW)
+        g_low = glow_s[here, :]
+        g_hidden = mul_nt(g_low, w_down)
+        g_gate = (g_hidden * up * sig * (1.0 + gate * (1.0 - sig))).astype(LOW)
+        g_up = (g_hidden * silu).astype(LOW)
+        gg_s[here, :] = g_gate
+        gu_s[here, :] = g_up
+        e_two = mul_nn(g_gate, w_gate) + mul_nn(g_up, w_up)
+        scale = scale_s[here, 1:2]
+        unit = mid_s[here, :] * scale
+        stat_s[1:2, :] += jnp.sum(e_two * unit, axis=0, keepdims=True)
+        scaled = e_two * gain_two
+        g_mid = g_low.astype(WIDE) + scale * (
+            scaled - unit * jnp.mean(scaled * unit, axis=-1, keepdims=True)
+        )
+        gmid_s[here, :] = g_mid
+        g_mid_low = g_mid.astype(LOW)
+        gml_s[here, :] = g_mid_low
+        gatt_s[here, :] = mul_nt(g_mid_low, weight(3, 4)).astype(LOW)
+        return carry
+
+    lax.fori_loop(0, rows // BLOCK, feed, 0)
+
+    def grad_put(index, left, right):
+        start, count = pieces[index]
+        grad_s[:, :, start : start + count, :] = (
+            mul_tn(left, right).reshape(DEPTH, ACROSS, count, width).astype(LOW)
+        )
+
+    class Reduce:
+        def __init__(self, start, count, refs):
+            self.start_row, self.half, self.quarter = start, count // 2, count // 4
+            (
+                self.in_zero,
+                self.acc_zero,
+                self.in_one,
+                self.acc_one,
+                self.in_two,
+                self.acc_two,
+                self.in_three,
+                self.advance,
+                self.send_zero,
+                self.send_one,
+                self.send_two,
+                self.send_three,
+                self.recv_zero,
+                self.recv_one,
+                self.recv_two,
+                self.recv_three,
+                self.adv_send,
+                self.row_send,
+                self.row_recv,
+            ) = refs
+            self.keep_quarter = pl.ds(pl.multiple_of(y * self.quarter, 16), self.quarter)
+            self.give_quarter = pl.ds(pl.multiple_of((1 - y) * self.quarter, 16), self.quarter)
+            self.first_quarter = pl.ds(0, self.quarter)
+
+        def half_of(self, core):
+            return pl.ds(pl.multiple_of(self.start_row + core * self.half, 16), self.half)
+
+        def rows_of(self, quarter):
+            first = pl.multiple_of(self.start_row + quarter * self.quarter, 16)
+            return pl.ds(first, self.quarter)
+
+        def zero(self, k):
+            return remote(
+                grad_s.at[line[k], :, self.half_of(1 - c)],
+                self.in_zero.at[k],
+                self.send_zero.at[k],
+                self.recv_zero.at[k],
+                sibling,
+            )
+
+        def one(self, k, core):
+            if core == 0:
+                src, dst = self.acc_zero.at[k, :, self.give_quarter], self.in_one.at[
+                    k, :, self.first_quarter
+                ]
+            else:
+                src, dst = self.acc_zero.at[k, 1 - x], self.in_one.at[k, 0]
+            where = facing if core == 0 else beside
+            return remote(src, dst, self.send_one.at[k], self.recv_one.at[k], where)
+
+        def two(self, k, core):
+            if core == 0:
+                src = self.acc_one.at[k, 1 - x, self.first_quarter]
+            else:
+                src = self.acc_one.at[k, 0, self.give_quarter]
+            where = beside if core == 0 else facing
+            return remote(src, self.in_two.at[k], self.send_two.at[k], self.recv_two.at[k], where)
+
+        def three(self, k):
+            return remote(
+                self.acc_two.at[k],
+                self.in_three.at[k],
+                self.send_three.at[k],
+                self.recv_three.at[k],
+                device(line[k], x, y, c),
+            )
+
+        def start(self):
+            for k in TURNS:
+                self.zero(k).start()
+
+        def step(self, t):
+            def add(left, right):
+                return (left.astype(WIDE) + right.astype(WIDE)).astype(LOW)
+
+            quarter = self.quarter
+            if t < DEPTH:
+                k = TURNS[t]
+                self.zero(k).wait_recv()
+                self.acc_zero[k] = add(grad_s[line[k], :, self.half_of(c)], self.in_zero[k])
+                for core in range(2):
+
+                    @pl.when(c == core)
+                    def _():
+                        self.one(k, core).start()
+
+            if 1 <= t <= DEPTH:
+                k = TURNS[t - 1]
+
+                @pl.when(c == 0)
+                def _():
+                    self.one(k, 0).wait_recv()
+                    self.acc_one[k, :, :quarter] = add(
+                        self.acc_zero[k, :, self.keep_quarter], self.in_one[k, :, :quarter]
+                    )
+                    self.two(k, 0).start()
+
+                @pl.when(c == 1)
+                def _():
+                    self.one(k, 1).wait_recv()
+                    self.acc_one[k, 0] = add(self.acc_zero[k, x], self.in_one[k, 0])
+                    self.two(k, 1).start()
+
+            if 2 <= t:
+                k = TURNS[t - 2]
+
+                @pl.when(c == 0)
+                def _():
+                    self.two(k, 0).wait_recv()
+                    self.acc_two[k] = add(self.acc_one[k, x, :quarter], self.in_two[k])
+
+                @pl.when(c == 1)
+                def _():
+                    self.two(k, 1).wait_recv()
+                    self.acc_two[k] = add(self.acc_one[k, 0, self.keep_quarter], self.in_two[k])
+
+                if k != 0:
+                    self.three(k).start()
+
+        def segments(self, index):
+            found = []
+            begin = self.start_row + index * self.quarter
+            for m, (start, count) in enumerate(pieces):
+                first, last = max(start, begin), min(start + count, begin + self.quarter)
+                if first < last:
+                    found.append((m, first - begin, first - start, last - first))
+            return found
+
+        def adv_copy(self, index, i):
+            m, first, to, count = self.segments(index)[i]
+            return remote(
+                self.advance.at[pl.ds(first, count)],
+                stage(m).at[shard, pl.ds(to, count)],
+                self.adv_send.at[i],
+                adv_recv.at[0],
+                device(*OWNERS[m]),
+            )
+
+        def row_copy(self, j, quarter, where):
+            here = grows_ref.at[self.rows_of(quarter)]
+            return remote(here, here, self.row_send.at[j], self.row_recv.at[j], where)
+
+        def finish(self):
+            total = self.acc_two[0].astype(WIDE)
+            for k in range(1, DEPTH):
+                self.three(k).wait_recv()
+                total = total + self.in_three[k].astype(WIDE)
+            old = momenta[self.rows_of(part), :]
+            self.advance[...] = total + MUON_MU * (MUON_MU * old + total)
+            for index in range(4):
+                for i, (m, first, to, count) in enumerate(self.segments(index)):
+
+                    @pl.when((part == index) & jnp.logical_not(owned(m)))
+                    def _():
+                        self.adv_copy(index, i).start()
+
+                    @pl.when((part == index) & owned(m))
+                    def _():
+                        pltpu.make_async_copy(
+                            self.advance.at[pl.ds(first, count)],
+                            stage(m).at[shard, pl.ds(to, count)],
+                            adv_recv.at[0],
+                        ).start()
+
+            grows_ref[self.rows_of(part), :] = total.astype(LOW)
+            for j, where in enumerate((sibling, facing, corner)):
+                self.row_copy(j, part, where).start()
+
+        def done(self):
+            mates = ((sibling, 0, 1), (facing, 1, 0), (corner, 1, 1))
+            for j, (where, dy, dc) in enumerate(mates):
+                self.row_copy(j, 2 * (c ^ dc) + (y ^ dy), where).wait_recv()
+                self.row_copy(j, part, where).wait_send()
+            for index in range(4):
+                for i, (m, first, to, count) in enumerate(self.segments(index)):
+
+                    @pl.when((part == index) & jnp.logical_not(owned(m)))
+                    def _():
+                        self.adv_copy(index, i).wait_send()
+
+            for k in TURNS:
+                self.zero(k).wait_send()
+                if k != 0:
+                    self.three(k).wait_send()
+                for core in range(2):
+
+                    @pl.when(c == core)
+                    def _():
+                        self.one(k, core).wait_send()
+                        self.two(k, core).wait_send()
+
+    def owned(m):
+        oz, ox, oy, oc = OWNERS[m]
+        return (z == oz) & (x == ox) & (y == oy) & (c == oc)
+
+    def stage(m):
+        return y_attn if m < 4 else y_ff
+
+    reduces = [Reduce(*spans[i], per_part[i * each + 8 : (i + 1) * each]) for i in range(2)]
+    attn_reduce, ff_reduce = reduces
+
+    grad_put(4, gg_s[...], n2_s[...])
+    grad_put(5, gu_s[...], n2_s[...])
+    grad_put(6, hid_s[...], glow_s[...])
+    ff_reduce.start()
+
+    def attend_back(i, carry):
+        here = block_of(i, PAIR)
+        row = var_row(i)
+        same_var = column(row) == row
+        cosine = rope_s[here, :LANES]
+        sine = rope_s[here, LANES:]
+        for hp in range(heads // 2):
+            first = hp * LANES
+            q2 = two_heads(low_s[here, first : first + LANES])
+            k = low_s[here, width + first : width + first + LANES]
+            v = low_s[here, 2 * width + first : 2 * width + first + LANES]
+            probs = probs_s[i, hp]
+            ga2 = two_heads(gatt_s[here, first : first + LANES])
+            g_probs = mul_nt(ga2, v)
+            row_dot = jnp.sum(probs * g_probs, axis=-1, keepdims=True)
+            g_scores = probs * (g_probs - row_dot)
+            for j in range(2):
+                h = 2 * hp + j
+                mine = g_scores[j * PAIR : (j + 1) * PAIR]
+                stat_s[8 + h : 9 + h, :PAIR] += jnp.sum(
+                    jnp.where(same_var, mine, 0.0), axis=0, keepdims=True
+                )
+                stat_s[16 + h : 17 + h, :PAIR] += jnp.sum(
+                    jnp.where(same_var, 0.0, mine), axis=0, keepdims=True
+                )
+            low_scores = g_scores.astype(LOW)
+            both = mul_nn(low_scores, k)
+            dq = jnp.where(low_head, both[:PAIR], both[PAIR:])
+            dk = mul_tn(low_scores, q2)
+            dv = mul_tn(probs.astype(LOW), ga2)
+            gqkv_s[here, first : first + LANES] = (
+                (dq * cosine - swapped(dq) * sine) * query_scale
+            ).astype(LOW)
+            gqkv_s[here, width + first : width + first + LANES] = (
+                dk * cosine - swapped(dk) * sine
+            ).astype(LOW)
+            gqkv_s[here, 2 * width + first : 2 * width + first + LANES] = dv.astype(LOW)
+        for t in range(DEPTH + 2):
+
+            @pl.when(i == t)
+            def _():
+                ff_reduce.step(t)
+
+        return carry
+
+    lax.fori_loop(0, rows // PAIR, attend_back, 0)
+    for j in range(3):
+        grad_put(j, gqkv_s[:, j * width : (j + 1) * width], n1_s[...])
+    grad_put(3, att_s[...], gml_s[...])
+    attn_reduce.start()
+    ff_reduce.finish()
+
+    def last(i):
+        here = block_of(i, 2 * BLOCK)
+        e_one = mul_nn(gqkv_s[here, :], weight(0, 3))
+        scale = scale_s[here, 0:1]
+        unit = tok_ref[here, :].astype(WIDE) * scale
+        stat_s[0:1, :] += jnp.sum(e_one * unit, axis=0, keepdims=True)
+        scaled = e_one * gain_one
+        gtok_ref[here, :] = (
+            gmid_s[here, :]
+            + scale * (scaled - unit * jnp.mean(scaled * unit, axis=-1, keepdims=True))
+        ).astype(LOW)
+
+    def outgoing(i):
+        here = block_of(i, 2 * BLOCK)
+        out_ref[here, :] = (mid_s[here, :] + mul_nn(hid_s[here, :], weight(6, 7))).astype(LOW)
+
+    def stat_copy(step, src, where):
+        return remote(src, stat_in.at[step], stat_send.at[step], stat_recv.at[step], where)
+
+    attn_reduce.step(0)
+    last(0)
+    attn_reduce.step(1)
+    last(1)
+    stat_copy(0, stat_s, sibling).start()
+    attn_reduce.step(2)
+    outgoing(0)
+    stat_copy(0, stat_s, sibling).wait()
+    stat_acc[0] = stat_s[...] + stat_in[0]
+    stat_copy(1, stat_acc.at[0], facing).start()
+    attn_reduce.step(3)
+    outgoing(1)
+    attn_reduce.step(4)
+    attn_reduce.step(5)
+    stat_copy(1, stat_acc.at[0], facing).wait()
+    stat_acc[1] = stat_acc[0] + stat_in[1]
+    stat_copy(2, stat_acc.at[1], beside).start()
+    attn_reduce.finish()
+    stat_copy(2, stat_acc.at[1], beside).wait()
+    stat_acc[2] = stat_acc[1] + stat_in[2]
+    stat_line[z] = stat_acc[2]
+
+    def stat_send_line(j):
+        return remote(
+            stat_acc.at[2],
+            stat_line.at[z],
+            stat_send.at[2 + j],
+            stat_recv.at[2 + j],
+            device(line[j], x, y, c),
+        )
+
+    for j in range(1, DEPTH):
+        stat_send_line(j).start()
+
+    attn_owner = functools.reduce(jnp.logical_or, [owned(m) for m in range(4)])
+    ff_owner = functools.reduce(jnp.logical_or, [owned(m) for m in range(4, 7)])
+
+    def arrived(buffer):
+        pltpu.make_async_copy(buffer, buffer, adv_recv.at[0]).wait()
+
+    @pl.when(attn_owner)
+    def _():
+        arrived(y_attn)
+        gram_s[...] = gram_wide(y_attn[...].reshape(-1, width))
+
+    @pl.when(ff_owner)
+    def _():
+        arrived(y_ff)
+        gram_s[...] = gram_wide(y_ff[...].reshape(-1, width))
+
+    @pl.when(attn_owner | ff_owner)
+    def _():
+        unit = lax.broadcasted_iota(jnp.int32, (width, width), 0) == lax.broadcasted_iota(
+            jnp.int32, (width, width), 1
+        )
+        gram_mat = gram_s[...]
+        trace = jnp.sum(jnp.where(unit, gram_mat, 0.0), keepdims=True)
+        inverse = 1.0 / (jnp.sqrt(trace) + NS_EPS)
+        diagonal = jnp.where(unit, COEF_A, 0.0)
+        gram_mat = gram_mat * (inverse * inverse)
+
+        def poly(value):
+            return diagonal + COEF_B * value + COEF_C * mul_wide(value, value)
+
+        step_mat = poly(gram_mat)
+        gram_s[...] = mul_wide(mul_wide(gram_mat, step_mat), step_mat)
+        chain_s[...] = step_mat * inverse
+
+        def turn(i, carry):
+            now = gram_s[...]
+            step_now = poly(now)
+            both = mul_wide(jnp.concatenate([now, chain_s[...]], axis=0), step_now)
+            chain_s[...] = both[width:]
+            gram_s[...] = mul_wide(both[:width], step_now)
+            return carry
+
+        lax.fori_loop(0, NS_ITERS - 2, turn, 0)
+        chain_s[...] = mul_wide(chain_s[...], poly(gram_s[...]))
+
+    @pl.when(attn_owner)
+    def _():
+        value = y_attn[...].reshape(-1, width)
+        x_attn[...] = mul_wide(value, chain_s[...]).astype(LOW).reshape(x_attn.shape)
+
+    @pl.when(ff_owner)
+    def _():
+        value = y_ff[...].reshape(-1, width)
+        x_ff[...] = mul_wide(value, chain_s[...]).astype(LOW).reshape(x_ff.shape)
+
+    chips = DEPTH * ACROSS * SIDES
+
+    def x_copy(m, i):
+        start, count = pieces[m]
+        source = x_attn if m < 4 else x_ff
+        to = i // SIDES
+        return remote(
+            source.at[to],
+            xrows_ref.at[pl.ds(start, count)],
+            x_send.at[i],
+            x_recv.at[m],
+            (to, lax.rem(i, SIDES) * CORES + OWNERS[m][3]),
+        )
+
+    mine = shard * SIDES + y
+    for m in range(7):
+        start, count = pieces[m]
+        source = x_attn if m < 4 else x_ff
+
+        @pl.when(owned(m))
+        def _():
+            def send(i, carry):
+                x_copy(m, lax.rem(mine + i, chips)).start()
+                return carry
+
+            lax.fori_loop(1, chips, send, 0)
+            pltpu.make_async_copy(
+                source.at[shard], xrows_ref.at[pl.ds(start, count)], x_recv.at[m]
+            ).start()
+
+    for j in range(1, DEPTH):
+        remote(
+            stat_acc.at[2],
+            stat_line.at[lax.rem(z + DEPTH - j, DEPTH)],
+            stat_send.at[2 + j],
+            stat_recv.at[2 + j],
+            device(line[j], x, y, c),
+        ).wait()
+    total_ref[...] = (stat_line[0] + stat_line[1]) + (stat_line[2] + stat_line[3])
+    for one in gathers:
+        one.sent()
+    for one in reduces:
+        one.done()
+
+    def fan_copy(m):
+        start, count = pieces[m]
+        rows_m = xrows_ref.at[pl.ds(start, count)]
+        return remote(rows_m, rows_m, fan_send.at[m], fan_recv.at[m], sibling)
+
+    for m in range(7):
+        start, count = pieces[m]
+
+        @pl.when(c == OWNERS[m][3])
+        def _():
+            rows_m = xrows_ref.at[pl.ds(start, count)]
+            pltpu.make_async_copy(rows_m, rows_m, x_recv.at[m]).wait()
+            fan_copy(m).start()
+
+    for m in range(7):
+
+        @pl.when(c != OWNERS[m][3])
+        def _():
+            fan_copy(m).wait_recv()
+
+        @pl.when(c == OWNERS[m][3])
+        def _():
+            fan_copy(m).wait_send()
+
+        @pl.when(owned(m))
+        def _():
+            def sent(i, carry):
+                x_copy(m, lax.rem(mine + i, chips)).wait_send()
+                return carry
+
+            lax.fori_loop(1, chips, sent, 0)
+
+
+def rotary_table():
+    half = HEAD_DIM // 2
+    frequency = (ROPE_BASE ** (-2.0 * np.arange(half) / HEAD_DIM)).astype(np.float32)
+    angles = np.arange(TIME_SLOTS, dtype=np.float32)[:, None] * frequency[None, :]
+    cosine = np.cos(angles.astype(np.float64)).astype(np.float32)
+    sine = np.sin(angles.astype(np.float64)).astype(np.float32)
+    table = np.concatenate([cosine] * 4 + [-sine, sine, -sine, sine], axis=1)
+    parts = []
+    for _ in range(3):
+        parts.append(table.astype(LOW))
+        table = table - parts[-1].astype(np.float32)
+    return np.stack(parts)
+
+
+def whole_step(tokens, cotangent, lengths, variates, times, gains, attn_bias, weights, momenta):
+    rows, width = tokens.shape
+    heads = attn_bias.shape[1]
+    attn_rows, ff_rows = weights[1].shape[0], weights[3].shape[0]
+    pieces = offsets(attn_rows, ff_rows)
+    ff = ff_rows * DEPTH * ACROSS
+    shards = DEPTH * ACROSS
+    shard_rows = 4 * attn_rows + 3 * ff_rows
+    low = lambda *shape: pltpu.VMEM(shape, LOW)
+    wide = lambda *shape: pltpu.VMEM(shape, WIDE)
+    dma = lambda *shape: pltpu.SemaphoreType.DMA(shape)
+
+    def part_scratch(count):
+        half, quarter = count // 2, count // 4
+        relative = 2 * DEPTH - 1
+        return [
+            dma(DEPTH),
+            dma(DEPTH),
+            dma(relative),
+            dma(2, relative),
+            dma(DEPTH),
+            dma(DEPTH),
+            dma(relative),
+            dma(2, relative),
+            low(DEPTH, ACROSS, half, width),
+            low(DEPTH, ACROSS, half, width),
+            low(DEPTH, ACROSS, half, width),
+            low(DEPTH, ACROSS, half, width),
+            low(DEPTH, quarter, width),
+            low(DEPTH, quarter, width),
+            low(DEPTH, quarter, width),
+            wide(quarter, width),
+            *[dma(DEPTH) for _ in range(8)],
+            dma(3),
+            dma(3),
+            dma(3),
+        ]
+
+    return pl.pallas_call(
+        functools.partial(whole_kernel, pieces),
+        out_shape=(
+            jax.ShapeDtypeStruct((rows, width), LOW),
+            jax.ShapeDtypeStruct((rows, width), LOW),
+            jax.ShapeDtypeStruct((shard_rows, width), LOW),
+            jax.ShapeDtypeStruct((shard_rows, width), LOW),
+            jax.ShapeDtypeStruct((STATS, width), WIDE),
+        ),
+        in_specs=[SCALARS] * 2 + [WHOLE] * 14,
+        out_specs=(WHOLE,) * 5,
+        scratch_shapes=[
+            low(shards, shard_rows, width),
+            low(DEPTH, ACROSS, shard_rows, width),
+            wide(shard_rows, width),
+            low(rows, width),
+            low(rows, width),
+            low(rows, width),
+            low(rows, width),
+            low(rows, width),
+            low(rows, ff),
+            low(rows, ff),
+            low(rows, ff),
+            low(rows, 3 * width),
+            low(rows, 3 * width),
+            wide(rows // PAIR, heads // 2, 2 * PAIR, PAIR),
+            wide(rows, width),
+            wide(rows, width),
+            low(rows, width),
+            wide(rows, 2),
+            wide(rows, 2 * LANES),
+            wide(shards, attn_rows, width),
+            wide(shards, ff_rows, width),
+            low(shards, attn_rows, width),
+            low(shards, ff_rows, width),
+            wide(width, width),
+            wide(width, width),
+            wide(STATS, width),
+            wide(3, STATS, width),
+            wide(3, STATS, width),
+            wide(DEPTH, STATS, width),
+            dma(6),
+            dma(6),
+            dma(1),
+            dma(shards * SIDES),
+            dma(7),
+            dma(7),
+            dma(7),
+            *part_scratch(4 * attn_rows),
+            *part_scratch(3 * ff_rows),
+        ],
+        compiler_params=pltpu.CompilerParams(
+            vmem_limit_bytes=60 << 20, collective_id=0, has_side_effects=True
+        ),
+        name="whole",
+    )(
+        lengths,
+        attn_bias,
+        tokens,
+        cotangent,
+        variates,
+        times.reshape(rows // PAIR, PAIR),
+        jnp.asarray(rotary_table()),
+        gains,
+        *weights,
+        *momenta,
+    )
+
+
+def update_kernel(
+    pieces,
+    factors,
+    grow_ref,
+    xrow_ref,
+    stat_ref,
+    w_qkv,
+    w_out,
+    w_gate_up,
+    w_down,
+    m_qkv,
+    m_out,
+    m_gate_up,
+    m_down,
+    gains,
+    bias,
+    gain_moment,
+    gain_square,
+    bias_moment,
+    bias_square,
+    g_qkv,
+    g_out,
+    g_gate_up,
+    g_down,
+    nm_qkv,
+    nm_out,
+    nm_gate_up,
+    nm_down,
+    nw_qkv,
+    nw_out,
+    nw_gate_up,
+    nw_down,
+    g_gains,
+    n_gain_moment,
+    n_gain_square,
+    n_gains,
+    g_bias,
+    n_bias_moment,
+    n_bias_square,
+    n_bias,
+):
+    shrink = 1.0 - MUON_RATE * MUON_DECAY
+
+    def one(index, turned, g, m, w, nm, nw):
+        start, count = pieces[index]
+        grad = grow_ref[start : start + count, :].astype(WIDE)
+        ortho = xrow_ref[start : start + count, :].astype(WIDE)
+        if turned:
+            grad, ortho = grad.T, ortho.T
+        g[...] = grad
+        nm[...] = MUON_MU * m[...] + grad
+        nw[...] = w[...] * shrink - factors[index] * ortho
+
+    for j in range(3):
+        one(j, False, *[r.at[j] for r in (g_qkv, m_qkv, w_qkv, nm_qkv, nw_qkv)])
+    one(3, False, g_out, m_out, w_out, nm_out, nw_out)
+    for j in range(2):
+        refs = (g_gate_up, m_gate_up, w_gate_up, nm_gate_up, nw_gate_up)
+        one(4 + j, True, *[r.at[j] for r in refs])
+    one(6, False, g_down, m_down, w_down, nm_down, nw_down)
+
+    grad = stat_ref[0:2, :]
+    g_gains[...] = grad
+    n_gain_moment[...], n_gain_square[...], n_gains[...] = adam_step(
+        gains[...], grad, gain_moment[...], gain_square[...]
+    )
+    heads = bias.shape[1]
+    sums = jnp.sum(stat_ref[8:24, :PAIR].T, axis=0, keepdims=True)
+    grad = jnp.concatenate([sums[:, :heads], sums[:, 8 : 8 + heads]], axis=0)
+    g_bias[...] = grad
+    n_bias_moment[...], n_bias_square[...], n_bias[...] = adam_step(
+        bias[...], grad, bias_moment[...], bias_square[...]
+    )
+
+
+def update(factors, grad_rows, ortho_rows, stats, weights, momenta, small):
+    pieces = offsets(weights[1].shape[0], weights[3].shape[0])
+    gains, bias = small[:2]
+    like = lambda a: jax.ShapeDtypeStruct(a.shape, WIDE)
+    outs = [like(a) for a in (*weights, *weights, *weights, *[gains] * 4, *[bias] * 4)]
+    return pl.pallas_call(
+        functools.partial(update_kernel, pieces, factors),
+        out_shape=tuple(outs),
+        in_specs=[WHOLE] * 17,
+        out_specs=(WHOLE,) * len(outs),
+        compiler_params=pltpu.CompilerParams(vmem_limit_bytes=58 << 20),
+        name="update",
+    )(grad_rows, ortho_rows, stats, *weights, *momenta, *small)
 
 
 def body(
@@ -423,6 +1555,31 @@
     fsdp = lax.axis_size("fsdp")
     ff = ff_rows * fsdp
     attn_width = attn_rows * fsdp
+    shrink = 1.0 - MUON_RATE * MUON_DECAY
+    scale_attn = MUON_RATE * 0.2 * math.sqrt(max(width, attn_width))
+    scale_ff = MUON_RATE * 0.2 * math.sqrt(max(width, ff))
+    sizes = (fsdp, lax.axis_size("ns"))
+    if sizes == (DEPTH * ACROSS, SIDES * CORES) and attn_rows == 48 and ff_rows == 128:
+        turn = lambda a: jnp.swapaxes(a, 1, 2)
+        shards = (turn(weight_qkv), weight_out, weight_gate_up, weight_down)
+        momenta = (turn(momentum_qkv), momentum_out, momentum_gate_up, momentum_down)
+        out_tokens, grad_tokens, grad_rows, ortho_rows, stats = whole_step(
+            tokens, cotangent, lengths, variates, times, gains, attn_bias, shards, momenta
+        )
+        outs = list(
+            update(
+                (scale_attn,) * 4 + (scale_ff,) * 3,
+                grad_rows,
+                ortho_rows,
+                stats,
+                shards,
+                momenta,
+                (gains, attn_bias, gain_moment, gain_square, bias_moment, bias_square),
+            )
+        )
+        for i in (0, 4, 8):
+            outs[i] = turn(outs[i])
+        return (out_tokens, grad_tokens, *outs)
     weights = pack(weight_qkv, weight_out, weight_gate_up, weight_down)
     momenta = pack(momentum_qkv, momentum_out, momentum_gate_up, momentum_down)
     full = lax.all_gather(weights.astype(LOW), "fsdp", axis=0, tiled=False)
@@ -432,7 +1589,7 @@
         full = jnp.concatenate(
             [full[:, s : s + n].reshape(1, fsdp * n, width) for s, n in pieces], axis=1
         )
-    out_tokens, grad_tokens, grads, gain_rows, bias_rows = layer(
+    out_tokens, grad_tokens, grads, stats = layer(
         tokens, cotangent, lengths, variates, times, full, gains, attn_bias, ff, WIDE
     )
     if not aligned:
@@ -442,8 +1599,8 @@
         )
     summed = lax.psum_scatter(grads, "fsdp", scatter_dimension=0, tiled=False)
     grad_rows = lax.psum(summed.astype(LOW), "ns").astype(WIDE)
-    bias_part = jnp.sum(bias_rows, axis=1).reshape(2, 8)[:, :heads]
-    grad_gains, grad_bias = lax.psum((gain_rows, bias_part), ("fsdp", "ns"))
+    bias_part = jnp.sum(stats[8:, :PAIR], axis=1).reshape(2, 8)[:, :heads]
+    grad_gains, grad_bias = lax.psum((stats[:2], bias_part), ("fsdp", "ns"))
 
     new_momenta = MUON_MU * momenta + grad_rows
     advance = grad_rows + MUON_MU * new_momenta
@@ -461,9 +1618,6 @@
         ]
     )
     factor = newton_schulz(lax.psum(grams, "fsdp"))
-    shrink = 1.0 - MUON_RATE * MUON_DECAY
-    scale_attn = MUON_RATE * 0.2 * math.sqrt(max(width, attn_width))
-    scale_ff = MUON_RATE * 0.2 * math.sqrt(max(width, ff))
     turned = jnp.concatenate(
         [
             (scale_attn if i < 4 else scale_ff)

time: 650 us -> 131 us (0.20); the launches traced: 638 us -> 130 us
  waiting for transfers between devices: 323 us -> 0 us
  matrix products: 191 us -> 0 us
  Pallas kernels: 38.2 us -> 127 us
  blocking collectives: 44.6 us -> 0 us
  other arithmetic: 15.1 us -> 0 us
  between operations: 14.7 us -> 0.7 us
  local copies, waits for them, and re-layouts: 11.6 us -> 2.29 us
    dot_general x31 -> x0, matrix products: 191 us -> none  [the longest x17 177 us: product(): jnp.einsum('mde,mef->mdf', left, right, precision=lax.Precision.HIGHEST,...]
    psum x2 -> x0, waiting for transfers between devices: 134 us -> none  [the longest x1 102 us: body(): factor = newton_schulz(lax.psum(grams, 'fsdp'))]
    reduce_scatter x1 -> x0, waiting for transfers between devices: 129 us -> none  [body(): summed = lax.psum_scatter(grads, 'fsdp', scatter_dimension=0, tiled=False)]
    pallas_call x1 -> x2, Pallas kernels: 38.2 us -> 127 us  [the longest x1 124 us: whole_step(): pl.pallas_call(functools.partial(whole_kernel, pieces), out_shape=(jax.Sh...]
    all_gather x1 -> x0, waiting for transfers between devices: 60.3 us -> none  [body(): full = lax.all_gather(weights.astype(LOW), 'fsdp', axis=0, tiled=False)]
    psum x1 -> x0, blocking collectives: 44.6 us -> none  [body(): grad_gains, grad_bias = lax.psum((gain_rows, bias_part), ('fsdp', 'ns'))]
  transfers between devices with their start and end apart: 4 -> 0, of which waited for: 4 -> 0; matrix products, arithmetic and copies ran while one was open for 2% -> 0% of each run, Pallas kernels for 0% -> 0%
where the time goes in v4:
time: 131 us; the launch traced here: 130 us
  Pallas kernels  127 us (97%)
  local copies, waits for them, and re-layouts  2.29 us (2%)
    pallas_call x1, Pallas kernels, whole_step(): pl.pallas_call(functools.partial(whole_kernel, pieces), out_shape=(jax.Sh...  124 us
    pallas_call x1, Pallas kernels, update(): pl.pallas_call(functools.partial(update_kernel, pieces, factors), out_sha...  3.62 us

profile of v4, /device:TPU:15, one launch (start us, length us, event | category | flops | bytes accessed | tf_op | source)
XLA Modules:
  0.0 130.4 jit_solution(13112667423363398327)
XLA Ops:
  0.7 123.8 %whole.1 = (bf16[1024,384]{1,0:T(8,128)(2,1)}, bf16[1024,384]{1,0:T(8,128)(2,1)}, bf16[576,384]{1,0:T(8,128)(2,1)}, bf16[576,384]{1,0:T(8,128)(2,1)}, f32[24,384]{1,0:T(8,128)}) custom-call(s32[16]{0:T(128)} %lengths.1, f32[2,6]{1,0:T(2,128)} %bias.3, bf16[1024,384]{1,0:T(8,128)(2,1)} %tok_ref.1, bf16[1024,384]{1,0:T(8,128)(2,1)} %cot_ref.1, ...), custom_call_target="tpu_custom_call" | custom-call | tf_op jit(solution)/shard_map/whole/pallas_call | solution.py:1371
  124.5 0.0 copy-start.1
  124.5 3.6 %update.1 = (f32[3,48,384]{2,1,0:T(8,128)}, f32[48,384]{1,0:T(8,128)}, f32[2,384,128]{2,1,0:T(8,128)}, f32[128,384]{1,0:T(8,128)}, f32[3,48,384]{2,1,0:T(8,128)}...) custom-call(bf16[576,384]{1,0:T(8,128)(2,1)} %get-tuple-element.49.g, ...), custom_call_target="tpu_custom_call" | custom-call | tf_op jit(solution)/shard_map/update/pallas_call | solution.py:1520
  128.1 0.0 copy-done.1
  128.1 0.0 copy-start
  128.1 0.9 copy.44
  129.0 0.5 copy-done
  129.5 0.9 copy.45
Async XLA Ops:
  124.5 3.6 %copy-start.1 = (bf16[1024,384]{1,0:T(8,128)(2,1)S(1)}, bf16[1024,384]{1,0:T(8,128)(2,1)}, u32[]{:S(2)}) copy-start(bf16[1024,384]{1,0:T(8,128)(2,1)} %get-tuple-element.94) | copy-start | bytes 2359300
  128.1 1.4 %copy-start = (bf16[1024,384]{1,0:T(8,128)(2,1)S(1)}, bf16[1024,384]{1,0:T(8,128)(2,1)}, u32[]{:S(2)}) copy-start(bf16[1024,384]{1,0:T(8,128)(2,1)} %get-tuple-element.95) | copy-start | bytes 2359300

commit v5 on v4

--- a/solution.py
+++ b/solution.py
@@ -38,6 +38,7 @@
 STATS = 24
 WHOLE = pl.BlockSpec(memory_space=pltpu.VMEM)
 SCALARS = pl.BlockSpec(memory_space=pltpu.SMEM)
+ANYWHERE = pl.BlockSpec(memory_space=pl.ANY)
 
 
 def mul_nn(left, right):
@@ -443,6 +444,12 @@
     return high, (value - high.astype(WIDE)).astype(LOW)
 
 
+def square_wide(value):
+    high, low = halves(value)
+    cross = mul_nn(high, low)
+    return mul_nn(high, high) + (cross + cross.T)
+
+
 def mul_wide(left, right):
     columns = right.shape[1]
     left_high, left_low = halves(left)
@@ -461,8 +468,8 @@
     pieces,
     lengths,
     bias,
-    tok_ref,
-    cot_ref,
+    tok_hbm,
+    cot_hbm,
     var_ref,
     time_ref,
     table_ref,
@@ -471,15 +478,22 @@
     wout_ref,
     wgate_up_ref,
     wdown_ref,
-    mqkv_ref,
-    mout_ref,
-    mgate_up_ref,
-    mdown_ref,
+    mqkv_hbm,
+    mout_hbm,
+    mgate_up_hbm,
+    mdown_hbm,
     out_ref,
     gtok_ref,
     grows_ref,
     xrows_ref,
     total_ref,
+    tok_ref,
+    cot_ref,
+    mqkv_ref,
+    mout_ref,
+    mgate_up_ref,
+    mdown_ref,
+    load_sem,
     w_s,
     grad_s,
     momenta,
@@ -501,6 +515,8 @@
     rope_s,
     y_attn,
     y_ff,
+    g_attn,
+    g_ff,
     x_attn,
     x_ff,
     gram_s,
@@ -512,6 +528,7 @@
     stat_send,
     stat_recv,
     adv_recv,
+    mom_recv,
     x_send,
     x_recv,
     fan_send,
@@ -539,6 +556,21 @@
         return carry
 
     lax.fori_loop(0, world - 1, hello, 0)
+    loads = [
+        pltpu.make_async_copy(src, dst, load_sem.at[i])
+        for i, (src, dst) in enumerate(
+            (
+                (tok_hbm, tok_ref),
+                (cot_hbm, cot_ref),
+                (mqkv_hbm, mqkv_ref),
+                (mout_hbm, mout_ref),
+                (mgate_up_hbm, mgate_up_ref),
+                (mdown_hbm, mdown_ref),
+            )
+        )
+    ]
+    for one in loads:
+        one.start()
 
     def put(index, value):
         start, count = pieces[index]
@@ -690,8 +722,215 @@
     each = len(per_part) // 2
     gathers = [Gather(*spans[i], per_part[i * each : i * each + 8]) for i in range(2)]
     attn_gather, ff_gather = gathers
+    class Reduce:
+        def __init__(self, start, count, refs):
+            self.start_row, self.half, self.quarter = start, count // 2, count // 4
+            (
+                self.in_zero,
+                self.acc_zero,
+                self.in_one,
+                self.acc_one,
+                self.in_two,
+                self.acc_two,
+                self.in_three,
+                self.send_zero,
+                self.send_one,
+                self.send_two,
+                self.send_three,
+                self.recv_zero,
+                self.recv_one,
+                self.recv_two,
+                self.recv_three,
+                self.mom_send,
+                self.adv_send,
+                self.row_send,
+                self.row_recv,
+            ) = refs
+            self.keep_quarter = pl.ds(pl.multiple_of(y * self.quarter, 16), self.quarter)
+            self.give_quarter = pl.ds(pl.multiple_of((1 - y) * self.quarter, 16), self.quarter)
+            self.first_quarter = pl.ds(0, self.quarter)
+
+        def half_of(self, core):
+            return pl.ds(pl.multiple_of(self.start_row + core * self.half, 16), self.half)
+
+        def rows_of(self, quarter):
+            first = pl.multiple_of(self.start_row + quarter * self.quarter, 16)
+            return pl.ds(first, self.quarter)
+
+        def zero(self, k):
+            return remote(
+                grad_s.at[line[k], :, self.half_of(1 - c)],
+                self.in_zero.at[k],
+                self.send_zero.at[k],
+                self.recv_zero.at[k],
+                sibling,
+            )
+
+        def one(self, k, core):
+            if core == 0:
+                src, dst = self.acc_zero.at[k, :, self.give_quarter], self.in_one.at[
+                    k, :, self.first_quarter
+                ]
+            else:
+                src, dst = self.acc_zero.at[k, 1 - x], self.in_one.at[k, 0]
+            where = facing if core == 0 else beside
+            return remote(src, dst, self.send_one.at[k], self.recv_one.at[k], where)
+
+        def two(self, k, core):
+            if core == 0:
+                src = self.acc_one.at[k, 1 - x, self.first_quarter]
+            else:
+                src = self.acc_one.at[k, 0, self.give_quarter]
+            where = beside if core == 0 else facing
+            return remote(src, self.in_two.at[k], self.send_two.at[k], self.recv_two.at[k], where)
+
+        def three(self, k):
+            return remote(
+                self.acc_two.at[k],
+                self.in_three.at[k],
+                self.send_three.at[k],
+                self.recv_three.at[k],
+                device(line[k], x, y, c),
+            )
+
+        def start(self):
+            for k in TURNS:
+                self.zero(k).start()
+
+        def add(self, left, right):
+            return (left.astype(WIDE) + right.astype(WIDE)).astype(LOW)
+
+        def first(self):
+            for k in TURNS:
+                self.zero(k).wait_recv()
+                self.acc_zero[k] = self.add(grad_s[line[k], :, self.half_of(c)], self.in_zero[k])
+                for core in range(2):
+
+                    @pl.when(c == core)
+                    def _():
+                        self.one(k, core).start()
+
+        def second(self, t):
+            k, quarter = TURNS[t], self.quarter
+
+            @pl.when(c == 0)
+            def _():
+                self.one(k, 0).wait_recv()
+                self.acc_one[k, :, :quarter] = self.add(
+                    self.acc_zero[k, :, self.keep_quarter], self.in_one[k, :, :quarter]
+                )
+                self.two(k, 0).start()
+
+            @pl.when(c == 1)
+            def _():
+                self.one(k, 1).wait_recv()
+                self.acc_one[k, 0] = self.add(self.acc_zero[k, x], self.in_one[k, 0])
+                self.two(k, 1).start()
+
+        def third(self, t):
+            k, quarter = TURNS[t], self.quarter
+
+            @pl.when(c == 0)
+            def _():
+                self.two(k, 0).wait_recv()
+                self.acc_two[k] = self.add(self.acc_one[k, x, :quarter], self.in_two[k])
+
+            @pl.when(c == 1)
+            def _():
+                self.two(k, 1).wait_recv()
+                self.acc_two[k] = self.add(self.acc_one[k, 0, self.keep_quarter], self.in_two[k])
+
+            if k != 0:
+                self.three(k).start()
+
+        def segments(self, index):
+            found = []
+            begin = self.start_row + index * self.quarter
+            for m, (start, count) in enumerate(pieces):
+                first, last = max(start, begin), min(start + count, begin + self.quarter)
+                if first < last:
+                    found.append((m, first - begin, first - start, last - first))
+            return found
+
+        def to_owner(self, kind, index, i, stays=False):
+            m, first, to, count = self.segments(index)[i]
+            begin = self.start_row + index * self.quarter + first
+            source = (momenta, grows_ref)[kind].at[pl.ds(begin, count)]
+            target = stage(kind, m).at[shard, pl.ds(to, count)]
+            sent = (self.mom_send, self.adv_send)[kind].at[i]
+            got = (mom_recv, adv_recv)[kind].at[0]
+            if stays:
+                return pltpu.make_async_copy(source, target, got)
+            return remote(source, target, sent, got, device(*OWNERS[m]))
+
+        def all_to_owners(self, kind):
+            for index in range(4):
+                for i, (m, _, _, _) in enumerate(self.segments(index)):
+
+                    @pl.when((part == index) & jnp.logical_not(owned(m)))
+                    def _():
+                        self.to_owner(kind, index, i).start()
+
+                    @pl.when((part == index) & owned(m))
+                    def _():
+                        self.to_owner(kind, index, i, stays=True).start()
+
+        def send_momenta(self):
+            self.all_to_owners(0)
+
+        def row_copy(self, j, quarter, where):
+            here = grows_ref.at[self.rows_of(quarter)]
+            return remote(here, here, self.row_send.at[j], self.row_recv.at[j], where)
+
+        def finish(self):
+            total = self.acc_two[0].astype(WIDE)
+            for k in range(1, DEPTH):
+                self.three(k).wait_recv()
+                total = total + self.in_three[k].astype(WIDE)
+            grows_ref[self.rows_of(part), :] = total.astype(LOW)
+            self.all_to_owners(1)
+            for j, where in enumerate((sibling, facing, corner)):
+                self.row_copy(j, part, where).start()
+
+        def done(self):
+            mates = ((sibling, 0, 1), (facing, 1, 0), (corner, 1, 1))
+            for j, (where, dy, dc) in enumerate(mates):
+                self.row_copy(j, 2 * (c ^ dc) + (y ^ dy), where).wait_recv()
+                self.row_copy(j, part, where).wait_send()
+            for index in range(4):
+                for i, (m, _, _, _) in enumerate(self.segments(index)):
+
+                    @pl.when((part == index) & jnp.logical_not(owned(m)))
+                    def _():
+                        for kind in range(2):
+                            self.to_owner(kind, index, i).wait_send()
+
+            for k in TURNS:
+                self.zero(k).wait_send()
+                if k != 0:
+                    self.three(k).wait_send()
+                for core in range(2):
+
+                    @pl.when(c == core)
+                    def _():
+                        self.one(k, core).wait_send()
+                        self.two(k, core).wait_send()
+
+    def owned(m):
+        oz, ox, oy, oc = OWNERS[m]
+        return (z == oz) & (x == ox) & (y == oy) & (c == oc)
+
+    def stage(kind, m):
+        return ((y_attn, y_ff), (g_attn, g_ff))[kind][int(m >= 4)]
+
+    reduces = [Reduce(*spans[i], per_part[i * each + 8 : (i + 1) * each]) for i in range(2)]
+    attn_reduce, ff_reduce = reduces
+
     attn_gather.start()
-
+    ff_gather.start()
+
+    for one in loads:
+        one.wait()
     for i, (value, turned) in enumerate(((mgate_up_ref[0], 4), (mgate_up_ref[1], 5))):
         start, count = pieces[turned]
         momenta[start : start + count, :] = value.T
@@ -743,7 +982,8 @@
 
     for d in range(1, DEPTH):
         attn_gather.hop(d)
-    ff_gather.start()
+        if d < DEPTH - 1:
+            ff_gather.hop(d)
     for d in range(DEPTH):
         attn_gather.from_beside(d)
     attn_gather.arrive()
@@ -819,18 +1059,24 @@
         scale = lax.rsqrt(jnp.mean(mid * mid, axis=-1, keepdims=True) + EPS_NORM)
         scale_s[here, 1:2] = scale
         n2_s[here, :] = (mid * scale * gain_two).astype(LOW)
-        for d in range(1, DEPTH):
+        @pl.when(i == 0)
+        def _():
+            ff_gather.hop(DEPTH - 1)
+            ff_gather.from_beside(0)
+            ff_gather.from_beside(1)
+
+        for d in range(2, DEPTH):
 
             @pl.when(i == d - 1)
             def _():
-                ff_gather.hop(d)
+                ff_gather.from_beside(d)
 
         return carry
 
     lax.fori_loop(0, rows // BLOCK, attend, 0)
-    for d in range(DEPTH):
-        ff_gather.from_beside(d)
     ff_gather.arrive()
+    for one in reduces:
+        one.send_momenta()
 
     def feed(i, carry):
         here = block_of(i, BLOCK)
@@ -868,211 +1114,6 @@
         grad_s[:, :, start : start + count, :] = (
             mul_tn(left, right).reshape(DEPTH, ACROSS, count, width).astype(LOW)
         )
-
-    class Reduce:
-        def __init__(self, start, count, refs):
-            self.start_row, self.half, self.quarter = start, count // 2, count // 4
-            (
-                self.in_zero,
-                self.acc_zero,
-                self.in_one,
-                self.acc_one,
-                self.in_two,
-                self.acc_two,
-                self.in_three,
-                self.advance,
-                self.send_zero,
-                self.send_one,
-                self.send_two,
-                self.send_three,
-                self.recv_zero,
-                self.recv_one,
-                self.recv_two,
-                self.recv_three,
-                self.adv_send,
-                self.row_send,
-                self.row_recv,
-            ) = refs
-            self.keep_quarter = pl.ds(pl.multiple_of(y * self.quarter, 16), self.quarter)
-            self.give_quarter = pl.ds(pl.multiple_of((1 - y) * self.quarter, 16), self.quarter)
-            self.first_quarter = pl.ds(0, self.quarter)
-
-        def half_of(self, core):
-            return pl.ds(pl.multiple_of(self.start_row + core * self.half, 16), self.half)
-
-        def rows_of(self, quarter):
-            first = pl.multiple_of(self.start_row + quarter * self.quarter, 16)
-            return pl.ds(first, self.quarter)
-
-        def zero(self, k):
-            return remote(
-                grad_s.at[line[k], :, self.half_of(1 - c)],
-                self.in_zero.at[k],
-                self.send_zero.at[k],
-                self.recv_zero.at[k],
-                sibling,
-            )
-
-        def one(self, k, core):
-            if core == 0:
-                src, dst = self.acc_zero.at[k, :, self.give_quarter], self.in_one.at[
-                    k, :, self.first_quarter
-                ]
-            else:
-                src, dst = self.acc_zero.at[k, 1 - x], self.in_one.at[k, 0]
-            where = facing if core == 0 else beside
-            return remote(src, dst, self.send_one.at[k], self.recv_one.at[k], where)
-
-        def two(self, k, core):
-            if core == 0:
-                src = self.acc_one.at[k, 1 - x, self.first_quarter]
-            else:
-                src = self.acc_one.at[k, 0, self.give_quarter]
-            where = beside if core == 0 else facing
-            return remote(src, self.in_two.at[k], self.send_two.at[k], self.recv_two.at[k], where)
-
-        def three(self, k):
-            return remote(
-                self.acc_two.at[k],
-                self.in_three.at[k],
-                self.send_three.at[k],
-                self.recv_three.at[k],
-                device(line[k], x, y, c),
-            )
-
-        def start(self):
-            for k in TURNS:
-                self.zero(k).start()
-
-        def step(self, t):
-            def add(left, right):
-                return (left.astype(WIDE) + right.astype(WIDE)).astype(LOW)
-
-            quarter = self.quarter
-            if t < DEPTH:
-                k = TURNS[t]
-                self.zero(k).wait_recv()
-                self.acc_zero[k] = add(grad_s[line[k], :, self.half_of(c)], self.in_zero[k])
-                for core in range(2):
-
-                    @pl.when(c == core)
-                    def _():
-                        self.one(k, core).start()
-
-            if 1 <= t <= DEPTH:
-                k = TURNS[t - 1]
-
-                @pl.when(c == 0)
-                def _():
-                    self.one(k, 0).wait_recv()
-                    self.acc_one[k, :, :quarter] = add(
-                        self.acc_zero[k, :, self.keep_quarter], self.in_one[k, :, :quarter]
-                    )
-                    self.two(k, 0).start()
-
-                @pl.when(c == 1)
-                def _():
-                    self.one(k, 1).wait_recv()
-                    self.acc_one[k, 0] = add(self.acc_zero[k, x], self.in_one[k, 0])
-                    self.two(k, 1).start()
-
-            if 2 <= t:
-                k = TURNS[t - 2]
-
-                @pl.when(c == 0)
-                def _():
-                    self.two(k, 0).wait_recv()
-                    self.acc_two[k] = add(self.acc_one[k, x, :quarter], self.in_two[k])
-
-                @pl.when(c == 1)
-                def _():
-                    self.two(k, 1).wait_recv()
-                    self.acc_two[k] = add(self.acc_one[k, 0, self.keep_quarter], self.in_two[k])
-
-                if k != 0:
-                    self.three(k).start()
-
-        def segments(self, index):
-            found = []
-            begin = self.start_row + index * self.quarter
-            for m, (start, count) in enumerate(pieces):
-                first, last = max(start, begin), min(start + count, begin + self.quarter)
-                if first < last:
-                    found.append((m, first - begin, first - start, last - first))
-            return found
-
-        def adv_copy(self, index, i):
-            m, first, to, count = self.segments(index)[i]
-            return remote(
-                self.advance.at[pl.ds(first, count)],
-                stage(m).at[shard, pl.ds(to, count)],
-                self.adv_send.at[i],
-                adv_recv.at[0],
-                device(*OWNERS[m]),
-            )
-
-        def row_copy(self, j, quarter, where):
-            here = grows_ref.at[self.rows_of(quarter)]
-            return remote(here, here, self.row_send.at[j], self.row_recv.at[j], where)
-
-        def finish(self):
-            total = self.acc_two[0].astype(WIDE)
-            for k in range(1, DEPTH):
-                self.three(k).wait_recv()
-                total = total + self.in_three[k].astype(WIDE)
-            old = momenta[self.rows_of(part), :]
-            self.advance[...] = total + MUON_MU * (MUON_MU * old + total)
-            for index in range(4):
-                for i, (m, first, to, count) in enumerate(self.segments(index)):
-
-                    @pl.when((part == index) & jnp.logical_not(owned(m)))
-                    def _():
-                        self.adv_copy(index, i).start()
-
-                    @pl.when((part == index) & owned(m))
-                    def _():
-                        pltpu.make_async_copy(
-                            self.advance.at[pl.ds(first, count)],
-                            stage(m).at[shard, pl.ds(to, count)],
-                            adv_recv.at[0],
-                        ).start()
-
-            grows_ref[self.rows_of(part), :] = total.astype(LOW)
-            for j, where in enumerate((sibling, facing, corner)):
-                self.row_copy(j, part, where).start()
-
-        def done(self):
-            mates = ((sibling, 0, 1), (facing, 1, 0), (corner, 1, 1))
-            for j, (where, dy, dc) in enumerate(mates):
-                self.row_copy(j, 2 * (c ^ dc) + (y ^ dy), where).wait_recv()
-                self.row_copy(j, part, where).wait_send()
-            for index in range(4):
-                for i, (m, first, to, count) in enumerate(self.segments(index)):
-
-                    @pl.when((part == index) & jnp.logical_not(owned(m)))
-                    def _():
-                        self.adv_copy(index, i).wait_send()
-
-            for k in TURNS:
-                self.zero(k).wait_send()
-                if k != 0:
-                    self.three(k).wait_send()
-                for core in range(2):
-
-                    @pl.when(c == core)
-                    def _():
-                        self.one(k, core).wait_send()
-                        self.two(k, core).wait_send()
-
-    def owned(m):
-        oz, ox, oy, oc = OWNERS[m]
-        return (z == oz) & (x == ox) & (y == oy) & (c == oc)
-
-    def stage(m):
-        return y_attn if m < 4 else y_ff
-
-    reduces = [Reduce(*spans[i], per_part[i * each + 8 : (i + 1) * each]) for i in range(2)]
-    attn_reduce, ff_reduce = reduces
 
     grad_put(4, gg_s[...], n2_s[...])
     grad_put(5, gu_s[...], n2_s[...])
@@ -1116,11 +1157,19 @@
                 dk * cosine - swapped(dk) * sine
             ).astype(LOW)
             gqkv_s[here, 2 * width + first : 2 * width + first + LANES] = dv.astype(LOW)
-        for t in range(DEPTH + 2):
-
-            @pl.when(i == t)
+        @pl.when(i == 0)
+        def _():
+            ff_reduce.first()
+
+        for t in range(DEPTH):
+
+            @pl.when(i == t + 2)
             def _():
-                ff_reduce.step(t)
+                ff_reduce.second(t)
+
+            @pl.when(i == t + 4)
+            def _():
+                ff_reduce.third(t)
 
         return carry
 
@@ -1129,7 +1178,6 @@
         grad_put(j, gqkv_s[:, j * width : (j + 1) * width], n1_s[...])
     grad_put(3, att_s[...], gml_s[...])
     attn_reduce.start()
-    ff_reduce.finish()
 
     def last(i):
         here = block_of(i, 2 * BLOCK)
@@ -1150,20 +1198,21 @@
     def stat_copy(step, src, where):
         return remote(src, stat_in.at[step], stat_send.at[step], stat_recv.at[step], where)
 
-    attn_reduce.step(0)
+    attn_reduce.first()
     last(0)
-    attn_reduce.step(1)
+    ff_reduce.finish()
     last(1)
     stat_copy(0, stat_s, sibling).start()
-    attn_reduce.step(2)
-    outgoing(0)
+    attn_reduce.second(0)
+    attn_reduce.second(1)
+    attn_reduce.second(2)
+    attn_reduce.third(0)
+    attn_reduce.second(3)
     stat_copy(0, stat_s, sibling).wait()
     stat_acc[0] = stat_s[...] + stat_in[0]
     stat_copy(1, stat_acc.at[0], facing).start()
-    attn_reduce.step(3)
-    outgoing(1)
-    attn_reduce.step(4)
-    attn_reduce.step(5)
+    for t in range(1, DEPTH):
+        attn_reduce.third(t)
     stat_copy(1, stat_acc.at[0], facing).wait()
     stat_acc[1] = stat_acc[0] + stat_in[1]
     stat_copy(2, stat_acc.at[1], beside).start()
@@ -1186,58 +1235,6 @@
 
     attn_owner = functools.reduce(jnp.logical_or, [owned(m) for m in range(4)])
     ff_owner = functools.reduce(jnp.logical_or, [owned(m) for m in range(4, 7)])
-
-    def arrived(buffer):
-        pltpu.make_async_copy(buffer, buffer, adv_recv.at[0]).wait()
-
-    @pl.when(attn_owner)
-    def _():
-        arrived(y_attn)
-        gram_s[...] = gram_wide(y_attn[...].reshape(-1, width))
-
-    @pl.when(ff_owner)
-    def _():
-        arrived(y_ff)
-        gram_s[...] = gram_wide(y_ff[...].reshape(-1, width))
-
-    @pl.when(attn_owner | ff_owner)
-    def _():
-        unit = lax.broadcasted_iota(jnp.int32, (width, width), 0) == lax.broadcasted_iota(
-            jnp.int32, (width, width), 1
-        )
-        gram_mat = gram_s[...]
-        trace = jnp.sum(jnp.where(unit, gram_mat, 0.0), keepdims=True)
-        inverse = 1.0 / (jnp.sqrt(trace) + NS_EPS)
-        diagonal = jnp.where(unit, COEF_A, 0.0)
-        gram_mat = gram_mat * (inverse * inverse)
-
-        def poly(value):
-            return diagonal + COEF_B * value + COEF_C * mul_wide(value, value)
-
-        step_mat = poly(gram_mat)
-        gram_s[...] = mul_wide(mul_wide(gram_mat, step_mat), step_mat)
-        chain_s[...] = step_mat * inverse
-
-        def turn(i, carry):
-            now = gram_s[...]
-            step_now = poly(now)
-            both = mul_wide(jnp.concatenate([now, chain_s[...]], axis=0), step_now)
-            chain_s[...] = both[width:]
-            gram_s[...] = mul_wide(both[:width], step_now)
-            return carry
-
-        lax.fori_loop(0, NS_ITERS - 2, turn, 0)
-        chain_s[...] = mul_wide(chain_s[...], poly(gram_s[...]))
-
-    @pl.when(attn_owner)
-    def _():
-        value = y_attn[...].reshape(-1, width)
-        x_attn[...] = mul_wide(value, chain_s[...]).astype(LOW).reshape(x_attn.shape)
-
-    @pl.when(ff_owner)
-    def _():
-        value = y_ff[...].reshape(-1, width)
-        x_ff[...] = mul_wide(value, chain_s[...]).astype(LOW).reshape(x_ff.shape)
 
     chips = DEPTH * ACROSS * SIDES
 
@@ -1254,20 +1251,103 @@
         )
 
     mine = shard * SIDES + y
-    for m in range(7):
+    unit_mat = lax.broadcasted_iota(jnp.int32, (width, width), 0) == lax.broadcasted_iota(
+        jnp.int32, (width, width), 1
+    )
+    diagonal = jnp.where(unit_mat, COEF_A, 0.0)
+
+    def advance(y_buf, g_buf):
+        pltpu.make_async_copy(y_buf, y_buf, mom_recv.at[0]).wait()
+        pltpu.make_async_copy(g_buf, g_buf, adv_recv.at[0]).wait()
+        grad = g_buf[...].astype(WIDE)
+        return grad + MUON_MU * (MUON_MU * y_buf[...] + grad)
+
+    def poly(value):
+        return diagonal + COEF_B * value + COEF_C * square_wide(value)
+
+    def send_x(m, first, count):
+        def send(i, carry):
+            @pl.when(i != mine)
+            def _():
+                x_copy(m, i).start()
+
+            return carry
+
+        lax.fori_loop(first, first + count, send, 0)
+
+    def keep_x(m):
         start, count = pieces[m]
         source = x_attn if m < 4 else x_ff
-
-        @pl.when(owned(m))
-        def _():
-            def send(i, carry):
-                x_copy(m, lax.rem(mine + i, chips)).start()
-                return carry
-
-            lax.fori_loop(1, chips, send, 0)
-            pltpu.make_async_copy(
-                source.at[shard], xrows_ref.at[pl.ds(start, count)], x_recv.at[m]
-            ).start()
+        pltpu.make_async_copy(
+            source.at[shard], xrows_ref.at[pl.ds(start, count)], x_recv.at[m]
+        ).start()
+
+    @pl.when(attn_owner)
+    def _():
+        value = advance(y_attn, g_attn).reshape(-1, width)
+        total = jnp.sum(jnp.sum(value * value, axis=0, keepdims=True), axis=1, keepdims=True)
+        chain_s[...] = value * (1.0 / (jnp.sqrt(total) + NS_EPS))
+
+        def turn(i, carry):
+            now = chain_s[...]
+            chain_s[...] = mul_wide(now, poly(gram_wide(now)))
+            return carry
+
+        lax.fori_loop(0, NS_ITERS, turn, 0)
+        x_attn[...] = chain_s[...].astype(LOW).reshape(x_attn.shape)
+        for m in range(4):
+
+            @pl.when(owned(m))
+            def _():
+                send_x(m, 0, chips)
+                keep_x(m)
+
+    @pl.when(ff_owner)
+    def _():
+        y_ff[...] = advance(y_ff, g_ff)
+        gram_mat = gram_wide(y_ff[...].reshape(-1, width))
+        trace = jnp.sum(jnp.where(unit_mat, gram_mat, 0.0), keepdims=True)
+        inverse = 1.0 / (jnp.sqrt(trace) + NS_EPS)
+        gram_mat = gram_mat * (inverse * inverse)
+        step_mat = poly(gram_mat)
+        gram_s[...] = mul_wide(mul_wide(gram_mat, step_mat), step_mat)
+        chain_s[...] = step_mat * inverse
+
+        def turn(i, carry):
+            now = gram_s[...]
+            step_now = poly(now)
+            both = mul_wide(jnp.concatenate([now, chain_s[...]], axis=0), step_now)
+            chain_s[...] = both[width:]
+            gram_s[...] = mul_wide(both[:width], step_now)
+            return carry
+
+        lax.fori_loop(0, NS_ITERS - 2, turn, 0)
+        chain_s[...] = mul_wide(chain_s[...], poly(gram_s[...]))
+
+        def give(i, carry):
+            at = lax.rem(z + 2 + i, DEPTH)
+            these = pl.ds(at * ACROSS, ACROSS)
+            value = y_ff[these].reshape(-1, width)
+            x_ff[these] = mul_wide(value, chain_s[...]).astype(LOW).reshape(
+                ACROSS, x_ff.shape[1], width
+            )
+            for m in range(4, 7):
+
+                @pl.when(owned(m))
+                def _():
+                    send_x(m, at * (ACROSS * SIDES), ACROSS * SIDES)
+
+            return carry
+
+        lax.fori_loop(0, DEPTH, give, 0)
+        for m in range(4, 7):
+
+            @pl.when(owned(m))
+            def _():
+                keep_x(m)
+
+    outgoing(0)
+    outgoing(1)
 
     for j in range(1, DEPTH):
         remote(
@@ -1361,8 +1441,8 @@
             low(DEPTH, quarter, width),
             low(DEPTH, quarter, width),
             low(DEPTH, quarter, width),
-            wide(quarter, width),
             *[dma(DEPTH) for _ in range(8)],
+            dma(3),
             dma(3),
             dma(3),
             dma(3),
@@ -1377,9 +1457,13 @@
             jax.ShapeDtypeStruct((shard_rows, width), LOW),
             jax.ShapeDtypeStruct((STATS, width), WIDE),
         ),
-        in_specs=[SCALARS] * 2 + [WHOLE] * 14,
+        in_specs=[SCALARS] * 2 + [ANYWHERE] * 2 + [WHOLE] * 8 + [ANYWHERE] * 4,
         out_specs=(WHOLE,) * 5,
         scratch_shapes=[
+            low(rows, width),
+            low(rows, width),
+            *[wide(*m.shape) for m in momenta],
+            dma(6),
             low(shards, shard_rows, width),
             low(DEPTH, ACROSS, shard_rows, width),
             wide(shard_rows, width),
@@ -1403,6 +1487,8 @@
             wide(shards, ff_rows, width),
             low(shards, attn_rows, width),
             low(shards, ff_rows, width),
+            low(shards, attn_rows, width),
+            low(shards, ff_rows, width),
             wide(width, width),
             wide(width, width),
             wide(STATS, width),
@@ -1411,6 +1497,7 @@
             wide(DEPTH, STATS, width),
             dma(6),
             dma(6),
+            dma(1),
             dma(1),
             dma(shards * SIDES),
             dma(7),
@@ -1457,6 +1544,8 @@
     gain_square,
     bias_moment,
     bias_square,
+    out_in,
+    gtok_in,
     g_qkv,
     g_out,
     g_gate_up,
@@ -1477,7 +1566,16 @@
     n_bias_moment,
     n_bias_square,
     n_bias,
+    out_tokens,
+    grad_tokens,
+    sems,
 ):
+    copies = (
+        pltpu.make_async_copy(out_in, out_tokens, sems.at[0]),
+        pltpu.make_async_copy(gtok_in, grad_tokens, sems.at[1]),
+    )
+    for one_copy in copies:
+        one_copy.start()
     shrink = 1.0 - MUON_RATE * MUON_DECAY
 
     def one(index, turned, g, m, w, nm, nw):
@@ -1510,21 +1608,24 @@
     n_bias_moment[...], n_bias_square[...], n_bias[...] = adam_step(
         bias[...], grad, bias_moment[...], bias_square[...]
     )
-
-
-def update(factors, grad_rows, ortho_rows, stats, weights, momenta, small):
+    for one_copy in copies:
+        one_copy.wait()
+
+
+def update(factors, grad_rows, ortho_rows, stats, weights, momenta, small, rows):
     pieces = offsets(weights[1].shape[0], weights[3].shape[0])
     gains, bias = small[:2]
     like = lambda a: jax.ShapeDtypeStruct(a.shape, WIDE)
     outs = [like(a) for a in (*weights, *weights, *weights, *[gains] * 4, *[bias] * 4)]
     return pl.pallas_call(
         functools.partial(update_kernel, pieces, factors),
-        out_shape=tuple(outs),
-        in_specs=[WHOLE] * 17,
-        out_specs=(WHOLE,) * len(outs),
+        out_shape=(*outs, *[jax.ShapeDtypeStruct(r.shape, r.dtype) for r in rows]),
+        in_specs=[WHOLE] * 19,
+        out_specs=(*[WHOLE] * len(outs), *[ANYWHERE] * 2),
+        scratch_shapes=[pltpu.SemaphoreType.DMA((2,))],
         compiler_params=pltpu.CompilerParams(vmem_limit_bytes=58 << 20),
         name="update",
-    )(grad_rows, ortho_rows, stats, *weights, *momenta, *small)
+    )(grad_rows, ortho_rows, stats, *weights, *momenta, *small, *rows)
 
 
 def body(
@@ -1575,8 +1676,11 @@
                 shards,
                 momenta,
                 (gains, attn_bias, gain_moment, gain_square, bias_moment, bias_square),
+                (out_tokens, grad_tokens),
             )
         )
+        out_tokens, grad_tokens = outs[-2:]
+        outs = outs[:-2]
         for i in (0, 4, 8):
             outs[i] = turn(outs[i])
         return (out_tokens, grad_tokens, *outs)

time: 131 us -> 113 us (0.86)
  Pallas kernels: 127 us -> 112 us
  local copies, waits for them, and re-layouts: 2.29 us -> 0 us
    pallas_call x1, Pallas kernels: 124 us -> 107 us  [whole_step(): pl.pallas_call(functools.partial(whole_kernel, pieces), out_shape=(jax.Sh...]
    unnamed x6 -> x0, local copies, waits for them, and re-layouts: 2.29 us -> none
    pallas_call x1, Pallas kernels: 3.62 us -> 5.07 us  [update(): pl.pallas_call(functools.partial(update_kernel, pieces, factors), out_sha...]
where the time goes in v5:
time: 113 us
  Pallas kernels  112 us (99%)
    pallas_call x1, Pallas kernels, whole_step(): pl.pallas_call(functools.partial(whole_kernel, pieces), out_shape=(jax.Sh...  107 us
    pallas_call x1, Pallas kernels, update(): pl.pallas_call(functools.partial(update_kernel, pieces, factors), out_sha...  5.07 us

profile of v5, /device:TPU:15, one launch (start us, length us, event | category | flops | bytes accessed | tf_op | source)
XLA Modules:
  0.0 112.5 jit_solution(11916083978571941325)
XLA Ops:
  0.7 106.6 %whole.1 = (bf16[1024,384]{1,0:T(8,128)(2,1)}, bf16[1024,384]{1,0:T(8,128)(2,1)}, bf16[576,384]{1,0:T(8,128)(2,1)}, bf16[576,384]{1,0:T(8,128)(2,1)}, f32[24,384]{1,0:T(8,128)}) custom-call(s32[16]{0:T(128)} %lengths.1, f32[2,6]{1,0:T(2,128)} %bias.3, bf16[1024,384]{1,0:T(8,128)(2,1)} %tok_hbm.1, bf16[1024,384]{1,0:T(8,128)(2,1)} %cot_hbm.1, ...), custom_call_target="tpu_custom_call" | custom-call | tf_op jit(solution)/shard_map/whole/pallas_call | solution.py:1451
  107.3 5.1 %update.1 = (f32[3,48,384]{2,1,0:T(8,128)}, f32[48,384]{1,0:T(8,128)}, f32[2,384,128]{2,1,0:T(8,128)}, f32[128,384]{1,0:T(8,128)}, f32[3,48,384]{2,1,0:T(8,128)}...) custom-call(bf16[576,384]{1,0:T(8,128)(2,1)} %get-tuple-element.49.g, ...), custom_call_target="tpu_custom_call" | custom-call | tf_op jit(solution)/shard_map/update/pallas_call | solution.py:1620

commit v6 on v5

--- a/solution.py
+++ b/solution.py
@@ -397,7 +397,6 @@
 
 DEPTH, ACROSS = 4, 2
 SIDES, CORES = 2, 2
-TURNS = (2, 1, 3, 0)
 OWNERS = (
     (2, 0, 0, 0),
     (2, 1, 0, 1),
@@ -548,6 +547,12 @@
     world = DEPTH * ACROSS * SIDES * CORES
     rank = shard * (SIDES * CORES) + y * CORES + c
     line = [lax.rem(z + k, DEPTH) for k in range(DEPTH)]
+
+    def far_first(t):
+        low_z = jnp.minimum(z, DEPTH - 1 - z)
+        turn = DEPTH - 1 - t
+        turn = low_z if turn == 0 else jnp.where(turn - 1 < low_z, turn - 1, turn)
+        return jnp.where(z == low_z, turn, DEPTH - 1 - turn)
     part = 2 * c + y
 
     def hello(i, carry):
@@ -724,6 +729,7 @@
     attn_gather, ff_gather = gathers
     class Reduce:
         def __init__(self, start, count, refs):
+            self.order, self.own = far_first, DEPTH - 1
             self.start_row, self.half, self.quarter = start, count // 2, count // 4
             (
                 self.in_zero,
@@ -757,14 +763,17 @@
             first = pl.multiple_of(self.start_row + quarter * self.quarter, 16)
             return pl.ds(first, self.quarter)
 
-        def zero(self, k):
+        def zero(self, t):
             return remote(
-                grad_s.at[line[k], :, self.half_of(1 - c)],
-                self.in_zero.at[k],
-                self.send_zero.at[k],
-                self.recv_zero.at[k],
+                grad_s.at[self.order(t), :, self.half_of(1 - c)],
+                self.in_zero.at[t],
+                self.send_zero.at[t],
+                self.recv_zero.at[t],
                 sibling,
             )
+
+        def crosses(self, t, way):
+            return (c + t) % 2 == way
 
         def one(self, k, core):
             if core == 0:
@@ -784,64 +793,65 @@
             where = beside if core == 0 else facing
             return remote(src, self.in_two.at[k], self.send_two.at[k], self.recv_two.at[k], where)
 
-        def three(self, k):
+        def three(self, t):
             return remote(
-                self.acc_two.at[k],
-                self.in_three.at[k],
-                self.send_three.at[k],
-                self.recv_three.at[k],
-                device(line[k], x, y, c),
+                self.acc_two.at[t],
+                self.in_three.at[z],
+                self.send_three.at[t],
+                self.recv_three.at[z],
+                device(self.order(t), x, y, c),
             )
-
-        def start(self):
-            for k in TURNS:
-                self.zero(k).start()
 
         def add(self, left, right):
             return (left.astype(WIDE) + right.astype(WIDE)).astype(LOW)
 
-        def first(self):
-            for k in TURNS:
-                self.zero(k).wait_recv()
-                self.acc_zero[k] = self.add(grad_s[line[k], :, self.half_of(c)], self.in_zero[k])
-                for core in range(2):
-
-                    @pl.when(c == core)
-                    def _():
-                        self.one(k, core).start()
+        def start(self):
+            for t in range(DEPTH):
+                self.zero(t).start()
+
+        def first(self, t):
+            self.zero(t).wait_recv()
+            kept = grad_s[self.order(t), :, self.half_of(c)]
+            self.acc_zero[t] = self.add(kept, self.in_zero[t])
+            for core in range(2):
+
+                @pl.when(self.crosses(t, core))
+                def _():
+                    self.one(t, core).start()
 
         def second(self, t):
-            k, quarter = TURNS[t], self.quarter
-
-            @pl.when(c == 0)
+            quarter = self.quarter
+
+            @pl.when(self.crosses(t, 0))
             def _():
-                self.one(k, 0).wait_recv()
-                self.acc_one[k, :, :quarter] = self.add(
-                    self.acc_zero[k, :, self.keep_quarter], self.in_one[k, :, :quarter]
+                self.one(t, 0).wait_recv()
+                self.acc_one[t, :, :quarter] = self.add(
+                    self.acc_zero[t, :, self.keep_quarter], self.in_one[t, :, :quarter]
                 )
-                self.two(k, 0).start()
-
-            @pl.when(c == 1)
+                self.two(t, 0).start()
+
+            @pl.when(self.crosses(t, 1))
             def _():
-                self.one(k, 1).wait_recv()
-                self.acc_one[k, 0] = self.add(self.acc_zero[k, x], self.in_one[k, 0])
-                self.two(k, 1).start()
+                self.one(t, 1).wait_recv()
+                self.acc_one[t, 0] = self.add(self.acc_zero[t, x], self.in_one[t, 0])
+                self.two(t, 1).start()
 
         def third(self, t):
-            k, quarter = TURNS[t], self.quarter
-
-            @pl.when(c == 0)
+            quarter = self.quarter
+
+            @pl.when(self.crosses(t, 0))
             def _():
-                self.two(k, 0).wait_recv()
-                self.acc_two[k] = self.add(self.acc_one[k, x, :quarter], self.in_two[k])
-
-            @pl.when(c == 1)
+                self.two(t, 0).wait_recv()
+                self.acc_two[t] = self.add(self.acc_one[t, x, :quarter], self.in_two[t])
+
+            @pl.when(self.crosses(t, 1))
             def _():
-                self.two(k, 1).wait_recv()
-                self.acc_two[k] = self.add(self.acc_one[k, 0, self.keep_quarter], self.in_two[k])
-
-            if k != 0:
-                self.three(k).start()
+                self.two(t, 1).wait_recv()
+                self.acc_two[t] = self.add(self.acc_one[t, 0, self.keep_quarter], self.in_two[t])
+
+            @pl.when(self.order(t) != z)
+            def _():
+                self.three(t).start()
 
         def segments(self, index):
             found = []
@@ -883,10 +893,13 @@
             return remote(here, here, self.row_send.at[j], self.row_recv.at[j], where)
 
         def finish(self):
-            total = self.acc_two[0].astype(WIDE)
-            for k in range(1, DEPTH):
-                self.three(k).wait_recv()
-                total = total + self.in_three[k].astype(WIDE)
+            total = self.acc_two[self.own].astype(WIDE)
+            for j in range(1, DEPTH):
+                there = self.in_three.at[line[j]]
+                remote(
+                    there, there, self.send_three.at[0], self.recv_three.at[line[j]], sibling
+                ).wait_recv()
+                total = total + self.in_three[line[j]].astype(WIDE)
             grows_ref[self.rows_of(part), :] = total.astype(LOW)
             self.all_to_owners(1)
             for j, where in enumerate((sibling, facing, corner)):
@@ -905,16 +918,19 @@
                         for kind in range(2):
                             self.to_owner(kind, index, i).wait_send()
 
-            for k in TURNS:
-                self.zero(k).wait_send()
-                if k != 0:
-                    self.three(k).wait_send()
+            for t in range(DEPTH):
+                self.zero(t).wait_send()
+
+                @pl.when(self.order(t) != z)
+                def _():
+                    self.three(t).wait_send()
+
                 for core in range(2):
 
-                    @pl.when(c == core)
+                    @pl.when(self.crosses(t, core))
                     def _():
-                        self.one(k, core).wait_send()
-                        self.two(k, core).wait_send()
+                        self.one(t, core).wait_send()
+                        self.two(t, core).wait_send()
 
     def owned(m):
         oz, ox, oy, oc = OWNERS[m]
@@ -1119,6 +1135,7 @@
     grad_put(5, gu_s[...], n2_s[...])
     grad_put(6, hid_s[...], glow_s[...])
     ff_reduce.start()
+    grad_put(3, att_s[...], gml_s[...])
 
     def attend_back(i, carry):
         here = block_of(i, PAIR)
@@ -1159,25 +1176,29 @@
             gqkv_s[here, 2 * width + first : 2 * width + first + LANES] = dv.astype(LOW)
         @pl.when(i == 0)
         def _():
-            ff_reduce.first()
-
-        for t in range(DEPTH):
-
-            @pl.when(i == t + 2)
-            def _():
-                ff_reduce.second(t)
-
-            @pl.when(i == t + 4)
-            def _():
-                ff_reduce.third(t)
+            for t in range(DEPTH):
+                ff_reduce.first(t)
+
+        @pl.when(i == 4)
+        def _():
+            ff_reduce.second(0)
+            ff_reduce.second(1)
+
+        @pl.when(i == 6)
+        def _():
+            ff_reduce.third(0)
+            ff_reduce.third(1)
+            ff_reduce.second(2)
+            ff_reduce.second(3)
 
         return carry
 
     lax.fori_loop(0, rows // PAIR, attend_back, 0)
     for j in range(3):
         grad_put(j, gqkv_s[:, j * width : (j + 1) * width], n1_s[...])
-    grad_put(3, att_s[...], gml_s[...])
     attn_reduce.start()
+    ff_reduce.third(2)
+    ff_reduce.third(3)
 
     def last(i):
         here = block_of(i, 2 * BLOCK)
@@ -1198,41 +1219,24 @@
     def stat_copy(step, src, where):
         return remote(src, stat_in.at[step], stat_send.at[step], stat_recv.at[step], where)
 
-    attn_reduce.first()
+    for t in range(DEPTH):
+        attn_reduce.first(t)
     last(0)
-    ff_reduce.finish()
     last(1)
     stat_copy(0, stat_s, sibling).start()
+    ff_reduce.finish()
     attn_reduce.second(0)
     attn_reduce.second(1)
-    attn_reduce.second(2)
-    attn_reduce.third(0)
-    attn_reduce.second(3)
     stat_copy(0, stat_s, sibling).wait()
     stat_acc[0] = stat_s[...] + stat_in[0]
     stat_copy(1, stat_acc.at[0], facing).start()
-    for t in range(1, DEPTH):
+    attn_reduce.second(2)
+    attn_reduce.second(3)
+    for t in range(DEPTH):
         attn_reduce.third(t)
     stat_copy(1, stat_acc.at[0], facing).wait()
     stat_acc[1] = stat_acc[0] + stat_in[1]
     stat_copy(2, stat_acc.at[1], beside).start()
-    attn_reduce.finish()
-    stat_copy(2, stat_acc.at[1], beside).wait()
-    stat_acc[2] = stat_acc[1] + stat_in[2]
-    stat_line[z] = stat_acc[2]
-
-    def stat_send_line(j):
-        return remote(
-            stat_acc.at[2],
-            stat_line.at[z],
-            stat_send.at[2 + j],
-            stat_recv.at[2 + j],
-            device(line[j], x, y, c),
-        )
-
-    for j in range(1, DEPTH):
-        stat_send_line(j).start()
-
     attn_owner = functools.reduce(jnp.logical_or, [owned(m) for m in range(4)])
     ff_owner = functools.reduce(jnp.logical_or, [owned(m) for m in range(4, 7)])
 
@@ -1265,43 +1269,6 @@
     def poly(value):
         return diagonal + COEF_B * value + COEF_C * square_wide(value)
 
-    def send_x(m, first, count):
-        def send(i, carry):
-            @pl.when(i != mine)
-            def _():
-                x_copy(m, i).start()
-
-            return carry
-
-        lax.fori_loop(first, first + count, send, 0)
-
-    def keep_x(m):
-        start, count = pieces[m]
-        source = x_attn if m < 4 else x_ff
-        pltpu.make_async_copy(
-            source.at[shard], xrows_ref.at[pl.ds(start, count)], x_recv.at[m]
-        ).start()
-
-    @pl.when(attn_owner)
-    def _():
-        value = advance(y_attn, g_attn).reshape(-1, width)
-        total = jnp.sum(jnp.sum(value * value, axis=0, keepdims=True), axis=1, keepdims=True)
-        chain_s[...] = value * (1.0 / (jnp.sqrt(total) + NS_EPS))
-
-        def turn(i, carry):
-            now = chain_s[...]
-            chain_s[...] = mul_wide(now, poly(gram_wide(now)))
-            return carry
-
-        lax.fori_loop(0, NS_ITERS, turn, 0)
-        x_attn[...] = chain_s[...].astype(LOW).reshape(x_attn.shape)
-        for m in range(4):
-
-            @pl.when(owned(m))
-            def _():
-                send_x(m, 0, chips)
-                keep_x(m)
-
     @pl.when(ff_owner)
     def _():
         y_ff[...] = advance(y_ff, g_ff)
@@ -1313,6 +1280,62 @@
         gram_s[...] = mul_wide(mul_wide(gram_mat, step_mat), step_mat)
         chain_s[...] = step_mat * inverse
 
+    attn_reduce.finish()
+    stat_copy(2, stat_acc.at[1], beside).wait()
+    stat_acc[2] = stat_acc[1] + stat_in[2]
+    stat_line[z] = stat_acc[2]
+
+    def stat_send_line(j):
+        return remote(
+            stat_acc.at[2],
+            stat_line.at[z],
+            stat_send.at[2 + j],
+            stat_recv.at[2 + j],
+            device(line[j], x, y, c),
+        )
+
+    for j in range(1, DEPTH):
+        stat_send_line(j).start()
+
+    def send_x(m, first, count):
+        def send(i, carry):
+            @pl.when(i != mine)
+            def _():
+                x_copy(m, i).start()
+
+            return carry
+
+        lax.fori_loop(first, first + count, send, 0)
+
+    def keep_x(m):
+        start, count = pieces[m]
+        source = x_attn if m < 4 else x_ff
+        pltpu.make_async_copy(
+            source.at[shard], xrows_ref.at[pl.ds(start, count)], x_recv.at[m]
+        ).start()
+
+    @pl.when(attn_owner)
+    def _():
+        value = advance(y_attn, g_attn).reshape(-1, width)
+        total = jnp.sum(jnp.sum(value * value, axis=0, keepdims=True), axis=1, keepdims=True)
+        chain_s[...] = value * (1.0 / (jnp.sqrt(total) + NS_EPS))
+
+        def turn(i, carry):
+            now = chain_s[...]
+            chain_s[...] = mul_wide(now, poly(gram_wide(now)))
+            return carry
+
+        lax.fori_loop(0, NS_ITERS, turn, 0)
+        x_attn[...] = chain_s[...].astype(LOW).reshape(x_attn.shape)
+        for m in range(4):
+
+            @pl.when(owned(m))
+            def _():
+                send_x(m, 0, chips)
+                keep_x(m)
+
+    @pl.when(ff_owner)
+    def _():
         def turn(i, carry):
             now = gram_s[...]
             step_now = poly(now)

time: 113 us -> 108 us (0.956)
  Pallas kernels: 112 us -> 107 us
    pallas_call x1, Pallas kernels: 107 us -> 102 us  [whole_step(): pl.pallas_call(functools.partial(whole_kernel, pieces), out_shape=(jax.Sh...]
where the time goes in v6:
time: 108 us; the launch traced here: 107 us
  Pallas kernels  107 us (99%)
    pallas_call x1, Pallas kernels, whole_step(): pl.pallas_call(functools.partial(whole_kernel, pieces), out_shape=(jax.Sh...  102 us
    pallas_call x1, Pallas kernels, update(): pl.pallas_call(functools.partial(update_kernel, pieces, factors), out_sha...  5.07 us

profile of v6, /device:TPU:15, one launch (start us, length us, event | category | flops | bytes accessed | tf_op | source)
XLA Modules:
  0.0 107.4 jit_solution(5303018234462003632)
XLA Ops:
  0.7 101.5 %whole.1 = (bf16[1024,384]{1,0:T(8,128)(2,1)}, bf16[1024,384]{1,0:T(8,128)(2,1)}, bf16[576,384]{1,0:T(8,128)(2,1)}, bf16[576,384]{1,0:T(8,128)(2,1)}, f32[24,384]{1,0:T(8,128)}) custom-call(s32[16]{0:T(128)} %lengths.1, f32[2,6]{1,0:T(2,128)} %bias.3, bf16[1024,384]{1,0:T(8,128)(2,1)} %tok_hbm.1, bf16[1024,384]{1,0:T(8,128)(2,1)} %cot_hbm.1, ...), custom_call_target="tpu_custom_call" | custom-call | tf_op jit(solution)/shard_map/whole/pallas_call | solution.py:1474
  102.2 5.1 %update.1 = (f32[3,48,384]{2,1,0:T(8,128)}, f32[48,384]{1,0:T(8,128)}, f32[2,384,128]{2,1,0:T(8,128)}, f32[128,384]{1,0:T(8,128)}, f32[3,48,384]{2,1,0:T(8,128)}...) custom-call(bf16[576,384]{1,0:T(8,128)(2,1)} %get-tuple-element.49.g, ...), custom_call_target="tpu_custom_call" | custom-call | tf_op jit(solution)/shard_map/update/pallas_call | solution.py:1643

commit v7 on v6

--- a/solution.py
+++ b/solution.py
@@ -481,8 +481,8 @@
     mout_hbm,
     mgate_up_hbm,
     mdown_hbm,
-    out_ref,
-    gtok_ref,
+    out_hbm,
+    gtok_hbm,
     grows_ref,
     xrows_ref,
     total_ref,
@@ -493,6 +493,9 @@
     mgate_up_ref,
     mdown_ref,
     load_sem,
+    out_ref,
+    gtok_ref,
+    out_sem,
     w_s,
     grad_s,
     momenta,
@@ -902,6 +905,8 @@
                 total = total + self.in_three[line[j]].astype(WIDE)
             grows_ref[self.rows_of(part), :] = total.astype(LOW)
             self.all_to_owners(1)
+
+        def give_rows(self):
             for j, where in enumerate((sibling, facing, corner)):
                 self.row_copy(j, part, where).start()
 
@@ -1095,7 +1100,7 @@
         one.send_momenta()
 
     def feed(i, carry):
-        here = block_of(i, BLOCK)
+        here = block_of(i, 2 * BLOCK)
         normed_two = n2_s[here, :]
         w_gate, w_up, w_down = weight(4, 5), weight(5, 6), weight(6, 7)
         gate = mul_nt(normed_two, w_gate)
@@ -1123,7 +1128,7 @@
         gatt_s[here, :] = mul_nt(g_mid_low, weight(3, 4)).astype(LOW)
         return carry
 
-    lax.fori_loop(0, rows // BLOCK, feed, 0)
+    lax.fori_loop(0, rows // (2 * BLOCK), feed, 0)
 
     def grad_put(index, left, right):
         start, count = pieces[index]
@@ -1223,6 +1228,11 @@
         attn_reduce.first(t)
     last(0)
     last(1)
+    leave = [
+        pltpu.make_async_copy(gtok_ref, gtok_hbm, out_sem.at[0]),
+        pltpu.make_async_copy(out_ref, out_hbm, out_sem.at[1]),
+    ]
+    leave[0].start()
     stat_copy(0, stat_s, sibling).start()
     ff_reduce.finish()
     attn_reduce.second(0)
@@ -1281,6 +1291,8 @@
         chain_s[...] = step_mat * inverse
 
     attn_reduce.finish()
+    for one in reduces:
+        one.give_rows()
     stat_copy(2, stat_acc.at[1], beside).wait()
     stat_acc[2] = stat_acc[1] + stat_in[2]
     stat_line[z] = stat_acc[2]
@@ -1371,6 +1383,7 @@
 
     outgoing(0)
     outgoing(1)
+    leave[1].start()
 
     for j in range(1, DEPTH):
         remote(
@@ -1417,6 +1430,9 @@
                 return carry
 
             lax.fori_loop(1, chips, sent, 0)
+
+    for one in leave:
+        one.wait()
 
 
 def rotary_table():
@@ -1481,12 +1497,15 @@
             jax.ShapeDtypeStruct((STATS, width), WIDE),
         ),
         in_specs=[SCALARS] * 2 + [ANYWHERE] * 2 + [WHOLE] * 8 + [ANYWHERE] * 4,
-        out_specs=(WHOLE,) * 5,
+        out_specs=(ANYWHERE, ANYWHERE, WHOLE, WHOLE, WHOLE),
         scratch_shapes=[
             low(rows, width),
             low(rows, width),
             *[wide(*m.shape) for m in momenta],
             dma(6),
+            low(rows, width),
+            low(rows, width),
+            dma(2),
             low(shards, shard_rows, width),
             low(DEPTH, ACROSS, shard_rows, width),
             wide(shard_rows, width),

time: 108 us -> 104 us (0.963)
  Pallas kernels: 107 us -> 103 us
    pallas_call x1, Pallas kernels: 102 us -> 98.1 us  [whole_step(): pl.pallas_call(functools.partial(whole_kernel, pieces), out_shape=(jax.Sh...]
where the time goes in v7:
time: 104 us
  Pallas kernels  103 us (99%)
    pallas_call x1, Pallas kernels, whole_step(): pl.pallas_call(functools.partial(whole_kernel, pieces), out_shape=(jax.Sh...  98.1 us
    pallas_call x1, Pallas kernels, update(): pl.pallas_call(functools.partial(update_kernel, pieces, factors), out_sha...  5.07 us

profile of v7, /device:TPU:15, one launch (start us, length us, event | category | flops | bytes accessed | tf_op | source)
XLA Modules:
  0.0 104.0 jit_solution(3532203712035907423)
XLA Ops:
  0.7 98.1 %whole.1 = (bf16[1024,384]{1,0:T(8,128)(2,1)}, bf16[1024,384]{1,0:T(8,128)(2,1)}, bf16[576,384]{1,0:T(8,128)(2,1)}, bf16[576,384]{1,0:T(8,128)(2,1)}, f32[24,384]{1,0:T(8,128)}) custom-call(s32[16]{0:T(128)} %lengths.1, f32[2,6]{1,0:T(2,128)} %bias.3, bf16[1024,384]{1,0:T(8,128)(2,1)} %tok_hbm.1, bf16[1024,384]{1,0:T(8,128)(2,1)} %cot_hbm.1, ...), custom_call_target="tpu_custom_call" | custom-call | tf_op jit(solution)/shard_map/whole/pallas_call | solution.py:1490
  98.8 5.1 %update.1 = (f32[3,48,384]{2,1,0:T(8,128)}, f32[48,384]{1,0:T(8,128)}, f32[2,384,128]{2,1,0:T(8,128)}, f32[128,384]{1,0:T(8,128)}, f32[3,48,384]{2,1,0:T(8,128)}...) custom-call(bf16[576,384]{1,0:T(8,128)(2,1)} %get-tuple-element.49.g, ...), custom_call_target="tpu_custom_call" | custom-call | tf_op jit(solution)/shard_map/update/pallas_call | solution.py:1662

commit v8 on v7

--- a/solution.py
+++ b/solution.py
@@ -399,12 +399,12 @@
 SIDES, CORES = 2, 2
 OWNERS = (
     (2, 0, 0, 0),
-    (2, 1, 0, 1),
-    (1, 1, 0, 0),
     (2, 1, 1, 0),
-    (2, 0, 1, 1),
-    (1, 0, 0, 1),
-    (1, 1, 1, 0),
+    (1, 1, 0, 1),
+    (1, 0, 1, 1),
+    (1, 0, 0, 0),
+    (2, 0, 1, 0),
+    (1, 1, 1, 1),
 )
 
 

time: 104 us -> 103 us (level)
  no operation moved by 1% of the time
where the time goes in v8:
time: 103 us
  Pallas kernels  102 us (99%)
    pallas_call x1, Pallas kernels, whole_step(): pl.pallas_call(functools.partial(whole_kernel, pieces), out_shape=(jax.Sh...  97.3 us
    pallas_call x1, Pallas kernels, update(): pl.pallas_call(functools.partial(update_kernel, pieces, factors), out_sha...  5.07 us

profile of v8, /device:TPU:15, one launch (start us, length us, event | category | flops | bytes accessed | tf_op | source)
XLA Modules:
  0.0 103.2 jit_solution(11717251214988184499)
XLA Ops:
  0.7 97.3 %whole.1 = (bf16[1024,384]{1,0:T(8,128)(2,1)}, bf16[1024,384]{1,0:T(8,128)(2,1)}, bf16[576,384]{1,0:T(8,128)(2,1)}, bf16[576,384]{1,0:T(8,128)(2,1)}, f32[24,384]{1,0:T(8,128)}) custom-call(s32[16]{0:T(128)} %lengths.1, f32[2,6]{1,0:T(2,128)} %bias.3, bf16[1024,384]{1,0:T(8,128)(2,1)} %tok_hbm.1, bf16[1024,384]{1,0:T(8,128)(2,1)} %cot_hbm.1, ...), custom_call_target="tpu_custom_call" | custom-call | tf_op jit(solution)/shard_map/whole/pallas_call | solution.py:1490
  98.0 5.1 %update.1 = (f32[3,48,384]{2,1,0:T(8,128)}, f32[48,384]{1,0:T(8,128)}, f32[2,384,128]{2,1,0:T(8,128)}, f32[128,384]{1,0:T(8,128)}, f32[3,48,384]{2,1,0:T(8,128)}...) custom-call(bf16[576,384]{1,0:T(8,128)(2,1)} %get-tuple-element.49.g, ...), custom_call_target="tpu_custom_call" | custom-call | tf_op jit(solution)/shard_map/update/pallas_call | solution.py:1662

commit v9 on v8

--- a/solution.py
+++ b/solution.py
@@ -447,6 +447,11 @@
     high, low = halves(value)
     cross = mul_nn(high, low)
     return mul_nn(high, high) + (cross + cross.T)
+
+
+def square_low(value):
+    low = value.astype(LOW)
+    return mul_nn(low, low)
 
 
 def mul_wide(left, right):
@@ -558,12 +563,16 @@
         return jnp.where(z == low_z, turn, DEPTH - 1 - turn)
     part = 2 * c + y
 
-    def hello(i, carry):
-        other = lax.rem(rank + 1 + i, world)
-        greet((other // (SIDES * CORES), lax.rem(other, SIDES * CORES)))
-        return carry
-
-    lax.fori_loop(0, world - 1, hello, 0)
+    for i in range(DEPTH * ACROSS):
+        for j in range(SIDES * CORES):
+            if i + j:
+                greet(
+                    (
+                        lax.rem(shard + i, DEPTH * ACROSS),
+                        lax.rem(y * CORES + c + j, SIDES * CORES),
+                    )
+                )
+
     loads = [
         pltpu.make_async_copy(src, dst, load_sem.at[i])
         for i, (src, dst) in enumerate(
@@ -1337,8 +1346,13 @@
             chain_s[...] = mul_wide(now, poly(gram_wide(now)))
             return carry
 
-        lax.fori_loop(0, NS_ITERS, turn, 0)
-        x_attn[...] = chain_s[...].astype(LOW).reshape(x_attn.shape)
+        lax.fori_loop(0, NS_ITERS - 1, turn, 0)
+        now = chain_s[...]
+        now_low = now.astype(LOW)
+        gram_mat = mul_tn(now_low, now_low)
+        rest = COEF_B * gram_mat + COEF_C * square_low(gram_mat)
+        last_x = COEF_A * now + mul_nn(now_low, rest.astype(LOW))
+        x_attn[...] = last_x.astype(LOW).reshape(x_attn.shape)
         for m in range(4):
 
             @pl.when(owned(m))
@@ -1357,7 +1371,11 @@
             return carry
 
         lax.fori_loop(0, NS_ITERS - 2, turn, 0)
-        chain_s[...] = mul_wide(chain_s[...], poly(gram_s[...]))
+        gram_mat = gram_s[...]
+        rest = (COEF_B * gram_mat + COEF_C * square_low(gram_mat)).astype(LOW)
+        now = chain_s[...]
+        high, small = halves(now)
+        chain_s[...] = COEF_A * now + (mul_nn(high, rest) + mul_nn(small, rest))
 
         def give(i, carry):
             at = lax.rem(z + 2 + i, DEPTH)

time: 103 us -> 103 us (level)
  no operation moved by 1% of the time
where the time goes in v9:
time: 103 us
  Pallas kernels  102 us (99%)
    pallas_call x1, Pallas kernels, whole_step(): pl.pallas_call(functools.partial(whole_kernel, pieces), out_shape=(jax.Sh...  96.9 us
    pallas_call x1, Pallas kernels, update(): pl.pallas_call(functools.partial(update_kernel, pieces, factors), out_sha...  5.07 us

profile of v9, /device:TPU:15, one launch (start us, length us, event | category | flops | bytes accessed | tf_op | source)
XLA Modules:
  0.0 102.8 jit_solution(292401413417244724)
XLA Ops:
  0.7 96.9 %whole.1 = (bf16[1024,384]{1,0:T(8,128)(2,1)}, bf16[1024,384]{1,0:T(8,128)(2,1)}, bf16[576,384]{1,0:T(8,128)(2,1)}, bf16[576,384]{1,0:T(8,128)(2,1)}, f32[24,384]{1,0:T(8,128)}) custom-call(s32[16]{0:T(128)} %lengths.1, f32[2,6]{1,0:T(2,128)} %bias.3, bf16[1024,384]{1,0:T(8,128)(2,1)} %tok_hbm.1, bf16[1024,384]{1,0:T(8,128)(2,1)} %cot_hbm.1, ...), custom_call_target="tpu_custom_call" | custom-call | tf_op jit(solution)/shard_map/whole/pallas_call | solution.py:1508
  97.6 5.1 %update.1 = (f32[3,48,384]{2,1,0:T(8,128)}, f32[48,384]{1,0:T(8,128)}, f32[2,384,128]{2,1,0:T(8,128)}, f32[128,384]{1,0:T(8,128)}, f32[3,48,384]{2,1,0:T(8,128)}...) custom-call(bf16[576,384]{1,0:T(8,128)(2,1)} %get-tuple-element.49.g, ...), custom_call_target="tpu_custom_call" | custom-call | tf_op jit(solution)/shard_map/update/pallas_call | solution.py:1680
